TPU v7x, 32 devices: a whole 2x2x4 slice. The times are simulated.
32 devices in a mesh: groups: 2 (over x), ctx: 8 (over z, y), dp: 2 (over core).
Axes of the slice: x: 2, y: 2, z: 4, core: 2. Of those that a mesh axis runs over, the one named last changes fastest.
Arguments:
- queries: bfloat16 [4, 2048, 512], P(('groups', 'dp'), 'ctx'), parts along dimension 0, may hold values from -6 to 6
- keys: bfloat16 [4, 2048, 512], P(('groups', 'dp'), 'ctx'), parts along dimension 0, may hold values from -6 to 6
- values: bfloat16 [4, 2048, 512], P(('groups', 'dp'), 'ctx'), parts along dimension 0, may hold values from -6 to 6
- gates: bfloat16 [4, 2048, 512], P(('groups', 'dp'), 'ctx'), parts along dimension 0, may hold values from -6 to 6
- out_weight: bfloat16 [512, 1024], replicated, may hold values from -0.25 to 0.25
- grad_out: bfloat16 [4, 2048, 1024], P(('groups', 'dp'), 'ctx'), parts along dimension 0, may hold values from -6 to 6
- lengths: int32 [4, 4], P(('groups', 'dp')), parts along dimension 0, may hold values from 1 to 1024, 2048 in all within a row
Outputs:
- output: bfloat16 [4, 2048, 1024], P(('groups', 'dp'), 'ctx'), parts along dimension 0
- grad_weight: float32 [1024, 1024], P(('groups', 'ctx', 'dp')), parts along dimension 0
- grad_queries: bfloat16 [4, 2048, 512], P(('groups', 'dp'), 'ctx'), parts along dimension 0
- grad_keys: bfloat16 [4, 2048, 512], P(('groups', 'dp'), 'ctx'), parts along dimension 0
- grad_values: bfloat16 [4, 2048, 512], P(('groups', 'dp'), 'ctx'), parts along dimension 0
- grad_gates: bfloat16 [4, 2048, 512], P(('groups', 'dp'), 'ctx'), parts along dimension 0
There are 2 independent parts, one for each index of `groups`. A program takes and returns all parts, laid end to end along the dimension named above; an argument that names none is the same for every part. Nothing has to cross between parts.
Inputs may be any that keep to these rules, and one draw needn't show every extreme that they name: `lengths`: in each packed row the 4 histories fill all 2048 positions in order, and one is exactly 1024 long.
All inputs are finite; a program needn't handle non-finite values.
Results may differ from a plain program's by a relative error of at most 0.0058.
Values may be sent and summed in bfloat16 or wider, within the bound.
No kernel may reach another device: no remote copies, remote signals or barrier semaphores. Data moves between devices by JAX's collectives and lax.ppermute only.
A program may use at most 128 MiB of HBM per device.

v0:
```python
import math

import jax
import jax.numpy as jnp
from jax import lax
from jax.sharding import PartitionSpec as P

HEAD = 128


EPS = 1e-05


def passed_along(block, axis, distance):
    devices = range(lax.axis_size(axis))
    route = [(i - distance, i) for i in devices if i - distance in devices]
    return lax.ppermute(block, axis, route)


def silu_slope(score):
    sigma = jax.nn.sigmoid(score)
    return sigma * (1.0 + score * (1.0 - sigma))


def owners(lengths_row, places):
    ends = jnp.cumsum(lengths_row)
    return jnp.sum((places[:, None] >= ends[None, :]).astype(jnp.int32), axis=1)


def live_mask(query_places, key_places, query_users, key_users):
    causal = key_places[None, :] <= query_places[:, None]
    inside = key_places[None, :] >= 0
    return causal & inside & (query_users[:, None] == key_users[None, :])


def local(queries, keys, values, gates, out_weight, grad_out, lengths):
    query_rows = queries[0]
    gate_rows = gates[0]
    out_grad = grad_out[0]
    tok, width = query_rows.shape
    heads = width // HEAD
    count = lax.axis_size("ctx")
    reach = min(8, count // 2)
    index = lax.axis_index("ctx")
    scale = 1.0 / math.sqrt(HEAD)
    base = index * tok
    query_places = base + jnp.arange(tok, dtype=jnp.int32)
    query_users = owners(lengths[0], query_places)
    key_places = base - reach * tok + jnp.arange((reach + 1) * tok, dtype=jnp.int32)
    key_users = owners(lengths[0], key_places)
    live = live_mask(query_places, key_places, query_users, key_users)
    pair = jnp.stack([keys[0], values[0]])
    arrived = [pair]
    current = pair
    for step in range(1, reach + 1):
        current = passed_along(current, "ctx", 1)
        arrived.append(current)
    window = jnp.concatenate(arrived[::-1], axis=1)
    key_window = window[0].reshape(-1, heads, HEAD)
    value_window = window[1].reshape(-1, heads, HEAD)
    query_heads = query_rows.reshape(tok, heads, HEAD)
    score = (
        jnp.einsum("qhd,khd->hqk", query_heads, key_window, preferred_element_type=jnp.float32)
        * scale
    )
    attend = jnp.where(live[None], jax.nn.silu(score), 0.0).astype(jnp.bfloat16)
    mixed = jnp.einsum(
        "hqk,khd->qhd", attend, value_window, preferred_element_type=jnp.float32
    ).reshape(tok, width)
    centered = mixed - jnp.mean(mixed, axis=1, keepdims=True)
    inverse = lax.rsqrt(jnp.mean(centered * centered, axis=1, keepdims=True) + EPS)
    normed = centered * inverse
    gated = (normed * gate_rows.astype(jnp.float32)).astype(jnp.bfloat16)
    output = jnp.dot(gated, out_weight, preferred_element_type=jnp.float32).astype(jnp.bfloat16)
    total_rows = lax.axis_size("dp") * count * tok
    grad_weight = lax.psum_scatter(
        lax.dot_general(
            gated, out_grad, (((0,), (0,)), ((), ())), preferred_element_type=jnp.float32
        ),
        ("ctx", "dp"),
        scatter_dimension=0,
        tiled=True,
    ) / math.sqrt(total_rows)
    grad_gated = lax.dot_general(
        out_grad, out_weight, (((1,), (1,)), ((), ())), preferred_element_type=jnp.float32
    )
    grad_gates = (grad_gated * normed).astype(jnp.bfloat16)
    grad_normed = grad_gated * gate_rows.astype(jnp.float32)
    grad_mixed = (
        (
            grad_normed
            - jnp.mean(grad_normed, axis=1, keepdims=True)
            - normed * jnp.mean(grad_normed * normed, axis=1, keepdims=True)
        )
        * inverse
    ).astype(jnp.bfloat16)
    grad_heads = grad_mixed.reshape(tok, heads, HEAD)
    value_terms = jnp.einsum(
        "hqk,qhd->khd", attend, grad_heads, preferred_element_type=jnp.float32
    ).reshape(-1, width)
    slope = jnp.einsum("qhd,khd->hqk", grad_heads, value_window, preferred_element_type=jnp.float32)
    score_grad = jnp.where(live[None], slope * silu_slope(score), 0.0).astype(jnp.bfloat16)
    grad_query = (
        jnp.einsum(
            "hqk,khd->qhd", score_grad, key_window, preferred_element_type=jnp.float32
        ).reshape(tok, width)
        * scale
    )
    key_terms = (
        jnp.einsum(
            "hqk,qhd->khd", score_grad, query_heads, preferred_element_type=jnp.float32
        ).reshape(-1, width)
        * scale
    )
    both = jnp.stack([key_terms, value_terms]).reshape(2, reach + 1, tok, width)
    summed = both[:, reach]
    for step in range(1, reach + 1):
        summed = summed + passed_along(both[:, reach - step], "ctx", -step)
    key_grad = summed[0]
    value_grad = summed[1]
    return (
        output[None],
        grad_weight,
        grad_query.astype(jnp.bfloat16)[None],
        key_grad.astype(jnp.bfloat16)[None],
        value_grad.astype(jnp.bfloat16)[None],
        grad_gates[None],
    )


def solution(mesh):
    in_specs = (
        P(("groups", "dp"), "ctx", None),
        P(("groups", "dp"), "ctx", None),
        P(("groups", "dp"), "ctx", None),
        P(("groups", "dp"), "ctx", None),
        P(),
        P(("groups", "dp"), "ctx", None),
        P(("groups", "dp"), None),
    )
    out_specs = (
        P(("groups", "dp"), "ctx", None),
        P(("groups", "ctx", "dp"), None),
        P(("groups", "dp"), "ctx", None),
        P(("groups", "dp"), "ctx", None),
        P(("groups", "dp"), "ctx", None),
        P(("groups", "dp"), "ctx", None),
    )
    return jax.shard_map(local, mesh=mesh, in_specs=in_specs, out_specs=out_specs, check_vma=False)
```

profile of v0, /device:TPU:12, one launch (start us, length us, event | category | flops | bytes accessed | tf_op | source)
XLA Modules:
  0.0 275.9 jit_solution(10771803123816984753)
XLA Ops:
  7.2 1.2 copy.50
  8.4 1.1 copy.49
  9.6 3.4 %collective-permute-start = (bf16[2,256,512]{1,2,0:T(8,128)(2,1)S(1)}, bf16[2,256,512]{1,2,0:T(8,128)(2,1)S(1)}, u32[]{:S(2)}, u32[]{:S(2)}) collective-permute-start(bf16[2,256,512]{1,2,0:T(8,128)(2,1)S(1)} %pad_maximum_fusion), channel_id=1, source_target_pairs={{0,2},{2,4},{4,6},{6,8},{8,10},{10,12},{12,14},{1,3},{3,5},{5,7},{... | collective-permute-start | bytes 1572872 | tf_op jit(solution)/shard_map/ppermute | solution.py:17
  13.0 12.1 %collective-permute-done = bf16[2,256,512]{1,2,0:T(8,128)(2,1)S(1)} collective-permute-done((bf16[2,256,512]{1,2,0:T(8,128)(2,1)S(1)}, bf16[2,256,512]{1,2,0:T(8,128)(2,1)S(1)}, u32[]{:S(2)}, u32[]{:S(2)}) %collective-permute-start) | collective-permute-done | bytes 524320 | tf_op jit(solution)/shard_map/ppermute | solution.py:17
  25.1 4.3 %collective-permute-start.1 = (bf16[2,256,512]{1,2,0:T(8,128)(2,1)S(1)}, bf16[2,256,512]{1,2,0:T(8,128)(2,1)S(1)}, u32[]{:S(2)}, u32[]{:S(2)}) collective-permute-start(bf16[2,256,512]{1,2,0:T(8,128)(2,1)S(1)} %collective-permute-done), channel_id=1, source_target_pairs={{0,2},{2,4},{4,6},{6,8},{8,10},{10,12},{12,14},{1,3},{3,5},{5,7},{... | collective-permute-start | bytes 1572872 | tf_op jit(solution)/shard_map/ppermute | solution.py:17
  29.5 10.4 %collective-permute-done.1 = bf16[2,256,512]{1,2,0:T(8,128)(2,1)S(1)} collective-permute-done((bf16[2,256,512]{1,2,0:T(8,128)(2,1)S(1)}, bf16[2,256,512]{1,2,0:T(8,128)(2,1)S(1)}, u32[]{:S(2)}, u32[]{:S(2)}) %collective-permute-start.1) | collective-permute-done | bytes 524320 | tf_op jit(solution)/shard_map/ppermute | solution.py:17
  39.8 5.2 %collective-permute-start.2 = (bf16[2,256,512]{1,2,0:T(8,128)(2,1)S(1)}, bf16[2,256,512]{1,2,0:T(8,128)(2,1)}, u32[]{:S(2)}, u32[]{:S(2)}) collective-permute-start(bf16[2,256,512]{1,2,0:T(8,128)(2,1)S(1)} %collective-permute-done.1), channel_id=1, source_target_pairs={{0,2},{2,4},{4,6},{6,8},{8,10},{10,12},{12,14},{1,3},{3,5},{5,7},{... | collective-permute-start | bytes 1572872 | tf_op jit(solution)/shard_map/ppermute | solution.py:17
  45.0 1.0 reshape_squeeze.11
  46.1 0.9 copy.55
  47.4 7.0 %collective-permute-done.2 = bf16[2,256,512]{1,2,0:T(8,128)(2,1)} collective-permute-done((bf16[2,256,512]{1,2,0:T(8,128)(2,1)S(1)}, bf16[2,256,512]{1,2,0:T(8,128)(2,1)}, u32[]{:S(2)}, u32[]{:S(2)}) %collective-permute-start.2) | collective-permute-done | bytes 524320 | tf_op jit(solution)/shard_map/ppermute | solution.py:17
  54.4 5.4 %collective-permute-start.3 = (bf16[2,256,512]{1,2,0:T(8,128)(2,1)}, bf16[2,256,512]{1,2,0:T(8,128)(2,1)S(1)}, u32[]{:S(2)}, u32[]{:S(2)}) collective-permute-start(bf16[2,256,512]{1,2,0:T(8,128)(2,1)} %collective-permute-done.2), channel_id=1, source_target_pairs={{0,2},{2,4},{4,6},{6,8},{8,10},{10,12},{12,14},{1,3},{3,5},{5,7},{... | collective-permute-start | bytes 1572872 | tf_op jit(solution)/shard_map/ppermute | solution.py:17
  59.8 1.1 compare_and_fusion
  60.9 7.7 %collective-permute-done.3 = bf16[2,256,512]{1,2,0:T(8,128)(2,1)S(1)} collective-permute-done((bf16[2,256,512]{1,2,0:T(8,128)(2,1)}, bf16[2,256,512]{1,2,0:T(8,128)(2,1)S(1)}, u32[]{:S(2)}, u32[]{:S(2)}) %collective-permute-start.3) | collective-permute-done | bytes 524320 | tf_op jit(solution)/shard_map/ppermute | solution.py:17
  68.6 1.1 constant_dynamic-update-slice_fusion.3
  70.0 4.3 %fusion.4 = (bf16[4,256,1280]{1,2,0:T(8,128)(2,1)S(1)}, f32[4,1280,256]{2,1,0:T(8,128)}) fusion(pred[256,1280]{0,1:T(8,128)(4,1)S(1)} %compare_and_fusion, bf16[1280,4,128]{0,2,1:T(8,128)(2,1)S(1)} %bitcast.117, bf16[256,4,128]{2,1,0:T(4,128)(2,1)S(1)} %reshape_squeeze.11), kind=kOutput, calls=%fused_computation.7 | convolution fusion | flops 344719360 | bytes 9764864 | tf_op jit(solution)/shard_map/qhd,khd->hqk/dot_general | solution.py:63
  74.3 1.5 copy-done.2
  75.9 0.6 fusion.34
  76.8 1.1 multiply_convert_fusion.2
  77.9 2.9 %fusion.20 = f32[512,1024]{1,0:T(8,128)} fusion(bf16[256,512]{0,1:T(8,128)(2,1)S(1)} %bitcast.121, bf16[1,256,1024]{2,1,0:T(8,128)(2,1)} %param.12), kind=kOutput, calls=%fused_computation.34 | convolution fusion | flops 268435456 | bytes 2883584 | tf_op jit(solution)/shard_map/dot_general | solution.py:77
  80.8 1.6 fusion.31
  82.5 0.9 fusion.23
  83.4 0.8 copy.80
  84.2 4.7 %fusion.9 = bf16[4,256,1280]{1,2,0:T(8,128)(2,1)S(1)} fusion(f32[4,1280,256]{2,1,0:T(8,128)} %get-tuple-element.37, bf16[256,4,128]{0,2,1:T(8,128)(2,1)} %bitcast.122, bf16[1280,4,128]{0,2,1:T(8,128)(2,1)S(1)} %bitcast.116, pred[256,1280]{0,1:T(8,128)(4,1)} %copy-done.13), kind=kOutput, calls=%fused_computation.12 | convolution fusion | flops 349962240 | bytes 9764864 | tf_op jit(solution)/shard_map/qhd,khd->hqk/dot_general | solution.py:101
  89.0 0.8 fusion.10
  89.9 0.6 copy-done.3
  90.5 6.5 %copy.61 = f32[1280,4,128]{2,1,0:T(4,128)} copy(f32[1280,4,128]{2,0,1:T(8,128)S(1)} %fusion.10) | data formatting | bytes 5242880 | tf_op jit(solution)/shard_map/mul | solution.py:110
  97.0 4.2 %mul.131 = f32[1,5,256,512]{3,2,1,0:T(8,128)} reshape(f32[1280,4,128]{2,1,0:T(4,128)} %copy.61) | data formatting | bytes 5242880 | tf_op jit(solution)/shard_map/mul | solution.py:110
  101.2 4.3 %convolution_bitcast_fusion = f32[1280,4,128]{0,2,1:T(8,128)} fusion(bf16[256,4,128]{0,2,1:T(8,128)(2,1)S(1)} %bitcast.123, bf16[4,256,1280]{1,2,0:T(8,128)(2,1)} %copy-done.2), kind=kOutput, calls=%fused_computation.15 | convolution fusion | flops 335544320 | bytes 5505024 | tf_op jit(solution)/shard_map/hqk,qhd->khd/dot_general | solution.py:98
  105.6 4.2 %copy.64 = f32[1280,4,128]{2,1,0:T(4,128)} copy(f32[1280,4,128]{0,2,1:T(8,128)} %convolution_bitcast_fusion) | data formatting | bytes 5242880 | tf_op jit(solution)/shard_map/hqk,qhd->khd/transpose | solution.py:98
  109.7 4.1 %stack.10 = f32[1,5,256,512]{3,2,1,0:T(8,128)} reshape(f32[1280,4,128]{2,1,0:T(4,128)} %copy.64) | data formatting | bytes 5242880 | tf_op jit(solution)/shard_map/stack | solution.py:115
  113.9 2.1 constant_dynamic-update-slice_fusion.6
  116.0 0.4 copy-done.5
  116.7 2.1 slice_bitcast_fusion.3
  118.8 2.3 copy-done.1
  121.2 1.3 collective-permute-start.7
  122.5 1.9 collective-permute-start.6
  124.4 1.9 collective-permute-start.5
  126.3 3.5 %collective-permute-start.4 = (f32[2,256,512]{2,1,0:T(8,128)}, f32[2,256,512]{2,1,0:T(8,128)}, u32[]{:S(2)}, u32[]{:S(2)}) collective-permute-start(f32[2,256,512]{2,1,0:T(8,128)} %get-tuple-element.26), channel_id=1, source_target_pairs={{2,0},{4,2},{6,4},{8,6},{10,8},{12,10},{14,12},{3,1},{5,3},{7,5},{... | collective-permute-start | bytes 3145736 | tf_op jit(solution)/shard_map/ppermute | solution.py:17
  129.8 0.5 fusion.12
  130.3 0.8 copy.69
  131.2 1.3 fusion.11
  132.5 17.8 %collective-permute-done.7 = f32[2,256,512]{2,1,0:T(8,128)S(1)} collective-permute-done((f32[2,256,512]{2,1,0:T(8,128)}, f32[2,256,512]{2,1,0:T(8,128)S(1)}, u32[]{:S(2)}, u32[]{:S(2)}) %collective-permute-start.7) | collective-permute-done | bytes 1048608 | tf_op jit(solution)/shard_map/ppermute | solution.py:17
  150.3 24.2 %collective-permute-done.6 = f32[2,256,512]{2,1,0:T(8,128)} collective-permute-done((f32[2,256,512]{2,1,0:T(8,128)}, f32[2,256,512]{2,1,0:T(8,128)}, u32[]{:S(2)}, u32[]{:S(2)}) %collective-permute-start.6) | collective-permute-done | bytes 1048608 | tf_op jit(solution)/shard_map/ppermute | solution.py:17
  174.5 43.7 %collective-permute-done.5 = f32[2,256,512]{2,1,0:T(8,128)} collective-permute-done((f32[2,256,512]{2,1,0:T(8,128)}, f32[2,256,512]{2,1,0:T(8,128)}, u32[]{:S(2)}, u32[]{:S(2)}) %collective-permute-start.5) | collective-permute-done | bytes 1048608 | tf_op jit(solution)/shard_map/ppermute | solution.py:17
  218.1 45.8 %collective-permute-done.4 = f32[2,256,512]{2,1,0:T(8,128)} collective-permute-done((f32[2,256,512]{2,1,0:T(8,128)}, f32[2,256,512]{2,1,0:T(8,128)}, u32[]{:S(2)}, u32[]{:S(2)}) %collective-permute-start.4) | collective-permute-done | bytes 1048608 | tf_op jit(solution)/shard_map/ppermute | solution.py:17
  264.0 2.7 fusion.17
  266.6 0.8 fusion.33
  267.5 1.6 broadcast_multiply_fusion
  (47 shorter events, 1.4 us)
Async XLA Ops:
  7.2 73.6 %copy-start = (bf16[512,1024]{1,0:T(8,128)(2,1)S(1)}, bf16[512,1024]{1,0:T(8,128)(2,1)}, u32[]{:S(2)}) copy-start(bf16[512,1024]{1,0:T(8,128)(2,1)} %param.11) | copy-start | bytes 3145732
  7.2 38.9 %copy-start.8 = (bf16[1,256,512]{2,1,0:T(8,128)(2,1)S(1)}, bf16[1,256,512]{2,1,0:T(8,128)(2,1)}, u32[]{:S(2)}) copy-start(bf16[1,256,512]{2,1,0:T(8,128)(2,1)} %param.10) | copy-start | bytes 786436
  7.2 39.8 %copy-start.14 = (s32[1,4]{1,0:T(1,128)S(1)}, s32[1,4]{1,0:T(1,128)}, u32[]{:S(2)}) copy-start(s32[1,4]{1,0:T(1,128)} %param.13) | copy-start | bytes 52
  7.2 260.3 %reduce-scatter.2.cloned.1.call-start = ((), (), s32[]{:S(2)}) async-start(), calls=%async_computation.1 | async-start | bytes 2228224 | tf_op jit(solution)/shard_map/reduce_scatter | solution.py:76
  9.6 15.6 %collective-permute-start = (bf16[2,256,512]{1,2,0:T(8,128)(2,1)S(1)}, bf16[2,256,512]{1,2,0:T(8,128)(2,1)S(1)}, u32[]{:S(2)}, u32[]{:S(2)}) collective-permute-start(bf16[2,256,512]{1,2,0:T(8,128)(2,1)S(1)} %pad_maximum_fusion), channel_id=1, source_target_pairs={{0,2},{2,4},{4,6},{6,8},{8,10},{10,12},{12,14},{1,3},{3,5},{5,7},{... | collective-permute-start | bytes 1572872 | tf_op jit(solution)/shard_map/ppermute | solution.py:17
  25.1 14.7 %collective-permute-start.1 = (bf16[2,256,512]{1,2,0:T(8,128)(2,1)S(1)}, bf16[2,256,512]{1,2,0:T(8,128)(2,1)S(1)}, u32[]{:S(2)}, u32[]{:S(2)}) collective-permute-start(bf16[2,256,512]{1,2,0:T(8,128)(2,1)S(1)} %collective-permute-done), channel_id=1, source_target_pairs={{0,2},{2,4},{4,6},{6,8},{8,10},{10,12},{12,14},{1,3},{3,5},{5,7},{... | collective-permute-start | bytes 1572872 | tf_op jit(solution)/shard_map/ppermute | solution.py:17
  39.8 14.6 %collective-permute-start.2 = (bf16[2,256,512]{1,2,0:T(8,128)(2,1)S(1)}, bf16[2,256,512]{1,2,0:T(8,128)(2,1)}, u32[]{:S(2)}, u32[]{:S(2)}) collective-permute-start(bf16[2,256,512]{1,2,0:T(8,128)(2,1)S(1)} %collective-permute-done.1), channel_id=1, source_target_pairs={{0,2},{2,4},{4,6},{6,8},{8,10},{10,12},{12,14},{1,3},{3,5},{5,7},{... | collective-permute-start | bytes 1572872 | tf_op jit(solution)/shard_map/ppermute | solution.py:17
  46.1 23.9 %copy-start.10 = (bf16[256,4,128]{2,1,0:T(4,128)(2,1)}, bf16[256,4,128]{2,1,0:T(4,128)(2,1)S(1)}, u32[]{:S(2)}) copy-start(bf16[256,4,128]{2,1,0:T(4,128)(2,1)S(1)} %reshape_squeeze.11) | copy-start | bytes 786436
  54.4 14.2 %collective-permute-start.3 = (bf16[2,256,512]{1,2,0:T(8,128)(2,1)}, bf16[2,256,512]{1,2,0:T(8,128)(2,1)S(1)}, u32[]{:S(2)}, u32[]{:S(2)}) collective-permute-start(bf16[2,256,512]{1,2,0:T(8,128)(2,1)} %collective-permute-done.2), channel_id=1, source_target_pairs={{0,2},{2,4},{4,6},{6,8},{8,10},{10,12},{12,14},{1,3},{3,5},{5,7},{... | collective-permute-start | bytes 1572872 | tf_op jit(solution)/shard_map/ppermute | solution.py:17
  60.9 9.1 %copy-start.13 = (pred[256,1280]{0,1:T(8,128)(4,1)}, pred[256,1280]{0,1:T(8,128)(4,1)S(1)}, u32[]{:S(2)}) copy-start(pred[256,1280]{0,1:T(8,128)(4,1)S(1)} %compare_and_fusion) | copy-start | bytes 983044
  70.0 4.3 %copy-start.6 = (bf16[1,1280,512]{1,2,0:T(8,128)(2,1)}, bf16[1,1280,512]{1,2,0:T(8,128)(2,1)S(1)}, u32[]{:S(2)}) copy-start(bf16[1,1280,512]{1,2,0:T(8,128)(2,1)S(1)} %get-tuple-element.30) | copy-start | bytes 3932164
  74.3 1.6 copy-start.2
  77.9 2.9 %copy-start.9 = (bf16[1,256,512]{2,1,0:T(8,128)(2,1)S(1)}, bf16[1,256,512]{2,1,0:T(8,128)(2,1)}, u32[]{:S(2)}) copy-start(bf16[1,256,512]{2,1,0:T(8,128)(2,1)} %param.10) | copy-start | bytes 786436
  84.2 4.7 %copy-start.11 = (bf16[256,4,128]{2,1,0:T(4,128)(2,1)S(1)}, bf16[256,4,128]{2,1,0:T(4,128)(2,1)}, u32[]{:S(2)}) copy-start(bf16[256,4,128]{2,1,0:T(4,128)(2,1)} %copy-done.10) | copy-start | bytes 786436
  89.0 1.5 copy-start.3
  97.0 4.2 %copy-start.12 = (bf16[256,512]{0,1:T(8,128)(2,1)S(1)}, bf16[256,512]{0,1:T(8,128)(2,1)}, u32[]{:S(2)}) copy-start(bf16[256,512]{0,1:T(8,128)(2,1)} %copy.80) | copy-start | bytes 786436
  113.9 2.5 copy-start.5
  116.7 4.5 %copy-start.1 = (f32[2,5,256,512]{3,2,1,0:T(8,128)}, f32[2,5,256,512]{3,2,1,0:T(8,128)S(1)}, u32[]{:S(2)}) copy-start(f32[2,5,256,512]{3,2,1,0:T(8,128)S(1)} %constant_dynamic-update-slice_fusion.5) | copy-start | bytes 15728644
  116.7 13.1 %copy-start.4 = (bf16[4,256,1280]{1,2,0:T(8,128)(2,1)S(1)}, bf16[4,256,1280]{1,2,0:T(8,128)(2,1)}, u32[]{:S(2)}) copy-start(bf16[4,256,1280]{1,2,0:T(8,128)(2,1)} %copy-done.3) | copy-start | bytes 7864324
  116.7 13.1 %copy-start.7 = (bf16[1,1280,512]{1,2,0:T(8,128)(2,1)S(1)}, bf16[1,1280,512]{1,2,0:T(8,128)(2,1)}, u32[]{:S(2)}) copy-start(bf16[1,1280,512]{1,2,0:T(8,128)(2,1)} %copy-done.6) | copy-start | bytes 3932164
  121.2 29.1 %collective-permute-start.7 = (f32[2,256,512]{2,1,0:T(8,128)}, f32[2,256,512]{2,1,0:T(8,128)S(1)}, u32[]{:S(2)}, u32[]{:S(2)}) collective-permute-start(f32[2,256,512]{2,1,0:T(8,128)} %get-tuple-element.28), channel_id=1, source_target_pairs={{8,0},{10,2},{12,4},{14,6},{9,1},{11,3},{13,5},{15,7},{24,16},{26,... | collective-permute-start | bytes 3145736 | tf_op jit(solution)/shard_map/ppermute | solution.py:17
  122.5 52.0 %collective-permute-start.6 = (f32[2,256,512]{2,1,0:T(8,128)}, f32[2,256,512]{2,1,0:T(8,128)}, u32[]{:S(2)}, u32[]{:S(2)}) collective-permute-start(f32[2,256,512]{2,1,0:T(8,128)} %get-tuple-element.29), channel_id=1, source_target_pairs={{6,0},{8,2},{10,4},{12,6},{14,8},{7,1},{9,3},{11,5},{13,7},{15,9},... | collective-permute-start | bytes 3145736 | tf_op jit(solution)/shard_map/ppermute | solution.py:17
  124.4 93.7 %collective-permute-start.5 = (f32[2,256,512]{2,1,0:T(8,128)}, f32[2,256,512]{2,1,0:T(8,128)}, u32[]{:S(2)}, u32[]{:S(2)}) collective-permute-start(f32[2,256,512]{2,1,0:T(8,128)} %get-tuple-element.27), channel_id=1, source_target_pairs={{4,0},{6,2},{8,4},{10,6},{12,8},{14,10},{5,1},{7,3},{9,5},{11,7},{... | collective-permute-start | bytes 3145736 | tf_op jit(solution)/shard_map/ppermute | solution.py:17
  126.3 137.6 %collective-permute-start.4 = (f32[2,256,512]{2,1,0:T(8,128)}, f32[2,256,512]{2,1,0:T(8,128)}, u32[]{:S(2)}, u32[]{:S(2)}) collective-permute-start(f32[2,256,512]{2,1,0:T(8,128)} %get-tuple-element.26), channel_id=1, source_target_pairs={{2,0},{4,2},{6,4},{8,6},{10,8},{12,10},{14,12},{3,1},{5,3},{7,5},{... | collective-permute-start | bytes 3145736 | tf_op jit(solution)/shard_map/ppermute | solution.py:17
Sparse Core Ops, SparseCore 0:
  80.9 103.8 reduce-scatter.1
where the time goes:
time: 277 us; the launch traced here: 276 us
  waiting for transfers between devices  169 us (61%)
  local copies, waits for them, and re-layouts  36.8 us (13%)
  starting transfers between devices  27 us (10%)
  matrix products  21.1 us (8%)
  between operations  14.4 us (5%)
  other arithmetic  7.93 us (3%)
    ppermute x8, waiting for transfers between devices, passed_along(): return lax.ppermute(block, axis, route)  169 us
    ppermute x8, starting transfers between devices, passed_along(): return lax.ppermute(block, axis, route)  26.9 us
    unnamed x38, local copies, waits for them, and re-layouts  11.4 us
    mul x2, local copies, waits for them, and re-layouts, local(): jnp.einsum('hqk,qhd->khd', score_grad, query_heads, preferred_element_typ...  10.7 us
  transfers between devices with their start and end apart: 9, of which 8 were waited for; matrix products, arithmetic and copies ran while one was open for 17% of the time, Pallas kernels for 0%

commit v1 on v0

v1 whole, which is shorter than its diff:
```python
import functools
import math

import jax
import jax.numpy as jnp
from jax import lax
from jax.experimental import pallas as pl
from jax.experimental.pallas import tpu as pltpu
from jax.sharding import PartitionSpec as P

HEAD = 128
EPS = 1e-05
SCALE = 1.0 / math.sqrt(HEAD)
BF16 = jnp.bfloat16
F32 = jnp.float32
VMEM = pl.BlockSpec(memory_space=pltpu.VMEM)
SMEM = pl.BlockSpec(memory_space=pltpu.SMEM)


def shifted(block, distance):
    devices = range(lax.axis_size("ctx"))
    return lax.ppermute(block, "ctx", [(i, i + distance) for i in devices if i + distance in devices])


def swapped(block, axis, step):
    return lax.ppermute(block, axis, [(i, i ^ step) for i in range(lax.axis_size(axis))])


def dot(a, b, da, db):
    return lax.dot_general(a, b, (((da,), (db,)), ((), ())), preferred_element_type=F32)


def ends_of(lengths_ref):
    ends, total = [], jnp.int32(0)
    for user in range(lengths_ref.shape[1]):
        total = total + lengths_ref[0, user]
        ends.append(total)
    return ends


def first_place(ends, places):
    first = jnp.zeros_like(places)
    for end in ends:
        first = jnp.where(places >= end, end, first)
    return first


def past_place(ends, places):
    past = jnp.zeros_like(places) + ends[-1]
    for end in ends[-2::-1]:
        past = jnp.where(places < end, end, past)
    return past


def score_parts(a, b):
    half = dot(a, b, 1, 1) * (0.5 * SCALE)
    return half, jnp.tanh(half)


def slopes(half, turn):
    attend = half * turn + half
    return attend, (1.0 + turn) + attend * (1.0 - turn)


def head_columns(width):
    return [slice(h, h + HEAD) for h in range(0, width, HEAD)]


def live_rows(ends, place, tok, distance):
    rows = place + lax.broadcasted_iota(jnp.int32, (tok, tok), 0)
    columns = place - distance * tok + lax.broadcasted_iota(jnp.int32, (tok, tok), 1)
    live = columns >= first_place(ends, rows)
    return live & (columns <= rows) if distance == 0 else live


def live_columns(ends, place, tok, distance):
    rows = place + lax.broadcasted_iota(jnp.int32, (tok, tok), 0)
    columns = place + distance * tok + lax.broadcasted_iota(jnp.int32, (tok, tok), 1)
    live = columns < past_place(ends, rows)
    return live & (columns >= rows) if distance == 0 else live


def mix_kernel(ahead, distances, project, *refs):
    count = len(distances)
    lengths_ref, q_ref = refs[:2]
    k_refs, v_refs = refs[2 : 2 + count], refs[2 + count : 2 + 2 * count]
    mixed_ref = refs[-1]
    if project:
        out_grad_ref, weight_ref, grad_gated_ref, mixed_ref = refs[2 + 2 * count :]
        grad_gated_ref[...] = dot(out_grad_ref[...], weight_ref[...], 1, 1)
    tok, width = q_ref.shape
    place = (lax.axis_index("ctx") + ahead) * tok
    ends = ends_of(lengths_ref)
    for n, distance in enumerate(distances):
        live = live_rows(ends, place, tok, distance)
        for cols in head_columns(width):
            half, turn = score_parts(q_ref[:, cols], k_refs[n][:, cols])
            attend = jnp.where(live, half * turn + half, 0.0).astype(BF16)
            term = dot(attend, v_refs[n][:, cols], 1, 0)
            if n > 0:
                term = term + mixed_ref[:, cols].astype(F32)
            mixed_ref[:, cols] = term.astype(mixed_ref.dtype)


def norm_kernel(near_ref, far_ref, grad_gated_ref, gates_ref, gated_ref, grad_gates_ref, grad_mixed_ref):
    mixed = near_ref[...] + far_ref[...].astype(F32)
    gates = gates_ref[...].astype(F32)
    grad_gated = grad_gated_ref[...]
    centered = mixed - jnp.mean(mixed, axis=1, keepdims=True)
    inverse = lax.rsqrt(jnp.mean(centered * centered, axis=1, keepdims=True) + EPS)
    normed = centered * inverse
    gated_ref[...] = (normed * gates).astype(BF16)
    grad_gates_ref[...] = (grad_gated * normed).astype(BF16)
    grad_normed = grad_gated * gates
    grad_mixed_ref[...] = (
        (
            grad_normed
            - jnp.mean(grad_normed, axis=1, keepdims=True)
            - normed * jnp.mean(grad_normed * normed, axis=1, keepdims=True)
        )
        * inverse
    ).astype(BF16)


def query_grad_kernel(ahead, distances, *refs):
    count = len(distances)
    lengths_ref, q_ref, grad_ref = refs[:3]
    k_refs, v_refs = refs[3 : 3 + count], refs[3 + count : 3 + 2 * count]
    out_ref = refs[-1]
    tok, width = q_ref.shape
    place = (lax.axis_index("ctx") + ahead) * tok
    ends = ends_of(lengths_ref)
    for n, distance in enumerate(distances):
        live = live_rows(ends, place, tok, distance)
        for cols in head_columns(width):
            _, slope = slopes(*score_parts(q_ref[:, cols], k_refs[n][:, cols]))
            pull = dot(grad_ref[:, cols], v_refs[n][:, cols], 1, 1)
            score_grad = jnp.where(live, pull * slope, 0.0).astype(BF16)
            term = dot(score_grad, k_refs[n][:, cols], 1, 0) * (0.5 * SCALE)
            if n > 0:
                term = term + out_ref[:, cols].astype(F32)
            out_ref[:, cols] = term.astype(out_ref.dtype)


def key_grad_kernel(distances, carried, *refs):
    count = len(distances)
    lengths_ref, k_ref, v_ref = refs[:3]
    q_refs, grad_refs = refs[3 : 3 + count], refs[3 + count : 3 + 2 * count]
    key_out, value_out = refs[-2:]
    tok, width = k_ref.shape
    place = lax.axis_index("ctx") * tok
    ends = ends_of(lengths_ref)
    lives = [live_columns(ends, place, tok, distance) for distance in distances]
    for cols in head_columns(width):
        if carried:
            key_grad = refs[3 + 2 * count][:, cols]
            value_grad = refs[4 + 2 * count][:, cols]
        else:
            key_grad = value_grad = jnp.zeros((tok, HEAD), F32)
        for n in range(count):
            attend, slope = slopes(*score_parts(k_ref[:, cols], q_refs[n][:, cols]))
            attend = jnp.where(lives[n], attend, 0.0).astype(BF16)
            value_grad = value_grad + dot(attend, grad_refs[n][:, cols], 1, 0)
            pull = dot(v_ref[:, cols], grad_refs[n][:, cols], 1, 1)
            score_grad = jnp.where(lives[n], pull * slope, 0.0).astype(BF16)
            key_grad = key_grad + dot(score_grad, q_refs[n][:, cols], 1, 0) * (0.5 * SCALE)
        key_out[:, cols] = key_grad.astype(key_out.dtype)
        value_out[:, cols] = value_grad.astype(value_out.dtype)


def out_kernel(gated_ref, weight_ref, out_ref):
    out_ref[...] = dot(gated_ref[...], weight_ref[...], 1, 0).astype(BF16)


def weight_kernel(parts, gated_ref, out_grad_ref, keep_ref, give_ref, total_ref):
    total_ref[...] = dot(gated_ref[...], out_grad_ref[...], 0, 0)
    rows = total_ref.shape[0] // (2 * parts)
    mine = lax.axis_index("dp")
    for part in range(parts):
        to = pl.ds(part * rows, rows)
        keep = pl.multiple_of((2 * part + mine) * rows, rows)
        give = pl.multiple_of((2 * part + 1 - mine) * rows, rows)
        keep_ref[to, :] = total_ref[pl.ds(keep, rows), :]
        give_ref[to, :] = total_ref[pl.ds(give, rows), :].astype(BF16)


def call(kernel, outs, args, flops, scratch=()):
    shapes = [jax.ShapeDtypeStruct(shape, dtype) for shape, dtype in outs]
    moved = sum(math.prod(a.shape) * a.dtype.itemsize for a in [*args, *shapes])
    return pl.pallas_call(
        kernel,
        out_shape=shapes,
        in_specs=[SMEM if a.dtype == jnp.int32 else VMEM for a in args],
        out_specs=[VMEM] * len(shapes),
        scratch_shapes=list(scratch),
        cost_estimate=pl.CostEstimate(flops=flops, bytes_accessed=moved, transcendentals=0),
        compiler_params=pltpu.CompilerParams(vmem_limit_bytes=48 * 1024 * 1024),
    )(*args)


def earlier_blocks(block, most):
    blocks = {0: block}
    even = lax.axis_index("ctx") % 2 == 0
    for distance in range(2, most + 1, 2):
        blocks[distance] = shifted(blocks[distance - 2], 2)
        blocks[distance - 1] = swapped(
            jnp.where(even, blocks[distance - 2], blocks[distance]), "ctx", 1
        )
    return blocks


def later_blocks(block, most):
    blocks = {0: block}
    for distance in range(1, most + 1):
        step = 2 - distance % 2
        blocks[distance] = shifted(blocks[distance - step], -step)
    return blocks


def summed_rows(keep, give):
    count, index = lax.axis_size("ctx"), lax.axis_index("ctx")
    total = keep + swapped(give, "dp", 1).astype(F32)
    step = 1
    while step < count:
        pairs = total.reshape(count // (2 * step), 2, -1, total.shape[-1])
        bit = (index // step) % 2
        give = lax.dynamic_index_in_dim(pairs, 1 - bit, 1, False).astype(BF16)
        keep = lax.dynamic_index_in_dim(pairs, bit, 1, False)
        total = (keep + swapped(give, "ctx", step).astype(F32)).reshape(-1, total.shape[-1])
        step *= 2
    return total


def local(queries, keys, values, gates, out_weight, grad_out, lengths):
    q, k, v, gate_rows, out_grad = queries[0], keys[0], values[0], gates[0], grad_out[0]
    tok, width = q.shape
    model = out_grad.shape[1]
    count = lax.axis_size("ctx")
    reach = min(8, count // 2)
    mid = reach // 2
    pair_flops = 2 * tok * tok * width
    key_at = earlier_blocks(k, mid)
    value_at = earlier_blocks(v, mid)
    query_at = later_blocks(q, reach)

    near = list(range(mid + 1))
    back = list(range(1, mid + 1))
    far = [mid + d for d in back]
    (far_term,) = call(
        functools.partial(mix_kernel, mid, far, False),
        [((tok, width), BF16)],
        [lengths, query_at[mid], *[key_at[d] for d in back], *[value_at[d] for d in back]],
        2 * pair_flops * len(back),
    )
    far_mixed = shifted(far_term, mid)
    grad_gated, near_mixed = call(
        functools.partial(mix_kernel, 0, near, True),
        [((tok, width), F32), ((tok, width), F32)],
        [lengths, q, *[key_at[d] for d in near], *[value_at[d] for d in near], out_grad, out_weight],
        2 * pair_flops * len(near) + 2 * tok * width * model,
    )
    gated, grad_gates, grad_mixed = call(
        norm_kernel,
        [((tok, width), BF16)] * 3,
        [near_mixed, far_mixed, grad_gated, gate_rows],
        20 * tok * width,
    )
    grad_at = later_blocks(grad_mixed, reach)
    keep, give = call(
        functools.partial(weight_kernel, count),
        [((width // 2, model), F32), ((width // 2, model), BF16)],
        [gated, out_grad],
        2 * tok * width * model,
        [pltpu.VMEM((width, model), F32)],
    )
    (output,) = call(
        out_kernel, [((tok, model), BF16)], [gated, out_weight], 2 * tok * width * model
    )
    (far_query_term,) = call(
        functools.partial(query_grad_kernel, mid, far),
        [((tok, width), BF16)],
        [lengths, query_at[mid], grad_at[mid], *[key_at[d] for d in back], *[value_at[d] for d in back]],
        3 * pair_flops * len(back),
    )
    far_query = shifted(far_query_term, mid)
    (near_query,) = call(
        functools.partial(query_grad_kernel, 0, near),
        [((tok, width), F32)],
        [lengths, q, grad_mixed, *[key_at[d] for d in near], *[value_at[d] for d in near]],
        3 * pair_flops * len(near),
    )
    key_part, value_part = call(
        functools.partial(key_grad_kernel, near, False),
        [((tok, width), F32)] * 2,
        [lengths, k, v, *[query_at[d] for d in near], *[grad_at[d] for d in near]],
        4 * pair_flops * len(near),
    )
    key_grad, value_grad = call(
        functools.partial(key_grad_kernel, far, True),
        [((tok, width), BF16)] * 2,
        [lengths, k, v, *[query_at[d] for d in far], *[grad_at[d] for d in far], key_part, value_part],
        4 * pair_flops * len(far),
    )
    query_grad = (near_query + far_query.astype(F32)).astype(BF16)
    total_rows = lax.axis_size("dp") * count * tok
    grad_weight = summed_rows(keep, give) / math.sqrt(total_rows)
    return (
        output[None],
        grad_weight,
        query_grad[None],
        key_grad[None],
        value_grad[None],
        grad_gates[None],
    )


def solution(mesh):
    rows = P(("groups", "dp"), "ctx", None)
    in_specs = (rows, rows, rows, rows, P(), rows, P(("groups", "dp"), None))
    out_specs = (rows, P(("groups", "ctx", "dp"), None), rows, rows, rows, rows)
    return jax.shard_map(local, mesh=mesh, in_specs=in_specs, out_specs=out_specs, check_vma=False)
```

time: 277 us -> 102 us (0.37)
  the two profiles are of different devices: /device:TPU:12 before, /device:TPU:0 now
where the time goes in v1:
time: 102 us; the launch traced here: 101 us
  starting transfers between devices  41.3 us (40%)
  waiting for transfers between devices  31.4 us (31%)
  Pallas kernels  19.5 us (19%)
  other arithmetic  4.99 us (5%)
  local copies, waits for them, and re-layouts  3.08 us (3%)
  between operations  1.06 us (1%)
    ppermute x12, starting transfers between devices, shifted(): lax.ppermute(block, 'ctx', [(i, i + distance) for i in devices if i + dis...  26.6 us
    pallas_call x9, Pallas kernels, call(): pl.pallas_call(kernel, out_shape=shapes, in_specs=[SMEM if a.dtype == jnp...  19.5 us
    ppermute x12, waiting for transfers between devices, shifted(): lax.ppermute(block, 'ctx', [(i, i + distance) for i in devices if i + dis...  17.9 us
    ppermute x6, starting transfers between devices, swapped(): lax.ppermute(block, axis, [(i, i ^ step) for i in range(lax.axis_size(axi...  14.6 us
    ppermute x6, waiting for transfers between devices, swapped(): lax.ppermute(block, axis, [(i, i ^ step) for i in range(lax.axis_size(axi...  13.5 us
    unnamed x24, local copies, waits for them, and re-layouts  2.21 us
  transfers between devices with their start and end apart: 18, of which 9 were waited for; matrix products, arithmetic and copies ran while one was open for 3% of the time, Pallas kernels for 15%

profile of v1, /device:TPU:0, one launch (start us, length us, event | category | flops | bytes accessed | tf_op | source)
XLA Modules:
  0.0 101.3 jit_solution(4165760522160553269)
XLA Ops:
  0.6 4.9 %collective-permute-start = (bf16[256,512]{1,0:T(8,128)(2,1)}, bf16[256,512]{1,0:T(8,128)(2,1)S(1)}, u32[]{:S(2)}, u32[]{:S(2)}) collective-permute-start(bf16[256,512]{1,0:T(8,128)(2,1)} %bitcast.29), channel_id=1, source_target_pairs={{0,4},{2,6},{4,8},{6,10},{8,12},{10,14},{1,5},{3,7},{5,9},{7,11},{... | collective-permute-start | bytes 786440 | tf_op jit(solution)/shard_map/ppermute | solution.py:22
  5.6 3.5 %collective-permute-start.2 = (bf16[256,512]{1,0:T(8,128)(2,1)}, bf16[256,512]{1,0:T(8,128)(2,1)S(1)}, u32[]{:S(2)}, u32[]{:S(2)}) collective-permute-start(bf16[256,512]{1,0:T(8,128)(2,1)} %bitcast.34), channel_id=1, source_target_pairs={{0,4},{2,6},{4,8},{6,10},{8,12},{10,14},{1,5},{3,7},{5,9},{7,11},{... | collective-permute-start | bytes 786440 | tf_op jit(solution)/shard_map/ppermute | solution.py:22
  9.1 1.3 %collective-permute-start.4 = (bf16[256,512]{1,0:T(8,128)(2,1)}, bf16[256,512]{1,0:T(8,128)(2,1)S(1)}, u32[]{:S(2)}, u32[]{:S(2)}) collective-permute-start(bf16[256,512]{1,0:T(8,128)(2,1)} %bitcast.39), channel_id=1, source_target_pairs={{4,0},{6,2},{8,4},{10,6},{12,8},{14,10},{5,1},{7,3},{9,5},{11,7},{... | collective-permute-start | bytes 786440 | tf_op jit(solution)/shard_map/ppermute | solution.py:22
  10.4 2.2 %collective-permute-done.refs_4_.refs_3_.refs_5_ = bf16[256,512]{1,0:T(8,128)(2,1)S(1)} collective-permute-done((bf16[256,512]{1,0:T(8,128)(2,1)}, bf16[256,512]{1,0:T(8,128)(2,1)S(1)}, u32[]{:S(2)}, u32[]{:S(2)}) %collective-permute-start) | collective-permute-done | bytes 262176 | tf_op jit(solution)/shard_map/ppermute | solution.py:22
  12.6 1.0 broadcast_select_fusion.1
  13.6 0.0 copy-start
  13.6 1.6 %collective-permute-start.1 = (bf16[256,512]{1,0:T(8,128)(2,1)S(1)}, bf16[256,512]{1,0:T(8,128)(2,1)S(1)}, u32[]{:S(2)}, u32[]{:S(2)}) collective-permute-start(bf16[256,512]{1,0:T(8,128)(2,1)S(1)} %broadcast_select_fusion.1), channel_id=1, source_target_pairs={{0,2},{2,0},{4,6},{6,4},{8,10},{10,8},{12,14},{14,12},{1,3},{3,1},... | collective-permute-start | bytes 786440 | tf_op jit(solution)/shard_map/ppermute | solution.py:26
  15.2 1.9 %collective-permute-done.2.refs_7_.refs_5_.refs_8_.refs_6_ = bf16[256,512]{1,0:T(8,128)(2,1)S(1)} collective-permute-done((bf16[256,512]{1,0:T(8,128)(2,1)}, bf16[256,512]{1,0:T(8,128)(2,1)S(1)}, u32[]{:S(2)}, u32[]{:S(2)}) %collective-permute-start.2) | collective-permute-done | bytes 262176 | tf_op jit(solution)/shard_map/ppermute | solution.py:22
  17.1 0.0 copy-start.1
  17.1 0.0 copy-start.4
  17.1 1.6 %collective-permute-start.3 = (bf16[256,512]{1,0:T(8,128)(2,1)S(1)}, bf16[256,512]{1,0:T(8,128)(2,1)S(1)}, u32[]{:S(2)}, u32[]{:S(2)}) collective-permute-start(bf16[256,512]{1,0:T(8,128)(2,1)S(1)} %broadcast_select_fusion), channel_id=1, source_target_pairs={{0,2},{2,0},{4,6},{6,4},{8,10},{10,8},{12,14},{14,12},{1,3},{3,1},... | collective-permute-start | bytes 786440 | tf_op jit(solution)/shard_map/ppermute | solution.py:26
  18.7 2.5 %collective-permute-done.1.refs_3_.refs_2_.refs_4_ = bf16[256,512]{1,0:T(8,128)(2,1)S(1)} collective-permute-done((bf16[256,512]{1,0:T(8,128)(2,1)S(1)}, bf16[256,512]{1,0:T(8,128)(2,1)S(1)}, u32[]{:S(2)}, u32[]{:S(2)}) %collective-permute-start.1) | collective-permute-done | bytes 262176 | tf_op jit(solution)/shard_map/ppermute | solution.py:26
  21.2 4.4 %collective-permute-done.3.refs_6_.refs_4_.refs_7_.refs_5_ = bf16[256,512]{1,0:T(8,128)(2,1)S(1)} collective-permute-done((bf16[256,512]{1,0:T(8,128)(2,1)S(1)}, bf16[256,512]{1,0:T(8,128)(2,1)S(1)}, u32[]{:S(2)}, u32[]{:S(2)}) %collective-permute-start.3) | collective-permute-done | bytes 262176 | tf_op jit(solution)/shard_map/ppermute | solution.py:26
  25.6 1.5 %shard_map.119 = bf16[256,512]{1,0:T(8,128)(2,1)S(1)} custom-call(s32[1,4]{1,0:T(1,128)S(1)} %copy-done.9, bf16[256,512]{1,0:T(8,128)(2,1)S(1)} %collective-permute-done.4.refs_1_.refs_5_, bf16[256,512]{1,0:T(8,128)(2,1)S(1)} %collective-permute-done.1.refs_3_.refs_2_.refs_4_, bf16[256,512]{1,0:T(8,128)(2,1)S(1)} %collective-permute-done.refs_4_.refs_3_.refs_5_, ...), custom_call_target="tpu_custom_call" | custom-call | flops 268435456 | bytes 1572880 | tf_op jit(solution)/shard_map/pallas_call | solution.py:190
  27.2 4.3 %collective-permute-start.5 = (bf16[256,512]{1,0:T(8,128)(2,1)S(1)}, bf16[256,512]{1,0:T(8,128)(2,1)S(1)}, u32[]{:S(2)}, u32[]{:S(2)}) collective-permute-start(bf16[256,512]{1,0:T(8,128)(2,1)S(1)} %shard_map.119), channel_id=1, source_target_pairs={{0,4},{2,6},{4,8},{6,10},{8,12},{10,14},{1,5},{3,7},{5,9},{7,11},{... | collective-permute-start | bytes 786440 | tf_op jit(solution)/shard_map/ppermute | solution.py:22
  31.5 0.0 copy-start.6
  31.5 2.0 %shard_map.118 = (f32[256,512]{1,0:T(8,128)S(1)}, f32[256,512]{1,0:T(8,128)S(1)}) custom-call(s32[1,4]{1,0:T(1,128)S(1)} %copy-done.9, bf16[256,512]{1,0:T(8,128)(2,1)S(1)} %bitcast.40, bf16[256,512]{1,0:T(8,128)(2,1)S(1)} %bitcast.30, bf16[256,512]{1,0:T(8,128)(2,1)S(1)} %collective-permute-done.1.refs_3_.refs_2_.refs_4_, ...), custom_call_target="tpu_custom_call" | custom-call | flops 671088640 | bytes 4456464 | tf_op jit(solution)/shard_map/pallas_call | solution.py:190
  33.5 2.5 %collective-permute-done.5.far_ref = bf16[256,512]{1,0:T(8,128)(2,1)S(1)} collective-permute-done((bf16[256,512]{1,0:T(8,128)(2,1)S(1)}, bf16[256,512]{1,0:T(8,128)(2,1)S(1)}, u32[]{:S(2)}, u32[]{:S(2)}) %collective-permute-start.5) | collective-permute-done | bytes 262176 | tf_op jit(solution)/shard_map/ppermute | solution.py:22
  36.1 1.0 shard_map.120
  37.1 1.4 %shard_map.122 = (f32[256,1024]{1,0:T(8,128)S(1)}, bf16[256,1024]{1,0:T(8,128)(2,1)}) custom-call(bf16[256,512]{1,0:T(8,128)(2,1)S(1)} %get-tuple-element.19.gated_ref, bf16[256,1024]{1,0:T(8,128)(2,1)S(1)} %bitcast.45), custom_call_target="tpu_custom_call" | custom-call | flops 268435456 | bytes 2359296 | tf_op jit(solution)/shard_map/pallas_call | solution.py:190
  38.5 1.0 copy-done.3
  39.5 2.2 %collective-permute-done.6 = bf16[256,1024]{1,0:T(8,128)(2,1)} collective-permute-done((bf16[256,1024]{1,0:T(8,128)(2,1)}, bf16[256,1024]{1,0:T(8,128)(2,1)}, u32[]{:S(2)}, u32[]{:S(2)}) %collective-permute-start.6) | collective-permute-done | bytes 524320 | tf_op jit(solution)/shard_map/ppermute | solution.py:26
  41.8 1.5 %convert_add_fusion = f32[256,1024]{1,0:T(8,128)S(1)} fusion(f32[256,1024]{1,0:T(8,128)} %copy-done.3, bf16[256,1024]{1,0:T(8,128)(2,1)} %collective-permute-done.6), kind=kLoop, calls=%fused_computation | loop fusion | flops 524288 | bytes 2621440 | tf_op jit(solution)/shard_map/add | solution.py:222
  43.3 0.8 fusion.1
  44.1 0.2 copy-done.10
  44.3 1.5 %collective-permute-start.7 = (bf16[4,32,1024]{2,1,0:T(8,128)(2,1)}, bf16[4,32,1024]{2,1,0:T(8,128)(2,1)}, u32[]{:S(2)}, u32[]{:S(2)}) collective-permute-start(bf16[4,32,1024]{2,1,0:T(8,128)(2,1)} %fusion.1), channel_id=1, source_target_pairs={{0,2},{2,0},{4,6},{6,4},{8,10},{10,8},{12,14},{14,12},{1,3},{3,1},... | collective-permute-start | bytes 786440 | tf_op jit(solution)/shard_map/ppermute | solution.py:26
  45.9 1.3 %collective-permute-start.16 = (bf16[256,512]{1,0:T(8,128)(2,1)S(1)}, bf16[256,512]{1,0:T(8,128)(2,1)}, u32[]{:S(2)}, u32[]{:S(2)}) collective-permute-start(bf16[256,512]{1,0:T(8,128)(2,1)S(1)} %bitcast.41), channel_id=1, source_target_pairs={{2,0},{4,2},{6,4},{8,6},{10,8},{12,10},{14,12},{3,1},{5,3},{7,5},{... | collective-permute-start | bytes 786440 | tf_op jit(solution)/shard_map/ppermute | solution.py:22
  47.2 1.3 %collective-permute-start.13 = (bf16[256,512]{1,0:T(8,128)(2,1)S(1)}, bf16[256,512]{1,0:T(8,128)(2,1)S(1)}, u32[]{:S(2)}, u32[]{:S(2)}) collective-permute-start(bf16[256,512]{1,0:T(8,128)(2,1)S(1)} %collective-permute-done.4.refs_1_.refs_5_), channel_id=1, source_target_pairs={{4,0},{6,2},{8,4},{10,6},{12,8},{14,10},{5,1},{7,3},{9,5},{11,7},{... | collective-permute-start | bytes 786440 | tf_op jit(solution)/shard_map/ppermute | solution.py:22
  48.5 1.3 %collective-permute-start.17 = (bf16[256,512]{1,0:T(8,128)(2,1)}, bf16[256,512]{1,0:T(8,128)(2,1)S(1)}, u32[]{:S(2)}, u32[]{:S(2)}) collective-permute-start(bf16[256,512]{1,0:T(8,128)(2,1)} %copy-done.7), channel_id=1, source_target_pairs={{2,0},{4,2},{6,4},{8,6},{10,8},{12,10},{14,12},{3,1},{5,3},{7,5},{... | collective-permute-start | bytes 786440 | tf_op jit(solution)/shard_map/ppermute | solution.py:22
  49.8 1.3 %collective-permute-start.10 = (bf16[256,512]{1,0:T(8,128)(2,1)}, bf16[256,512]{1,0:T(8,128)(2,1)S(1)}, u32[]{:S(2)}, u32[]{:S(2)}) collective-permute-start(bf16[256,512]{1,0:T(8,128)(2,1)} %copy-done.7), channel_id=1, source_target_pairs={{4,0},{6,2},{8,4},{10,6},{12,8},{14,10},{5,1},{7,3},{9,5},{11,7},{... | collective-permute-start | bytes 786440 | tf_op jit(solution)/shard_map/ppermute | solution.py:22
  51.1 0.9 copy-done.8
  52.1 3.2 %shard_map.123 = f32[256,512]{1,0:T(8,128)S(1)} custom-call(s32[1,4]{1,0:T(1,128)S(1)} %copy-done.9, bf16[256,512]{1,0:T(8,128)(2,1)S(1)} %bitcast.42, bf16[256,512]{1,0:T(8,128)(2,1)S(1)} %copy-done.8, bf16[256,512]{1,0:T(8,128)(2,1)S(1)} %bitcast.31, bf16[256,512]{1,0:T(8,128)(2,1)S(1)} %collective-permute-done.1.refs_3_.refs_2_.refs_4_, ...), custom_call_target="tpu_custom_call" | custom-call | flops 603979776 | bytes 2621456 | tf_op jit(solution)/shard_map/pallas_call | solution.py:190
  55.3 2.4 %collective-permute-done.7 = bf16[4,32,1024]{2,1,0:T(8,128)(2,1)} collective-permute-done((bf16[4,32,1024]{2,1,0:T(8,128)(2,1)}, bf16[4,32,1024]{2,1,0:T(8,128)(2,1)}, u32[]{:S(2)}, u32[]{:S(2)}) %collective-permute-start.7) | collective-permute-done | bytes 262176 | tf_op jit(solution)/shard_map/ppermute | solution.py:26
  57.7 1.0 %bitcast_add_fusion = f32[4,32,1024]{2,1,0:T(8,128)S(1)} fusion(bf16[4,32,1024]{2,1,0:T(8,128)(2,1)} %collective-permute-done.7, f32[4,2,32,1024]{3,2,1,0:T(8,128)S(1)} %bitcast.48, s32[]{:T(128)S(6)} %select_n.64), kind=kLoop, calls=%fused_computation.2 | loop fusion | flops 262144 | bytes 1310724 | tf_op jit(solution)/shard_map/add | solution.py:229
  58.7 3.1 %collective-permute-start.8 = (bf16[2,32,1024]{2,1,0:T(8,128)(2,1)S(1)}, bf16[2,32,1024]{2,1,0:T(8,128)(2,1)S(1)}, u32[]{:S(2)}, u32[]{:S(2)}) collective-permute-start(bf16[2,32,1024]{2,1,0:T(8,128)(2,1)S(1)} %fusion.2), channel_id=1, source_target_pairs={{0,4},{2,6},{4,0},{6,2},{8,12},{10,14},{12,8},{14,10},{1,5},{3,7},... | collective-permute-start | bytes 393224 | tf_op jit(solution)/shard_map/ppermute | solution.py:26
  61.8 1.2 %shard_map.121 = bf16[256,1024]{1,0:T(8,128)(2,1)} custom-call(bf16[256,512]{1,0:T(8,128)(2,1)S(1)} %get-tuple-element.19.gated_ref, bf16[512,1024]{1,0:T(8,128)(2,1)S(1)} %copy-done), custom_call_target="tpu_custom_call" | custom-call | flops 268435456 | bytes 1835008 | tf_op jit(solution)/shard_map/pallas_call | solution.py:190
  63.0 11.2 %collective-permute-done.10.refs_2_.refs_8_ = bf16[256,512]{1,0:T(8,128)(2,1)S(1)} collective-permute-done((bf16[256,512]{1,0:T(8,128)(2,1)}, bf16[256,512]{1,0:T(8,128)(2,1)S(1)}, u32[]{:S(2)}, u32[]{:S(2)}) %collective-permute-start.10) | collective-permute-done | bytes 262176 | tf_op jit(solution)/shard_map/ppermute | solution.py:22
  74.3 1.3 %collective-permute-start.12 = (bf16[256,512]{1,0:T(8,128)(2,1)S(1)}, bf16[256,512]{1,0:T(8,128)(2,1)S(1)}, u32[]{:S(2)}, u32[]{:S(2)}) collective-permute-start(bf16[256,512]{1,0:T(8,128)(2,1)S(1)} %collective-permute-done.4.refs_1_.refs_5_), channel_id=1, source_target_pairs={{2,0},{4,2},{6,4},{8,6},{10,8},{12,10},{14,12},{3,1},{5,3},{7,5},{... | collective-permute-start | bytes 786440 | tf_op jit(solution)/shard_map/ppermute | solution.py:22
  75.5 2.4 %shard_map.124 = bf16[256,512]{1,0:T(8,128)(2,1)S(1)} custom-call(s32[1,4]{1,0:T(1,128)S(1)} %copy-done.9, bf16[256,512]{1,0:T(8,128)(2,1)S(1)} %collective-permute-done.4.refs_1_.refs_5_, bf16[256,512]{1,0:T(8,128)(2,1)S(1)} %collective-permute-done.10.refs_2_.refs_8_, bf16[256,512]{1,0:T(8,128)(2,1)S(1)} %collective-permute-done.1.refs_3_.refs_2_.refs_4_, ...), custom_call_target="tpu_custom_call" | custom-call | flops 402653184 | bytes 1835024 | tf_op jit(solution)/shard_map/pallas_call | solution.py:190
  77.9 3.4 %collective-permute-start.11 = (bf16[256,512]{1,0:T(8,128)(2,1)S(1)}, bf16[256,512]{1,0:T(8,128)(2,1)S(1)}, u32[]{:S(2)}, u32[]{:S(2)}) collective-permute-start(bf16[256,512]{1,0:T(8,128)(2,1)S(1)} %shard_map.124), channel_id=1, source_target_pairs={{0,4},{2,6},{4,8},{6,10},{8,12},{10,14},{1,5},{3,7},{5,9},{7,11},{... | collective-permute-start | bytes 786440 | tf_op jit(solution)/shard_map/ppermute | solution.py:22
  81.4 1.5 %collective-permute-start.15 = (bf16[256,512]{1,0:T(8,128)(2,1)S(1)}, bf16[256,512]{1,0:T(8,128)(2,1)S(1)}, u32[]{:S(2)}, u32[]{:S(2)}) collective-permute-start(bf16[256,512]{1,0:T(8,128)(2,1)S(1)} %collective-permute-done.10.refs_2_.refs_8_), channel_id=1, source_target_pairs={{4,0},{6,2},{8,4},{10,6},{12,8},{14,10},{5,1},{7,3},{9,5},{11,7},{... | collective-permute-start | bytes 786440 | tf_op jit(solution)/shard_map/ppermute | solution.py:22
  82.9 3.8 %shard_map.125 = (f32[256,512]{1,0:T(8,128)S(1)}, f32[256,512]{1,0:T(8,128)S(1)}) custom-call(s32[1,4]{1,0:T(1,128)S(1)} %copy-done.9, bf16[256,512]{1,0:T(8,128)(2,1)S(1)} %bitcast.32, bf16[256,512]{1,0:T(8,128)(2,1)S(1)} %bitcast.37, bf16[256,512]{1,0:T(8,128)(2,1)S(1)} %bitcast.43, bf16[256,512]{1,0:T(8,128)(2,1)} %collective-permute-done.16.refs_4_, ...), custom_call_target="tpu_custom_call" | custom-call | flops 805306368 | bytes 3145744 | tf_op jit(solution)/shard_map/pallas_call | solution.py:190
  86.6 1.3 %collective-permute-start.14 = (bf16[256,512]{1,0:T(8,128)(2,1)S(1)}, bf16[256,512]{1,0:T(8,128)(2,1)S(1)}, u32[]{:S(2)}, u32[]{:S(2)}) collective-permute-start(bf16[256,512]{1,0:T(8,128)(2,1)S(1)} %collective-permute-done.10.refs_2_.refs_8_), channel_id=1, source_target_pairs={{2,0},{4,2},{6,4},{8,6},{10,8},{12,10},{14,12},{3,1},{5,3},{7,5},{... | collective-permute-start | bytes 786440 | tf_op jit(solution)/shard_map/ppermute | solution.py:22
  88.0 6.9 %collective-permute-start.9 = (bf16[1,32,1024]{2,1,0:T(8,128)(2,1)S(1)}, bf16[1,32,1024]{2,1,0:T(8,128)(2,1)S(1)}, u32[]{:S(2)}, u32[]{:S(2)}) collective-permute-start(bf16[1,32,1024]{2,1,0:T(8,128)(2,1)S(1)} %dynamic-slice_convert_fusion.1), channel_id=1, source_target_pairs={{0,8},{2,10},{4,12},{6,14},{8,0},{10,2},{12,4},{14,6},{1,9},{3,11}... | collective-permute-start | bytes 196616 | tf_op jit(solution)/shard_map/ppermute | solution.py:26
  94.9 0.8 fusion
  95.7 3.0 %shard_map.126 = (bf16[256,512]{1,0:T(8,128)(2,1)}, bf16[256,512]{1,0:T(8,128)(2,1)}) custom-call(s32[1,4]{1,0:T(1,128)S(1)} %copy-done.9, bf16[256,512]{1,0:T(8,128)(2,1)S(1)} %bitcast.33, bf16[256,512]{1,0:T(8,128)(2,1)S(1)} %bitcast.38, bf16[256,512]{1,0:T(8,128)(2,1)S(1)} %collective-permute-done.12.refs_3_, ...), custom_call_target="tpu_custom_call" | custom-call | flops 536870912 | bytes 3145744 | tf_op jit(solution)/shard_map/pallas_call | solution.py:190
  98.7 1.9 %collective-permute-done.9 = bf16[1,32,1024]{2,1,0:T(8,128)(2,1)S(1)} collective-permute-done((bf16[1,32,1024]{2,1,0:T(8,128)(2,1)S(1)}, bf16[1,32,1024]{2,1,0:T(8,128)(2,1)S(1)}, u32[]{:S(2)}, u32[]{:S(2)}) %collective-permute-start.9) | collective-permute-done | bytes 65568 | tf_op jit(solution)/shard_map/ppermute | solution.py:26
  100.6 0.7 multiply_bitcast_fusion
  (31 shorter events, 0.2 us)
Async XLA Ops:
  0.6 11.9 %collective-permute-start = (bf16[256,512]{1,0:T(8,128)(2,1)}, bf16[256,512]{1,0:T(8,128)(2,1)S(1)}, u32[]{:S(2)}, u32[]{:S(2)}) collective-permute-start(bf16[256,512]{1,0:T(8,128)(2,1)} %bitcast.29), channel_id=1, source_target_pairs={{0,4},{2,6},{4,8},{6,10},{8,12},{10,14},{1,5},{3,7},{5,9},{7,11},{... | collective-permute-start | bytes 786440 | tf_op jit(solution)/shard_map/ppermute | solution.py:22
  5.6 11.5 %collective-permute-start.2 = (bf16[256,512]{1,0:T(8,128)(2,1)}, bf16[256,512]{1,0:T(8,128)(2,1)S(1)}, u32[]{:S(2)}, u32[]{:S(2)}) collective-permute-start(bf16[256,512]{1,0:T(8,128)(2,1)} %bitcast.34), channel_id=1, source_target_pairs={{0,4},{2,6},{4,8},{6,10},{8,12},{10,14},{1,5},{3,7},{5,9},{7,11},{... | collective-permute-start | bytes 786440 | tf_op jit(solution)/shard_map/ppermute | solution.py:22
  9.1 9.6 %collective-permute-start.4 = (bf16[256,512]{1,0:T(8,128)(2,1)}, bf16[256,512]{1,0:T(8,128)(2,1)S(1)}, u32[]{:S(2)}, u32[]{:S(2)}) collective-permute-start(bf16[256,512]{1,0:T(8,128)(2,1)} %bitcast.39), channel_id=1, source_target_pairs={{4,0},{6,2},{8,4},{10,6},{12,8},{14,10},{5,1},{7,3},{9,5},{11,7},{... | collective-permute-start | bytes 786440 | tf_op jit(solution)/shard_map/ppermute | solution.py:22
  10.4 6.7 %copy-start.2 = (bf16[1,256,512]{2,1,0:T(8,128)(2,1)S(1)}, bf16[1,256,512]{2,1,0:T(8,128)(2,1)}, u32[]{:S(2)}) copy-start(bf16[1,256,512]{2,1,0:T(8,128)(2,1)} %param.9) | copy-start | bytes 786436
  12.6 13.1 %copy-start.9 = (s32[1,4]{1,0:T(1,128)S(1)}, s32[1,4]{1,0:T(1,128)}, u32[]{:S(2)}) copy-start(s32[1,4]{1,0:T(1,128)} %refs_0_.11) | copy-start | bytes 52
  13.6 17.9 %copy-start = (bf16[512,1024]{1,0:T(8,128)(2,1)S(1)}, bf16[512,1024]{1,0:T(8,128)(2,1)}, u32[]{:S(2)}) copy-start(bf16[512,1024]{1,0:T(8,128)(2,1)} %weight_ref.1) | copy-start | bytes 3145732
  13.6 7.7 %collective-permute-start.1 = (bf16[256,512]{1,0:T(8,128)(2,1)S(1)}, bf16[256,512]{1,0:T(8,128)(2,1)S(1)}, u32[]{:S(2)}, u32[]{:S(2)}) collective-permute-start(bf16[256,512]{1,0:T(8,128)(2,1)S(1)} %broadcast_select_fusion.1), channel_id=1, source_target_pairs={{0,2},{2,0},{4,6},{6,4},{8,10},{10,8},{12,14},{14,12},{1,3},{3,1},... | collective-permute-start | bytes 786440 | tf_op jit(solution)/shard_map/ppermute | solution.py:26
  17.1 14.4 %copy-start.1 = (bf16[1,256,512]{2,1,0:T(8,128)(2,1)S(1)}, bf16[1,256,512]{2,1,0:T(8,128)(2,1)}, u32[]{:S(2)}) copy-start(bf16[1,256,512]{2,1,0:T(8,128)(2,1)} %param.8) | copy-start | bytes 786436
  17.1 14.4 %copy-start.4 = (bf16[1,256,512]{2,1,0:T(8,128)(2,1)S(1)}, bf16[1,256,512]{2,1,0:T(8,128)(2,1)}, u32[]{:S(2)}) copy-start(bf16[1,256,512]{2,1,0:T(8,128)(2,1)} %param.7) | copy-start | bytes 786436
  17.1 14.4 %copy-start.5 = (bf16[1,256,1024]{2,1,0:T(8,128)(2,1)S(1)}, bf16[1,256,1024]{2,1,0:T(8,128)(2,1)}, u32[]{:S(2)}) copy-start(bf16[1,256,1024]{2,1,0:T(8,128)(2,1)} %param.12) | copy-start | bytes 1572868
  17.1 8.5 %collective-permute-start.3 = (bf16[256,512]{1,0:T(8,128)(2,1)S(1)}, bf16[256,512]{1,0:T(8,128)(2,1)S(1)}, u32[]{:S(2)}, u32[]{:S(2)}) collective-permute-start(bf16[256,512]{1,0:T(8,128)(2,1)S(1)} %broadcast_select_fusion), channel_id=1, source_target_pairs={{0,2},{2,0},{4,6},{6,4},{8,10},{10,8},{12,14},{14,12},{1,3},{3,1},... | collective-permute-start | bytes 786440 | tf_op jit(solution)/shard_map/ppermute | solution.py:26
  27.2 8.9 %collective-permute-start.5 = (bf16[256,512]{1,0:T(8,128)(2,1)S(1)}, bf16[256,512]{1,0:T(8,128)(2,1)S(1)}, u32[]{:S(2)}, u32[]{:S(2)}) collective-permute-start(bf16[256,512]{1,0:T(8,128)(2,1)S(1)} %shard_map.119), channel_id=1, source_target_pairs={{0,4},{2,6},{4,8},{6,10},{8,12},{10,14},{1,5},{3,7},{5,9},{7,11},{... | collective-permute-start | bytes 786440 | tf_op jit(solution)/shard_map/ppermute | solution.py:22
  31.5 4.6 %copy-start.6 = (bf16[1,256,512]{2,1,0:T(8,128)(2,1)S(1)}, bf16[1,256,512]{2,1,0:T(8,128)(2,1)}, u32[]{:S(2)}) copy-start(bf16[1,256,512]{2,1,0:T(8,128)(2,1)} %param.10) | copy-start | bytes 786436
  37.1 1.5 %copy-start.7 = (bf16[256,512]{1,0:T(8,128)(2,1)}, bf16[256,512]{1,0:T(8,128)(2,1)S(1)}, u32[]{:S(2)}) copy-start(bf16[256,512]{1,0:T(8,128)(2,1)S(1)} %get-tuple-element.22.refs_2_.refs_6_) | copy-start | bytes 786436
  38.5 1.0 copy-start.3
  39.5 2.3 %collective-permute-start.6 = (bf16[256,1024]{1,0:T(8,128)(2,1)}, bf16[256,1024]{1,0:T(8,128)(2,1)}, u32[]{:S(2)}, u32[]{:S(2)}) collective-permute-start(bf16[256,1024]{1,0:T(8,128)(2,1)} %get-tuple-element.21), channel_id=1, source_target_pairs={{0,1},{1,0},{2,3},{3,2},{4,5},{5,4},{6,7},{7,6},{8,9},{9,8},{10,11... | collective-permute-start | bytes 1572872 | tf_op jit(solution)/shard_map/ppermute | solution.py:26
  43.3 1.1 %copy-start.10 = (f32[256,1024]{1,0:T(8,128)}, f32[256,1024]{1,0:T(8,128)S(1)}, u32[]{:S(2)}) copy-start(f32[256,1024]{1,0:T(8,128)S(1)} %convert_add_fusion) | copy-start | bytes 3145732
  44.3 13.3 %collective-permute-start.7 = (bf16[4,32,1024]{2,1,0:T(8,128)(2,1)}, bf16[4,32,1024]{2,1,0:T(8,128)(2,1)}, u32[]{:S(2)}, u32[]{:S(2)}) collective-permute-start(bf16[4,32,1024]{2,1,0:T(8,128)(2,1)} %fusion.1), channel_id=1, source_target_pairs={{0,2},{2,0},{4,6},{6,4},{8,10},{10,8},{12,14},{14,12},{1,3},{3,1},... | collective-permute-start | bytes 786440 | tf_op jit(solution)/shard_map/ppermute | solution.py:26
  45.9 32.1 %collective-permute-start.16 = (bf16[256,512]{1,0:T(8,128)(2,1)S(1)}, bf16[256,512]{1,0:T(8,128)(2,1)}, u32[]{:S(2)}, u32[]{:S(2)}) collective-permute-start(bf16[256,512]{1,0:T(8,128)(2,1)S(1)} %bitcast.41), channel_id=1, source_target_pairs={{2,0},{4,2},{6,4},{8,6},{10,8},{12,10},{14,12},{3,1},{5,3},{7,5},{... | collective-permute-start | bytes 786440 | tf_op jit(solution)/shard_map/ppermute | solution.py:22
  47.2 48.4 %collective-permute-start.13 = (bf16[256,512]{1,0:T(8,128)(2,1)S(1)}, bf16[256,512]{1,0:T(8,128)(2,1)S(1)}, u32[]{:S(2)}, u32[]{:S(2)}) collective-permute-start(bf16[256,512]{1,0:T(8,128)(2,1)S(1)} %collective-permute-done.4.refs_1_.refs_5_), channel_id=1, source_target_pairs={{4,0},{6,2},{8,4},{10,6},{12,8},{14,10},{5,1},{7,3},{9,5},{11,7},{... | collective-permute-start | bytes 786440 | tf_op jit(solution)/shard_map/ppermute | solution.py:22
  48.5 32.9 %collective-permute-start.17 = (bf16[256,512]{1,0:T(8,128)(2,1)}, bf16[256,512]{1,0:T(8,128)(2,1)S(1)}, u32[]{:S(2)}, u32[]{:S(2)}) collective-permute-start(bf16[256,512]{1,0:T(8,128)(2,1)} %copy-done.7), channel_id=1, source_target_pairs={{2,0},{4,2},{6,4},{8,6},{10,8},{12,10},{14,12},{3,1},{5,3},{7,5},{... | collective-permute-start | bytes 786440 | tf_op jit(solution)/shard_map/ppermute | solution.py:22
  49.8 24.4 %collective-permute-start.10 = (bf16[256,512]{1,0:T(8,128)(2,1)}, bf16[256,512]{1,0:T(8,128)(2,1)S(1)}, u32[]{:S(2)}, u32[]{:S(2)}) collective-permute-start(bf16[256,512]{1,0:T(8,128)(2,1)} %copy-done.7), channel_id=1, source_target_pairs={{4,0},{6,2},{8,4},{10,6},{12,8},{14,10},{5,1},{7,3},{9,5},{11,7},{... | collective-permute-start | bytes 786440 | tf_op jit(solution)/shard_map/ppermute | solution.py:22
  51.1 1.0 copy-start.8
  52.1 5.6 %copy-start.11 = (f32[256,1024]{1,0:T(8,128)S(1)}, f32[256,1024]{1,0:T(8,128)}, u32[]{:S(2)}) copy-start(f32[256,1024]{1,0:T(8,128)} %copy-done.10) | copy-start | bytes 3145732
  58.7 27.9 %collective-permute-start.8 = (bf16[2,32,1024]{2,1,0:T(8,128)(2,1)S(1)}, bf16[2,32,1024]{2,1,0:T(8,128)(2,1)S(1)}, u32[]{:S(2)}, u32[]{:S(2)}) collective-permute-start(bf16[2,32,1024]{2,1,0:T(8,128)(2,1)S(1)} %fusion.2), channel_id=1, source_target_pairs={{0,4},{2,6},{4,0},{6,2},{8,12},{10,14},{12,8},{14,10},{1,5},{3,7},... | collective-permute-start | bytes 393224 | tf_op jit(solution)/shard_map/ppermute | solution.py:26
  74.3 21.4 %collective-permute-start.12 = (bf16[256,512]{1,0:T(8,128)(2,1)S(1)}, bf16[256,512]{1,0:T(8,128)(2,1)S(1)}, u32[]{:S(2)}, u32[]{:S(2)}) collective-permute-start(bf16[256,512]{1,0:T(8,128)(2,1)S(1)} %collective-permute-done.4.refs_1_.refs_5_), channel_id=1, source_target_pairs={{2,0},{4,2},{6,4},{8,6},{10,8},{12,10},{14,12},{3,1},{5,3},{7,5},{... | collective-permute-start | bytes 786440 | tf_op jit(solution)/shard_map/ppermute | solution.py:22
  77.9 10.1 %collective-permute-start.11 = (bf16[256,512]{1,0:T(8,128)(2,1)S(1)}, bf16[256,512]{1,0:T(8,128)(2,1)S(1)}, u32[]{:S(2)}, u32[]{:S(2)}) collective-permute-start(bf16[256,512]{1,0:T(8,128)(2,1)S(1)} %shard_map.124), channel_id=1, source_target_pairs={{0,4},{2,6},{4,8},{6,10},{8,12},{10,14},{1,5},{3,7},{5,9},{7,11},{... | collective-permute-start | bytes 786440 | tf_op jit(solution)/shard_map/ppermute | solution.py:22
  81.4 14.3 %collective-permute-start.15 = (bf16[256,512]{1,0:T(8,128)(2,1)S(1)}, bf16[256,512]{1,0:T(8,128)(2,1)S(1)}, u32[]{:S(2)}, u32[]{:S(2)}) collective-permute-start(bf16[256,512]{1,0:T(8,128)(2,1)S(1)} %collective-permute-done.10.refs_2_.refs_8_), channel_id=1, source_target_pairs={{4,0},{6,2},{8,4},{10,6},{12,8},{14,10},{5,1},{7,3},{9,5},{11,7},{... | collective-permute-start | bytes 786440 | tf_op jit(solution)/shard_map/ppermute | solution.py:22
  86.6 9.0 %collective-permute-start.14 = (bf16[256,512]{1,0:T(8,128)(2,1)S(1)}, bf16[256,512]{1,0:T(8,128)(2,1)S(1)}, u32[]{:S(2)}, u32[]{:S(2)}) collective-permute-start(bf16[256,512]{1,0:T(8,128)(2,1)S(1)} %collective-permute-done.10.refs_2_.refs_8_), channel_id=1, source_target_pairs={{2,0},{4,2},{6,4},{8,6},{10,8},{12,10},{14,12},{3,1},{5,3},{7,5},{... | collective-permute-start | bytes 786440 | tf_op jit(solution)/shard_map/ppermute | solution.py:22
  88.0 12.6 %collective-permute-start.9 = (bf16[1,32,1024]{2,1,0:T(8,128)(2,1)S(1)}, bf16[1,32,1024]{2,1,0:T(8,128)(2,1)S(1)}, u32[]{:S(2)}, u32[]{:S(2)}) collective-permute-start(bf16[1,32,1024]{2,1,0:T(8,128)(2,1)S(1)} %dynamic-slice_convert_fusion.1), channel_id=1, source_target_pairs={{0,8},{2,10},{4,12},{6,14},{8,0},{10,2},{12,4},{14,6},{1,9},{3,11}... | collective-permute-start | bytes 196616 | tf_op jit(solution)/shard_map/ppermute | solution.py:26

commit v2 on v1

v2 whole, which is shorter than its diff:
```python
import functools
import math

import jax
import jax.numpy as jnp
from jax import lax
from jax.experimental import pallas as pl
from jax.experimental.pallas import tpu as pltpu
from jax.sharding import PartitionSpec as P

HEAD = 128
EPS = 1e-05
SCALE = 1.0 / math.sqrt(HEAD)
BF16 = jnp.bfloat16
F32 = jnp.float32
VMEM = pl.BlockSpec(memory_space=pltpu.VMEM)
ANY = pl.BlockSpec(memory_space=pl.ANY)


def shifted(block, distance):
    devices = range(lax.axis_size("ctx"))
    return lax.ppermute(block, "ctx", [(i, i + distance) for i in devices if i + distance in devices])


def swapped(block, axis, step):
    return lax.ppermute(block, axis, [(i, i ^ step) for i in range(lax.axis_size(axis))])


def dot(a, b, da, db):
    return lax.dot_general(a, b, (((da,), (db,)), ((), ())), preferred_element_type=F32)


def ends_of(lengths_ref):
    ends, total = [], jnp.int32(0)
    for user in range(lengths_ref.shape[1]):
        total = total + lengths_ref[0, user]
        ends.append(total)
    return ends


def first_place(ends, places):
    first = jnp.zeros_like(places)
    for end in ends:
        first = jnp.where(places >= end, end, first)
    return first


def past_place(ends, places):
    past = jnp.zeros_like(places) + ends[-1]
    for end in ends[-2::-1]:
        past = jnp.where(places < end, end, past)
    return past


def crossing(ends, place, distance, tok):
    return first_place(ends, place) - (place - distance * tok), past_place(ends, place) - place


def own_mask(ends, place, tok, transposed):
    rows = place + lax.broadcasted_iota(jnp.int32, (tok, tok), 0)
    columns = place + lax.broadcasted_iota(jnp.int32, (tok, tok), 1)
    ids = place + lax.broadcasted_iota(jnp.int32, (tok, 1), 0)
    if transposed:
        return (columns >= rows) & (columns < past_place(ends, ids))
    return (columns <= rows) & (columns >= first_place(ends, ids))


def row_numbers(tok):
    return lax.broadcasted_iota(jnp.int32, (tok, HEAD), 0)


def half_scores(a, b):
    return dot(a, b, 1, 1) * (0.5 * SCALE)


def silu(half):
    return half * jnp.tanh(half) + half


def slopes(half):
    turn = jnp.tanh(half)
    attend = half * turn + half
    return attend, (1.0 + turn) + attend * (1.0 - turn)


def staggered(width, begin, finish):
    heads = [slice(h, h + HEAD) for h in range(0, width, HEAD)]
    begun = begin(heads[0])
    for now, after in zip(heads, heads[1:] + [None]):
        ready = begun
        if after is not None:
            begun = begin(after)
        finish(now, ready)


def mix_kernel(ahead, distances, project, *refs):
    count = len(distances)
    lengths_ref, q_ref = refs[:2]
    k_refs, v_refs = refs[2 : 2 + count], refs[2 + count : 2 + 2 * count]
    mixed_ref, total_ref = refs[-2:]
    if project:
        out_grad_ref, weight_ref, grad_gated_ref, total_ref = refs[2 + 2 * count :]
        grad_gated_ref[...] = dot(out_grad_ref[...], weight_ref[...], 1, 1)
    tok, width = q_ref.shape
    place = (lax.axis_index("ctx") + ahead) * tok
    ends = ends_of(lengths_ref)

    def pair(k_ref, v_ref, mask, dead, alive):
        def finish(cols, half):
            attend = silu(half)
            if mask is not None:
                total_ref[:, cols] = dot(jnp.where(mask, attend, 0.0).astype(BF16), v_ref[:, cols], 1, 0)
                return
            number = row_numbers(tok)
            v = jnp.where(number >= dead, v_ref[:, cols], 0.0).astype(BF16)
            term = dot(attend.astype(BF16), v, 1, 0)
            total_ref[:, cols] += jnp.where(number < alive, term, 0.0)

        staggered(width, lambda cols: half_scores(q_ref[:, cols], k_ref[:, cols]), finish)

    if distances[0] > 0:
        total_ref[...] = jnp.zeros_like(total_ref)
    for n, distance in enumerate(distances):
        if distance == 0:
            pair(k_refs[n], v_refs[n], own_mask(ends, place, tok, False), None, None)
        else:
            dead, alive = crossing(ends, place, distance, tok)
            pl.when(dead < tok)(functools.partial(pair, k_refs[n], v_refs[n], None, dead, alive))
    if not project:
        mixed_ref[...] = total_ref[...].astype(BF16)


def norm_kernel(near_ref, far_ref, grad_gated_ref, gates_ref, gated_ref, grad_gates_ref, grad_mixed_ref):
    mixed = near_ref[...] + far_ref[...].astype(F32)
    gates = gates_ref[...].astype(F32)
    grad_gated = grad_gated_ref[...]
    centered = mixed - jnp.mean(mixed, axis=1, keepdims=True)
    inverse = lax.rsqrt(jnp.mean(centered * centered, axis=1, keepdims=True) + EPS)
    normed = centered * inverse
    gated_ref[...] = (normed * gates).astype(BF16)
    grad_gates_ref[...] = (grad_gated * normed).astype(BF16)
    grad_normed = grad_gated * gates
    grad_mixed_ref[...] = (
        (
            grad_normed
            - jnp.mean(grad_normed, axis=1, keepdims=True)
            - normed * jnp.mean(grad_normed * normed, axis=1, keepdims=True)
        )
        * inverse
    ).astype(BF16)


def query_grad_kernel(ahead, distances, *refs):
    count = len(distances)
    lengths_ref, q_ref, grad_ref = refs[:3]
    k_refs, v_refs = refs[3 : 3 + count], refs[3 + count : 3 + 2 * count]
    out_ref, total_ref = refs[-2:]
    tok, width = q_ref.shape
    place = (lax.axis_index("ctx") + ahead) * tok
    ends = ends_of(lengths_ref)

    def pair(k_ref, v_ref, mask, dead, alive):
        def begin(cols):
            return half_scores(q_ref[:, cols], k_ref[:, cols]), dot(grad_ref[:, cols], v_ref[:, cols], 1, 1)

        def finish(cols, begun):
            half, pull = begun
            score_grad = pull * slopes(half)[1]
            if mask is not None:
                total_ref[:, cols] = dot(jnp.where(mask, score_grad, 0.0).astype(BF16), k_ref[:, cols], 1, 0)
                return
            number = row_numbers(tok)
            k = jnp.where(number >= dead, k_ref[:, cols], 0.0).astype(BF16)
            term = dot(score_grad.astype(BF16), k, 1, 0)
            total_ref[:, cols] += jnp.where(number < alive, term, 0.0)

        staggered(width, begin, finish)

    if distances[0] > 0:
        total_ref[...] = jnp.zeros_like(total_ref)
    for n, distance in enumerate(distances):
        if distance == 0:
            pair(k_refs[n], v_refs[n], own_mask(ends, place, tok, False), None, None)
        else:
            dead, alive = crossing(ends, place, distance, tok)
            pl.when(dead < tok)(functools.partial(pair, k_refs[n], v_refs[n], None, dead, alive))
    total = total_ref[...] * (0.5 * SCALE)
    out_ref[...] = total.astype(out_ref.dtype)


def key_grad_kernel(distances, last, *refs):
    count = len(distances)
    lengths_ref, k_ref, v_ref = refs[:3]
    q_refs, grad_refs = refs[3 : 3 + count], refs[3 + count : 3 + 2 * count]
    key_out, value_out, key_total, value_total = refs[-4:] if last else refs[-2:] * 2
    tok, width = k_ref.shape
    place = lax.axis_index("ctx") * tok
    ends = ends_of(lengths_ref)

    def pair(q_ref, grad_ref, mask, dead, alive):
        def begin(cols):
            return half_scores(k_ref[:, cols], q_ref[:, cols]), dot(v_ref[:, cols], grad_ref[:, cols], 1, 1)

        def finish(cols, begun):
            half, pull = begun
            attend, slope = slopes(half)
            score_grad = pull * slope
            if mask is not None:
                value_total[:, cols] = dot(jnp.where(mask, attend, 0.0).astype(BF16), grad_ref[:, cols], 1, 0)
                key_total[:, cols] = dot(jnp.where(mask, score_grad, 0.0).astype(BF16), q_ref[:, cols], 1, 0)
                return
            number = row_numbers(tok)
            grad = jnp.where(number < alive, grad_ref[:, cols], 0.0).astype(BF16)
            q = jnp.where(number < alive, q_ref[:, cols], 0.0).astype(BF16)
            value_term = dot(attend.astype(BF16), grad, 1, 0)
            key_term = dot(score_grad.astype(BF16), q, 1, 0)
            value_total[:, cols] += jnp.where(number >= dead, value_term, 0.0)
            key_total[:, cols] += jnp.where(number >= dead, key_term, 0.0)

        staggered(width, begin, finish)

    if distances[0] > 0:
        key_total[...] = refs[3 + 2 * count][...]
        value_total[...] = refs[4 + 2 * count][...]
    for n, distance in enumerate(distances):
        if distance == 0:
            pair(q_refs[n], grad_refs[n], own_mask(ends, place, tok, True), None, None)
        else:
            dead, alive = crossing(ends, place + distance * tok, distance, tok)
            pl.when(dead < tok)(functools.partial(pair, q_refs[n], grad_refs[n], None, dead, alive))
    if last:
        key_out[...] = (key_total[...] * (0.5 * SCALE)).astype(BF16)
        value_out[...] = value_total[...].astype(BF16)


def parted(total, bit, keep_ref, give_ref):
    for part in range(keep_ref.shape[0]):
        keep_ref[part] = total(2 * part + bit)
        give_ref[part] = total(2 * part + 1 - bit).astype(BF16)


def out_kernel(gated_ref, weight_ref, out_ref):
    out_ref[...] = dot(gated_ref[...], weight_ref[...], 1, 0).astype(BF16)


def weight_kernel(gated_ref, out_grad_ref, keep_ref, give_ref, total_ref):
    total_ref[...] = dot(gated_ref[...], out_grad_ref[...], 0, 0)
    rows = keep_ref.shape[1]
    parted(
        lambda chunk: total_ref[pl.ds(pl.multiple_of(chunk * rows, rows), rows), :],
        lax.axis_index("dp"),
        keep_ref,
        give_ref,
    )


def part_kernel(step, kept_ref, came_ref, keep_ref, give_ref):
    parted(
        lambda chunk: kept_ref[chunk] + came_ref[chunk].astype(F32),
        (lax.axis_index("ctx") // step) % 2,
        keep_ref,
        give_ref,
    )


def last_part_kernel(factor, kept_ref, came_ref, out_ref):
    out_ref[...] = (kept_ref[0] + came_ref[0].astype(F32)) * factor


def add_kernel(a_ref, b_ref, out_ref):
    out_ref[...] = (a_ref[...] + b_ref[...].astype(F32)).astype(out_ref.dtype)


def pick_kernel(even_ref, odd_ref, out_ref):
    even = lax.axis_index("ctx") % 2 == 0

    @pl.when(even)
    def _():
        out_ref[...] = even_ref[...]

    @pl.when(jnp.logical_not(even))
    def _():
        out_ref[...] = odd_ref[...]


def call(kernel, outs, args, micros, scratch=(), after=()):
    held = len(args)

    def body(*refs):
        kernel(*refs[:held], *refs[held + len(after) :])

    shapes = [jax.ShapeDtypeStruct(shape, dtype) for shape, dtype in outs]
    return pl.pallas_call(
        body,
        out_shape=shapes,
        in_specs=[VMEM] * len(args) + [ANY] * len(after),
        out_specs=[VMEM] * len(shapes),
        scratch_shapes=list(scratch),
        cost_estimate=pl.CostEstimate(flops=int(micros * 1.0e6), bytes_accessed=0, transcendentals=0),
        compiler_params=pltpu.CompilerParams(vmem_limit_bytes=48 * 1024 * 1024),
    )(*args, *after)


def picked(even_sends, odd_sends, after=()):
    (sent,) = call(
        pick_kernel, [(even_sends.shape, even_sends.dtype)], [even_sends, odd_sends], 0.2, (), after
    )
    return sent


def exchanged(even_sends, odd_sends):
    return swapped(picked(even_sends, odd_sends), "ctx", 1)


def earlier_blocks(block, most):
    blocks = {0: block}
    for distance in range(2, most + 1, 2):
        blocks[distance] = shifted(blocks[distance - 2], 2)
        blocks[distance - 1] = exchanged(blocks[distance - 2], blocks[distance])
    return blocks


def later_blocks(block, most):
    blocks = {0: block}
    for distance in range(2, most + 1, 2):
        blocks[distance] = shifted(blocks[distance - 2], -2)
    for distance in range(1, most, 2):
        blocks[distance] = exchanged(blocks[distance + 1], blocks[distance - 1])
    return blocks


def local(queries, keys, values, gates, out_weight, grad_out, lengths):
    q, k, v, gate_rows, out_grad = queries[0], keys[0], values[0], gates[0], grad_out[0]
    tok, width = q.shape
    model = out_grad.shape[1]
    count, cores = lax.axis_size("ctx"), lax.axis_size("dp")
    reach = min(8, count // 2)
    mid = reach // 2
    one, wide = [((tok, width), BF16)], [((tok, width), F32)]
    total = pltpu.VMEM((tok, width), F32)
    key_at = earlier_blocks(k, mid)
    value_at = earlier_blocks(v, mid)
    query_at = {0: q}
    for distance in range(2, reach + 1, 2):
        query_at[distance] = shifted(query_at[distance - 2], -2)

    near = list(range(mid + 1))
    back = list(range(1, mid + 1))
    far = [mid + d for d in back]
    back_keys = [key_at[d] for d in back] + [value_at[d] for d in back]
    near_keys = [key_at[d] for d in near] + [value_at[d] for d in near]
    (far_term,) = call(
        functools.partial(mix_kernel, mid, far, False),
        one,
        [lengths, query_at[mid], *back_keys],
        1.0,
        [total],
    )
    far_mixed = shifted(far_term, mid)
    sent = {d: picked(query_at[d + 1], query_at[d - 1], [far_term]) for d in range(1, reach, 2)}
    for distance, block in sent.items():
        query_at[distance] = swapped(block, "ctx", 1)
    grad_gated, near_mixed = call(
        functools.partial(mix_kernel, 0, near, True),
        wide * 2,
        [lengths, q, *near_keys, out_grad, out_weight],
        2.0,
        (),
        list(sent.values()),
    )
    gated, grad_gates, grad_mixed = call(
        norm_kernel,
        one * 3,
        [near_mixed, far_mixed, grad_gated, gate_rows],
        1.0,
    )
    grad_at = later_blocks(grad_mixed, reach)
    chunk = (width // (count * cores), model)
    keep, give = call(
        weight_kernel,
        [((count, *chunk), F32), ((count, *chunk), BF16)],
        [gated, out_grad],
        1.5,
        [pltpu.VMEM((width, model), F32)],
    )
    (output,) = call(out_kernel, [((tok, model), BF16)], [gated, out_weight], 1.0)
    came = swapped(give, "dp", 1)
    arrived = [came]
    step = 1
    while step < count:
        parts = (count // (2 * step), *chunk)
        keep, give = call(
            functools.partial(part_kernel, step),
            [(parts, F32), (parts, BF16)],
            [keep, came],
            0.8,
            (),
            [query_at[1]] if step == 1 else (),
        )
        came = swapped(give, "ctx", step)
        arrived.append(came)
        step *= 2
    (grad_weight,) = call(
        functools.partial(last_part_kernel, 1.0 / math.sqrt(cores * count * tok)),
        [(chunk, F32)],
        [keep, came],
        0.5,
    )
    (near_query,) = call(
        functools.partial(query_grad_kernel, 0, near),
        wide,
        [lengths, q, grad_mixed, *near_keys],
        2.5,
        [total],
    )
    (far_query_term,) = call(
        functools.partial(query_grad_kernel, mid, far),
        one,
        [lengths, query_at[mid], grad_at[mid], *back_keys],
        1.5,
        [total],
        [near_query, output, keep, *[query_at[d] for d in far]],
    )
    far_query = shifted(far_query_term, mid)
    grads = ()
    groups = [
        [d for d in near if d % 2 == 0],
        [d for d in near if d % 2 == 1] + [d for d in far if d % 2 == 0],
        [d for d in far if d % 2 == 1],
    ]
    for n, group in enumerate(groups):
        last = n == len(groups) - 1
        grads = call(
            functools.partial(key_grad_kernel, group, last),
            (one if last else wide) * 2,
            [lengths, k, v, *[query_at[d] for d in group], *[grad_at[d] for d in group], *grads],
            len(group) * 0.9,
            [total] * 2 if last else (),
            arrived[1:2] if n == 1 else (),
        )
    key_grad, value_grad = grads
    (query_grad,) = call(add_kernel, one, [near_query, far_query], 0.3)
    return (
        output[None],
        grad_weight,
        query_grad[None],
        key_grad[None],
        value_grad[None],
        grad_gates[None],
    )


def solution(mesh):
    rows = P(("groups", "dp"), "ctx", None)
    in_specs = (rows, rows, rows, rows, P(), rows, P(("groups", "dp"), None))
    out_specs = (rows, P(("groups", "ctx", "dp"), None), rows, rows, rows, rows)
    return jax.shard_map(local, mesh=mesh, in_specs=in_specs, out_specs=out_specs, check_vma=False)
```

time: 102 us -> 75.8 us (0.74)
  Pallas kernels: 19.5 us -> 10.7 us
  waiting for transfers between devices: 31.4 us -> 23.1 us
  other arithmetic: 4.99 us -> 0 us
  starting transfers between devices: 41.3 us -> 37.6 us
    ppermute x12 -> x8, waiting for transfers between devices: 17.9 us -> 8.78 us  [shifted(): lax.ppermute(block, 'ctx', [(i, i + distance) for i in devices if i + dis...]
    pallas_call x9 -> x21, Pallas kernels: 19.5 us -> 10.7 us  [call(): pl.pallas_call(body, out_shape=shapes, in_specs=[VMEM] * len(args) + [ANY...]
    ppermute x12 -> x8, starting transfers between devices: 26.6 us -> 19.9 us  [shifted(): lax.ppermute(block, 'ctx', [(i, i + distance) for i in devices if i + dis...]
    ppermute x6 -> x10, starting transfers between devices: 14.6 us -> 17.7 us  [swapped(): lax.ppermute(block, axis, [(i, i ^ step) for i in range(lax.axis_size(axi...]
    add x3 -> x0, other arithmetic: 2.53 us -> none  [the longest x1 1.49 us: summed_rows(): total = keep + swapped(give, 'dp', 1).astype(F32)]
    select_n x2 -> x0, other arithmetic: 1.02 us -> none  [earlier_blocks(): jnp.where(even, blocks[distance - 2], blocks[distance])]
    ppermute x6 -> x10, waiting for transfers between devices: 13.5 us -> 14.3 us  [swapped(): lax.ppermute(block, axis, [(i, i ^ step) for i in range(lax.axis_size(axi...]
    unnamed x24 -> x18, local copies, waits for them, and re-layouts: 2.21 us -> 2.88 us
  transfers between devices with their start and end apart: 18 -> 18, of which waited for: 9 -> 8; matrix products, arithmetic and copies ran while one was open for 3% -> 0% of each run, Pallas kernels for 15% -> 11%
where the time goes in v2:
time: 75.8 us; the launch traced here: 75.3 us
  starting transfers between devices  37.6 us (50%)
  waiting for transfers between devices  23.1 us (30%)
  Pallas kernels  10.7 us (14%)
  local copies, waits for them, and re-layouts  2.88 us (4%)
  between operations  0.93 us (1%)
    ppermute x8, starting transfers between devices, shifted(): lax.ppermute(block, 'ctx', [(i, i + distance) for i in devices if i + dis...  19.9 us
    ppermute x10, starting transfers between devices, swapped(): lax.ppermute(block, axis, [(i, i ^ step) for i in range(lax.axis_size(axi...  17.7 us
    ppermute x10, waiting for transfers between devices, swapped(): lax.ppermute(block, axis, [(i, i ^ step) for i in range(lax.axis_size(axi...  14.3 us
    pallas_call x21, Pallas kernels, call(): pl.pallas_call(body, out_shape=shapes, in_specs=[VMEM] * len(args) + [ANY...  10.7 us
    ppermute x8, waiting for transfers between devices, shifted(): lax.ppermute(block, 'ctx', [(i, i + distance) for i in devices if i + dis...  8.78 us
    unnamed x18, local copies, waits for them, and re-layouts  2.88 us
  transfers between devices with their start and end apart: 18, of which 8 were waited for; matrix products, arithmetic and copies ran while one was open for 0% of the time, Pallas kernels for 11%

profile of v2, /device:TPU:0, one launch (start us, length us, event | category | flops | bytes accessed | tf_op | source)
XLA Modules:
  0.0 75.3 jit_solution(12198062573954549568)
XLA Ops:
  0.6 4.9 %collective-permute-start = (bf16[256,512]{1,0:T(8,128)(2,1)}, bf16[256,512]{1,0:T(8,128)(2,1)S(1)}, u32[]{:S(2)}, u32[]{:S(2)}) collective-permute-start(bf16[256,512]{1,0:T(8,128)(2,1)} %bitcast.10), channel_id=1, source_target_pairs={{0,4},{2,6},{4,8},{6,10},{8,12},{10,14},{1,5},{3,7},{5,9},{7,11},{... | collective-permute-start | bytes 786440 | tf_op jit(solution)/shard_map/ppermute | solution.py:22
  5.6 3.5 %collective-permute-start.2 = (bf16[256,512]{1,0:T(8,128)(2,1)}, bf16[256,512]{1,0:T(8,128)(2,1)S(1)}, u32[]{:S(2)}, u32[]{:S(2)}) collective-permute-start(bf16[256,512]{1,0:T(8,128)(2,1)} %bitcast.17), channel_id=1, source_target_pairs={{0,4},{2,6},{4,8},{6,10},{8,12},{10,14},{1,5},{3,7},{5,9},{7,11},{... | collective-permute-start | bytes 786440 | tf_op jit(solution)/shard_map/ppermute | solution.py:22
  9.1 1.3 %collective-permute-start.4 = (bf16[256,512]{1,0:T(8,128)(2,1)}, bf16[256,512]{1,0:T(8,128)(2,1)S(1)}, u32[]{:S(2)}, u32[]{:S(2)}) collective-permute-start(bf16[256,512]{1,0:T(8,128)(2,1)} %bitcast.24), channel_id=1, source_target_pairs={{4,0},{6,2},{8,4},{10,6},{12,8},{14,10},{5,1},{7,3},{9,5},{11,7},{... | collective-permute-start | bytes 786440 | tf_op jit(solution)/shard_map/ppermute | solution.py:22
  10.4 2.2 %collective-permute-done.refs_1_.refs_3_.refs_4_.refs_5_ = bf16[256,512]{1,0:T(8,128)(2,1)S(1)} collective-permute-done((bf16[256,512]{1,0:T(8,128)(2,1)}, bf16[256,512]{1,0:T(8,128)(2,1)S(1)}, u32[]{:S(2)}, u32[]{:S(2)}) %collective-permute-start) | collective-permute-done | bytes 262176 | tf_op jit(solution)/shard_map/ppermute | solution.py:22
  12.6 0.9 %copy-done = bf16[1,256,512]{2,1,0:T(8,128)(2,1)S(1)} copy-done((bf16[1,256,512]{2,1,0:T(8,128)(2,1)S(1)}, bf16[1,256,512]{2,1,0:T(8,128)(2,1)}, u32[]{:S(2)}) %copy-start) | copy-done | bytes 262168
  13.6 0.0 copy-start.8
  13.6 1.6 %collective-permute-start.1 = (bf16[256,512]{1,0:T(8,128)(2,1)S(1)}, bf16[256,512]{1,0:T(8,128)(2,1)S(1)}, u32[]{:S(2)}, u32[]{:S(2)}) collective-permute-start(bf16[256,512]{1,0:T(8,128)(2,1)S(1)} %shard_map.118), channel_id=1, source_target_pairs={{0,2},{2,0},{4,6},{6,4},{8,10},{10,8},{12,14},{14,12},{1,3},{3,1},... | collective-permute-start | bytes 786440 | tf_op jit(solution)/shard_map/ppermute | solution.py:26
  15.2 1.9 %collective-permute-done.2.refs_1_.refs_5_.refs_7_.refs_8_.refs_6_ = bf16[256,512]{1,0:T(8,128)(2,1)S(1)} collective-permute-done((bf16[256,512]{1,0:T(8,128)(2,1)}, bf16[256,512]{1,0:T(8,128)(2,1)S(1)}, u32[]{:S(2)}, u32[]{:S(2)}) %collective-permute-start.2) | collective-permute-done | bytes 262176 | tf_op jit(solution)/shard_map/ppermute | solution.py:22
  17.1 0.0 copy-start.4
  17.1 1.6 %collective-permute-start.3 = (bf16[256,512]{1,0:T(8,128)(2,1)S(1)}, bf16[256,512]{1,0:T(8,128)(2,1)S(1)}, u32[]{:S(2)}, u32[]{:S(2)}) collective-permute-start(bf16[256,512]{1,0:T(8,128)(2,1)S(1)} %shard_map.119), channel_id=1, source_target_pairs={{0,2},{2,0},{4,6},{6,4},{8,10},{10,8},{12,14},{14,12},{1,3},{3,1},... | collective-permute-start | bytes 786440 | tf_op jit(solution)/shard_map/ppermute | solution.py:26
  18.7 1.3 %collective-permute-start.5 = (bf16[256,512]{1,0:T(8,128)(2,1)S(1)}, bf16[256,512]{1,0:T(8,128)(2,1)S(1)}, u32[]{:S(2)}, u32[]{:S(2)}) collective-permute-start(bf16[256,512]{1,0:T(8,128)(2,1)S(1)} %collective-permute-done.4.refs_1_.refs_0_.refs_4_), channel_id=1, source_target_pairs={{4,0},{6,2},{8,4},{10,6},{12,8},{14,10},{5,1},{7,3},{9,5},{11,7},{... | collective-permute-start | bytes 786440 | tf_op jit(solution)/shard_map/ppermute | solution.py:22
  20.0 1.3 %collective-permute-done.1.refs_2_.refs_3_.refs_4_ = bf16[256,512]{1,0:T(8,128)(2,1)S(1)} collective-permute-done((bf16[256,512]{1,0:T(8,128)(2,1)S(1)}, bf16[256,512]{1,0:T(8,128)(2,1)S(1)}, u32[]{:S(2)}, u32[]{:S(2)}) %collective-permute-start.1) | collective-permute-done | bytes 262176 | tf_op jit(solution)/shard_map/ppermute | solution.py:26
  21.2 4.4 %collective-permute-done.3.refs_4_.refs_6_.refs_7_.refs_5_ = bf16[256,512]{1,0:T(8,128)(2,1)S(1)} collective-permute-done((bf16[256,512]{1,0:T(8,128)(2,1)S(1)}, bf16[256,512]{1,0:T(8,128)(2,1)S(1)}, u32[]{:S(2)}, u32[]{:S(2)}) %collective-permute-start.3) | collective-permute-done | bytes 262176 | tf_op jit(solution)/shard_map/ppermute | solution.py:26
  25.6 0.1 shard_map.120.refs_2_
  25.8 0.0 copy-start.3
  25.8 4.4 %collective-permute-start.6 = (bf16[256,512]{1,0:T(8,128)(2,1)S(1)}, bf16[256,512]{1,0:T(8,128)(2,1)S(1)}, u32[]{:S(2)}, u32[]{:S(2)}) collective-permute-start(bf16[256,512]{1,0:T(8,128)(2,1)S(1)} %shard_map.120.refs_2_), channel_id=1, source_target_pairs={{0,4},{2,6},{4,8},{6,10},{8,12},{10,14},{1,5},{3,7},{5,9},{7,11},{... | collective-permute-start | bytes 786440 | tf_op jit(solution)/shard_map/ppermute | solution.py:22
  30.3 0.0 copy-start.1
  30.4 0.9 %copy-done.1 = bf16[1,256,512]{2,1,0:T(8,128)(2,1)S(1)} copy-done((bf16[1,256,512]{2,1,0:T(8,128)(2,1)S(1)}, bf16[1,256,512]{2,1,0:T(8,128)(2,1)}, u32[]{:S(2)}) %copy-start.1) | copy-done | bytes 262168
  31.2 0.2 copy-done.5
  31.4 0.9 %shard_map.123 = (f32[256,512]{1,0:T(8,128)S(1)}, f32[256,512]{1,0:T(8,128)S(1)}) custom-call(s32[1,4]{1,0:T(1,128)S(1)} %copy-done.8, bf16[256,512]{1,0:T(8,128)(2,1)S(1)} %bitcast.26, bf16[256,512]{1,0:T(8,128)(2,1)S(1)} %bitcast.12, bf16[256,512]{1,0:T(8,128)(2,1)S(1)} %collective-permute-done.1.refs_2_.refs_3_.refs_4_, ...), custom_call_target="tpu_custom_call" | custom-call | flops 2000000 | tf_op jit(solution)/shard_map/pallas_call | solution.py:293
  32.3 2.5 %collective-permute-done.6.refs_1_ = bf16[256,512]{1,0:T(8,128)(2,1)S(1)} collective-permute-done((bf16[256,512]{1,0:T(8,128)(2,1)S(1)}, bf16[256,512]{1,0:T(8,128)(2,1)S(1)}, u32[]{:S(2)}, u32[]{:S(2)}) %collective-permute-start.6) | collective-permute-done | bytes 262176 | tf_op jit(solution)/shard_map/ppermute | solution.py:22
  34.8 1.0 %shard_map.124 = (bf16[256,512]{1,0:T(8,128)(2,1)S(1)}, bf16[256,512]{1,0:T(8,128)(2,1)}, bf16[256,512]{1,0:T(8,128)(2,1)S(1)}) custom-call(f32[256,512]{1,0:T(8,128)S(1)} %get-tuple-element.25.refs_0_, bf16[256,512]{1,0:T(8,128)(2,1)S(1)} %collective-permute-done.6.refs_1_, f32[256,512]{1,0:T(8,128)S(1)} %get-tuple-element.26.refs_2_, ...), custom_call_target="tpu_custom_call" | custom-call | flops 1000000 | tf_op jit(solution)/shard_map/pallas_call | solution.py:293
  35.8 0.7 shard_map.126
  36.5 0.1 collective-permute-start.7
  36.6 1.6 %collective-permute-start.8 = (bf16[256,512]{1,0:T(8,128)(2,1)S(1)}, bf16[256,512]{1,0:T(8,128)(2,1)S(1)}, u32[]{:S(2)}, u32[]{:S(2)}) collective-permute-start(bf16[256,512]{1,0:T(8,128)(2,1)S(1)} %shard_map.121.refs_10_), channel_id=1, source_target_pairs={{0,2},{2,0},{4,6},{6,4},{8,10},{10,8},{12,14},{14,12},{1,3},{3,1},... | collective-permute-start | bytes 786440 | tf_op jit(solution)/shard_map/ppermute | solution.py:26
  38.2 1.3 %collective-permute-start.12 = (bf16[256,512]{1,0:T(8,128)(2,1)S(1)}, bf16[256,512]{1,0:T(8,128)(2,1)S(1)}, u32[]{:S(2)}, u32[]{:S(2)}) collective-permute-start(bf16[256,512]{1,0:T(8,128)(2,1)S(1)} %get-tuple-element.36.refs_2_.refs_1_.refs_5_), channel_id=1, source_target_pairs={{4,0},{6,2},{8,4},{10,6},{12,8},{14,10},{5,1},{7,3},{9,5},{11,7},{... | collective-permute-start | bytes 786440 | tf_op jit(solution)/shard_map/ppermute | solution.py:22
  39.4 5.9 %collective-permute-done.8.refs_2_.refs_3_ = bf16[256,512]{1,0:T(8,128)(2,1)S(1)} collective-permute-done((bf16[256,512]{1,0:T(8,128)(2,1)S(1)}, bf16[256,512]{1,0:T(8,128)(2,1)S(1)}, u32[]{:S(2)}, u32[]{:S(2)}) %collective-permute-start.8) | collective-permute-done | bytes 262176 | tf_op jit(solution)/shard_map/ppermute | solution.py:26
  45.3 0.1 shard_map.127
  45.4 1.6 %collective-permute-start.9 = (bf16[4,32,1024]{2,1,0:T(8,128)(2,1)S(1)}, bf16[4,32,1024]{2,1,0:T(8,128)(2,1)S(1)}, u32[]{:S(2)}, u32[]{:S(2)}) collective-permute-start(bf16[4,32,1024]{2,1,0:T(8,128)(2,1)S(1)} %get-tuple-element.31), channel_id=1, source_target_pairs={{0,2},{2,0},{4,6},{6,4},{8,10},{10,8},{12,14},{14,12},{1,3},{3,1},... | collective-permute-start | bytes 786440 | tf_op jit(solution)/shard_map/ppermute | solution.py:26
  47.0 2.2 %collective-permute-done.12.refs_2_.refs_1_.refs_0_.refs_6_ = bf16[256,512]{1,0:T(8,128)(2,1)S(1)} collective-permute-done((bf16[256,512]{1,0:T(8,128)(2,1)S(1)}, bf16[256,512]{1,0:T(8,128)(2,1)S(1)}, u32[]{:S(2)}, u32[]{:S(2)}) %collective-permute-start.12) | collective-permute-done | bytes 262176 | tf_op jit(solution)/shard_map/ppermute | solution.py:22
  49.2 1.3 %collective-permute-start.15 = (bf16[256,512]{1,0:T(8,128)(2,1)S(1)}, bf16[256,512]{1,0:T(8,128)(2,1)S(1)}, u32[]{:S(2)}, u32[]{:S(2)}) collective-permute-start(bf16[256,512]{1,0:T(8,128)(2,1)S(1)} %collective-permute-done.12.refs_2_.refs_1_.refs_0_.refs_6_), channel_id=1, source_target_pairs={{4,0},{6,2},{8,4},{10,6},{12,8},{14,10},{5,1},{7,3},{9,5},{11,7},{... | collective-permute-start | bytes 786440 | tf_op jit(solution)/shard_map/ppermute | solution.py:22
  50.5 0.6 collective-permute-start.13
  51.0 2.8 %collective-permute-done.9.refs_1_.refs_9_ = bf16[4,32,1024]{2,1,0:T(8,128)(2,1)S(1)} collective-permute-done((bf16[4,32,1024]{2,1,0:T(8,128)(2,1)S(1)}, bf16[4,32,1024]{2,1,0:T(8,128)(2,1)S(1)}, u32[]{:S(2)}, u32[]{:S(2)}) %collective-permute-start.9) | collective-permute-done | bytes 262176 | tf_op jit(solution)/shard_map/ppermute | solution.py:26
  53.8 0.1 shard_map.128
  53.9 2.7 %collective-permute-start.10 = (bf16[2,32,1024]{2,1,0:T(8,128)(2,1)S(1)}, bf16[2,32,1024]{2,1,0:T(8,128)(2,1)S(1)}, u32[]{:S(2)}, u32[]{:S(2)}) collective-permute-start(bf16[2,32,1024]{2,1,0:T(8,128)(2,1)S(1)} %get-tuple-element.33), channel_id=1, source_target_pairs={{0,4},{2,6},{4,0},{6,2},{8,12},{10,14},{12,8},{14,10},{1,5},{3,7},... | collective-permute-start | bytes 393224 | tf_op jit(solution)/shard_map/ppermute | solution.py:26
  56.6 0.8 %shard_map.131.refs_7_.refs_0_ = f32[256,512]{1,0:T(8,128)S(1)} custom-call(s32[1,4]{1,0:T(1,128)S(1)} %copy-done.8, bf16[256,512]{1,0:T(8,128)(2,1)S(1)} %bitcast.27, bf16[256,512]{1,0:T(8,128)(2,1)S(1)} %get-tuple-element.36.refs_2_.refs_1_.refs_5_, bf16[256,512]{1,0:T(8,128)(2,1)S(1)} %bitcast.13, ...), custom_call_target="tpu_custom_call" | custom-call | flops 2500000 | tf_op jit(solution)/shard_map/pallas_call | solution.py:293
  57.5 3.1 %collective-permute-start.17 = (bf16[256,512]{1,0:T(8,128)(2,1)S(1)}, bf16[256,512]{1,0:T(8,128)(2,1)S(1)}, u32[]{:S(2)}, u32[]{:S(2)}) collective-permute-start(bf16[256,512]{1,0:T(8,128)(2,1)S(1)} %shard_map.135), channel_id=1, source_target_pairs={{0,2},{2,0},{4,6},{6,4},{8,10},{10,8},{12,14},{14,12},{1,3},{3,1},... | collective-permute-start | bytes 786440 | tf_op jit(solution)/shard_map/ppermute | solution.py:26
  60.5 1.2 %shard_map.125.refs_8_ = bf16[256,1024]{1,0:T(8,128)(2,1)} custom-call(bf16[256,512]{1,0:T(8,128)(2,1)S(1)} %get-tuple-element.27.refs_0_, bf16[512,1024]{1,0:T(8,128)(2,1)S(1)} %copy-done.3), custom_call_target="tpu_custom_call" | custom-call | flops 1000000 | tf_op jit(solution)/shard_map/pallas_call | solution.py:293
  61.8 0.1 collective-permute-start.16
  62.0 0.9 %copy-done.6 = bf16[256,1024]{1,0:T(8,128)(2,1)S(1)} copy-done((bf16[256,1024]{1,0:T(8,128)(2,1)S(1)}, bf16[256,1024]{1,0:T(8,128)(2,1)}, u32[]{:S(2)}) %copy-start.6) | copy-done | bytes 524312
  62.8 0.2 shard_map.132
  63.0 1.9 %collective-permute-start.14 = (bf16[256,512]{1,0:T(8,128)(2,1)S(1)}, bf16[256,512]{1,0:T(8,128)(2,1)S(1)}, u32[]{:S(2)}, u32[]{:S(2)}) collective-permute-start(bf16[256,512]{1,0:T(8,128)(2,1)S(1)} %shard_map.132), channel_id=1, source_target_pairs={{0,4},{2,6},{4,8},{6,10},{8,12},{10,14},{1,5},{3,7},{5,9},{7,11},{... | collective-permute-start | bytes 786440 | tf_op jit(solution)/shard_map/ppermute | solution.py:22
  64.9 4.9 %collective-permute-start.11 = (bf16[1,32,1024]{2,1,0:T(8,128)(2,1)S(1)}, bf16[1,32,1024]{2,1,0:T(8,128)(2,1)S(1)}, u32[]{:S(2)}, u32[]{:S(2)}) collective-permute-start(bf16[1,32,1024]{2,1,0:T(8,128)(2,1)S(1)} %get-tuple-element.35), channel_id=1, source_target_pairs={{0,8},{2,10},{4,12},{6,14},{8,0},{10,2},{12,4},{14,6},{1,9},{3,11}... | collective-permute-start | bytes 196616 | tf_op jit(solution)/shard_map/ppermute | solution.py:26
  69.9 1.8 %shard_map.136 = (f32[256,512]{1,0:T(8,128)S(1)}, f32[256,512]{1,0:T(8,128)S(1)}) custom-call(s32[1,4]{1,0:T(1,128)S(1)} %copy-done.8, bf16[256,512]{1,0:T(8,128)(2,1)S(1)} %bitcast.14, bf16[256,512]{1,0:T(8,128)(2,1)S(1)} %bitcast.21, bf16[256,512]{1,0:T(8,128)(2,1)S(1)} %bitcast.28, bf16[256,512]{1,0:T(8,128)(2,1)S(1)} %collective-permute-done.4.refs_1_.refs_0_.refs_4_, ...), custom_call_target="tpu_custom_call" | custom-call | flops 1800000 | tf_op jit(solution)/shard_map/pallas_call | solution.py:293
  71.7 1.2 %shard_map.137 = (f32[256,512]{1,0:T(8,128)S(1)}, f32[256,512]{1,0:T(8,128)S(1)}) custom-call(s32[1,4]{1,0:T(1,128)S(1)} %copy-done.8, bf16[256,512]{1,0:T(8,128)(2,1)S(1)} %bitcast.15, bf16[256,512]{1,0:T(8,128)(2,1)S(1)} %bitcast.22, bf16[256,512]{1,0:T(8,128)(2,1)S(1)} %collective-permute-done.8.refs_2_.refs_3_, ...), custom_call_target="tpu_custom_call" | custom-call | flops 1800000 | tf_op jit(solution)/shard_map/pallas_call | solution.py:293
  73.0 1.0 %shard_map.138 = (bf16[256,512]{1,0:T(8,128)(2,1)}, bf16[256,512]{1,0:T(8,128)(2,1)}) custom-call(s32[1,4]{1,0:T(1,128)S(1)} %copy-done.8, bf16[256,512]{1,0:T(8,128)(2,1)S(1)} %bitcast.16, bf16[256,512]{1,0:T(8,128)(2,1)S(1)} %bitcast.23, bf16[256,512]{1,0:T(8,128)(2,1)S(1)} %collective-permute-done.13.refs_10_.refs_3_, ...), custom_call_target="tpu_custom_call" | custom-call | flops 900000 | tf_op jit(solution)/shard_map/pallas_call | solution.py:293
  73.9 0.7 shard_map.130
  74.6 0.7 shard_map.133
  (27 shorter events, 0.3 us)
Async XLA Ops:
  0.6 11.9 %collective-permute-start = (bf16[256,512]{1,0:T(8,128)(2,1)}, bf16[256,512]{1,0:T(8,128)(2,1)S(1)}, u32[]{:S(2)}, u32[]{:S(2)}) collective-permute-start(bf16[256,512]{1,0:T(8,128)(2,1)} %bitcast.10), channel_id=1, source_target_pairs={{0,4},{2,6},{4,8},{6,10},{8,12},{10,14},{1,5},{3,7},{5,9},{7,11},{... | collective-permute-start | bytes 786440 | tf_op jit(solution)/shard_map/ppermute | solution.py:22
  5.6 11.5 %collective-permute-start.2 = (bf16[256,512]{1,0:T(8,128)(2,1)}, bf16[256,512]{1,0:T(8,128)(2,1)S(1)}, u32[]{:S(2)}, u32[]{:S(2)}) collective-permute-start(bf16[256,512]{1,0:T(8,128)(2,1)} %bitcast.17), channel_id=1, source_target_pairs={{0,4},{2,6},{4,8},{6,10},{8,12},{10,14},{1,5},{3,7},{5,9},{7,11},{... | collective-permute-start | bytes 786440 | tf_op jit(solution)/shard_map/ppermute | solution.py:22
  9.1 9.6 %collective-permute-start.4 = (bf16[256,512]{1,0:T(8,128)(2,1)}, bf16[256,512]{1,0:T(8,128)(2,1)S(1)}, u32[]{:S(2)}, u32[]{:S(2)}) collective-permute-start(bf16[256,512]{1,0:T(8,128)(2,1)} %bitcast.24), channel_id=1, source_target_pairs={{4,0},{6,2},{8,4},{10,6},{12,8},{14,10},{5,1},{7,3},{9,5},{11,7},{... | collective-permute-start | bytes 786440 | tf_op jit(solution)/shard_map/ppermute | solution.py:22
  12.6 0.9 %copy-start = (bf16[1,256,512]{2,1,0:T(8,128)(2,1)S(1)}, bf16[1,256,512]{2,1,0:T(8,128)(2,1)}, u32[]{:S(2)}) copy-start(bf16[1,256,512]{2,1,0:T(8,128)(2,1)} %param.8) | copy-start | bytes 786436
  13.5 3.5 %copy-start.2 = (bf16[1,256,512]{2,1,0:T(8,128)(2,1)S(1)}, bf16[1,256,512]{2,1,0:T(8,128)(2,1)}, u32[]{:S(2)}) copy-start(bf16[1,256,512]{2,1,0:T(8,128)(2,1)} %param.9) | copy-start | bytes 786436
  13.6 12.1 %copy-start.8 = (s32[1,4]{1,0:T(1,128)S(1)}, s32[1,4]{1,0:T(1,128)}, u32[]{:S(2)}) copy-start(s32[1,4]{1,0:T(1,128)} %refs_0_.13) | copy-start | bytes 52
  13.6 7.7 %collective-permute-start.1 = (bf16[256,512]{1,0:T(8,128)(2,1)S(1)}, bf16[256,512]{1,0:T(8,128)(2,1)S(1)}, u32[]{:S(2)}, u32[]{:S(2)}) collective-permute-start(bf16[256,512]{1,0:T(8,128)(2,1)S(1)} %shard_map.118), channel_id=1, source_target_pairs={{0,2},{2,0},{4,6},{6,4},{8,10},{10,8},{12,14},{14,12},{1,3},{3,1},... | collective-permute-start | bytes 786440 | tf_op jit(solution)/shard_map/ppermute | solution.py:26
  17.1 13.2 %copy-start.4 = (bf16[1,256,512]{2,1,0:T(8,128)(2,1)S(1)}, bf16[1,256,512]{2,1,0:T(8,128)(2,1)}, u32[]{:S(2)}) copy-start(bf16[1,256,512]{2,1,0:T(8,128)(2,1)} %param.7) | copy-start | bytes 786436
  17.1 8.5 %collective-permute-start.3 = (bf16[256,512]{1,0:T(8,128)(2,1)S(1)}, bf16[256,512]{1,0:T(8,128)(2,1)S(1)}, u32[]{:S(2)}, u32[]{:S(2)}) collective-permute-start(bf16[256,512]{1,0:T(8,128)(2,1)S(1)} %shard_map.119), channel_id=1, source_target_pairs={{0,2},{2,0},{4,6},{6,4},{8,10},{10,8},{12,14},{14,12},{1,3},{3,1},... | collective-permute-start | bytes 786440 | tf_op jit(solution)/shard_map/ppermute | solution.py:26
  18.7 11.6 %collective-permute-start.5 = (bf16[256,512]{1,0:T(8,128)(2,1)S(1)}, bf16[256,512]{1,0:T(8,128)(2,1)S(1)}, u32[]{:S(2)}, u32[]{:S(2)}) collective-permute-start(bf16[256,512]{1,0:T(8,128)(2,1)S(1)} %collective-permute-done.4.refs_1_.refs_0_.refs_4_), channel_id=1, source_target_pairs={{4,0},{6,2},{8,4},{10,6},{12,8},{14,10},{5,1},{7,3},{9,5},{11,7},{... | collective-permute-start | bytes 786440 | tf_op jit(solution)/shard_map/ppermute | solution.py:22
  25.8 4.6 %copy-start.3 = (bf16[512,1024]{1,0:T(8,128)(2,1)S(1)}, bf16[512,1024]{1,0:T(8,128)(2,1)}, u32[]{:S(2)}) copy-start(bf16[512,1024]{1,0:T(8,128)(2,1)} %refs_1_.1) | copy-start | bytes 3145732
  25.8 9.0 %collective-permute-start.6 = (bf16[256,512]{1,0:T(8,128)(2,1)S(1)}, bf16[256,512]{1,0:T(8,128)(2,1)S(1)}, u32[]{:S(2)}, u32[]{:S(2)}) collective-permute-start(bf16[256,512]{1,0:T(8,128)(2,1)S(1)} %shard_map.120.refs_2_), channel_id=1, source_target_pairs={{0,4},{2,6},{4,8},{6,10},{8,12},{10,14},{1,5},{3,7},{5,9},{7,11},{... | collective-permute-start | bytes 786440 | tf_op jit(solution)/shard_map/ppermute | solution.py:22
  30.3 1.0 %copy-start.1 = (bf16[1,256,512]{2,1,0:T(8,128)(2,1)S(1)}, bf16[1,256,512]{2,1,0:T(8,128)(2,1)}, u32[]{:S(2)}) copy-start(bf16[1,256,512]{2,1,0:T(8,128)(2,1)} %param.8) | copy-start | bytes 786436
  30.3 1.1 %copy-start.5 = (bf16[1,256,1024]{2,1,0:T(8,128)(2,1)S(1)}, bf16[1,256,1024]{2,1,0:T(8,128)(2,1)}, u32[]{:S(2)}) copy-start(bf16[1,256,1024]{2,1,0:T(8,128)(2,1)} %param.12) | copy-start | bytes 1572868
  31.4 3.4 %copy-start.7 = (bf16[1,256,512]{2,1,0:T(8,128)(2,1)S(1)}, bf16[1,256,512]{2,1,0:T(8,128)(2,1)}, u32[]{:S(2)}) copy-start(bf16[1,256,512]{2,1,0:T(8,128)(2,1)} %param.10) | copy-start | bytes 786436
  36.5 8.8 %collective-permute-start.7 = (bf16[8,32,1024]{2,1,0:T(8,128)(2,1)S(1)}, bf16[8,32,1024]{2,1,0:T(8,128)(2,1)S(1)}, u32[]{:S(2)}, u32[]{:S(2)}) collective-permute-start(bf16[8,32,1024]{2,1,0:T(8,128)(2,1)S(1)} %get-tuple-element.29), channel_id=1, source_target_pairs={{0,1},{1,0},{2,3},{3,2},{4,5},{5,4},{6,7},{7,6},{8,9},{9,8},{10,11... | collective-permute-start | bytes 1572872 | tf_op jit(solution)/shard_map/ppermute | solution.py:26
  36.6 8.7 %collective-permute-start.8 = (bf16[256,512]{1,0:T(8,128)(2,1)S(1)}, bf16[256,512]{1,0:T(8,128)(2,1)S(1)}, u32[]{:S(2)}, u32[]{:S(2)}) collective-permute-start(bf16[256,512]{1,0:T(8,128)(2,1)S(1)} %shard_map.121.refs_10_), channel_id=1, source_target_pairs={{0,2},{2,0},{4,6},{6,4},{8,10},{10,8},{12,14},{14,12},{1,3},{3,1},... | collective-permute-start | bytes 786440 | tf_op jit(solution)/shard_map/ppermute | solution.py:26
  38.2 11.0 %collective-permute-start.12 = (bf16[256,512]{1,0:T(8,128)(2,1)S(1)}, bf16[256,512]{1,0:T(8,128)(2,1)S(1)}, u32[]{:S(2)}, u32[]{:S(2)}) collective-permute-start(bf16[256,512]{1,0:T(8,128)(2,1)S(1)} %get-tuple-element.36.refs_2_.refs_1_.refs_5_), channel_id=1, source_target_pairs={{4,0},{6,2},{8,4},{10,6},{12,8},{14,10},{5,1},{7,3},{9,5},{11,7},{... | collective-permute-start | bytes 786440 | tf_op jit(solution)/shard_map/ppermute | solution.py:22
  45.4 8.4 %collective-permute-start.9 = (bf16[4,32,1024]{2,1,0:T(8,128)(2,1)S(1)}, bf16[4,32,1024]{2,1,0:T(8,128)(2,1)S(1)}, u32[]{:S(2)}, u32[]{:S(2)}) collective-permute-start(bf16[4,32,1024]{2,1,0:T(8,128)(2,1)S(1)} %get-tuple-element.31), channel_id=1, source_target_pairs={{0,2},{2,0},{4,6},{6,4},{8,10},{10,8},{12,14},{14,12},{1,3},{3,1},... | collective-permute-start | bytes 786440 | tf_op jit(solution)/shard_map/ppermute | solution.py:26
  49.2 12.6 %collective-permute-start.15 = (bf16[256,512]{1,0:T(8,128)(2,1)S(1)}, bf16[256,512]{1,0:T(8,128)(2,1)S(1)}, u32[]{:S(2)}, u32[]{:S(2)}) collective-permute-start(bf16[256,512]{1,0:T(8,128)(2,1)S(1)} %collective-permute-done.12.refs_2_.refs_1_.refs_0_.refs_6_), channel_id=1, source_target_pairs={{4,0},{6,2},{8,4},{10,6},{12,8},{14,10},{5,1},{7,3},{9,5},{11,7},{... | collective-permute-start | bytes 786440 | tf_op jit(solution)/shard_map/ppermute | solution.py:22
  50.5 11.5 %collective-permute-start.13 = (bf16[256,512]{1,0:T(8,128)(2,1)S(1)}, bf16[256,512]{1,0:T(8,128)(2,1)S(1)}, u32[]{:S(2)}, u32[]{:S(2)}) collective-permute-start(bf16[256,512]{1,0:T(8,128)(2,1)S(1)} %shard_map.122.refs_11_), channel_id=1, source_target_pairs={{0,2},{2,0},{4,6},{6,4},{8,10},{10,8},{12,14},{14,12},{1,3},{3,1},... | collective-permute-start | bytes 786440 | tf_op jit(solution)/shard_map/ppermute | solution.py:26
  53.9 8.0 %collective-permute-start.10 = (bf16[2,32,1024]{2,1,0:T(8,128)(2,1)S(1)}, bf16[2,32,1024]{2,1,0:T(8,128)(2,1)S(1)}, u32[]{:S(2)}, u32[]{:S(2)}) collective-permute-start(bf16[2,32,1024]{2,1,0:T(8,128)(2,1)S(1)} %get-tuple-element.33), channel_id=1, source_target_pairs={{0,4},{2,6},{4,0},{6,2},{8,12},{10,14},{12,8},{14,10},{1,5},{3,7},... | collective-permute-start | bytes 393224 | tf_op jit(solution)/shard_map/ppermute | solution.py:26
  57.5 14.2 %collective-permute-start.17 = (bf16[256,512]{1,0:T(8,128)(2,1)S(1)}, bf16[256,512]{1,0:T(8,128)(2,1)S(1)}, u32[]{:S(2)}, u32[]{:S(2)}) collective-permute-start(bf16[256,512]{1,0:T(8,128)(2,1)S(1)} %shard_map.135), channel_id=1, source_target_pairs={{0,2},{2,0},{4,6},{6,4},{8,10},{10,8},{12,14},{14,12},{1,3},{3,1},... | collective-permute-start | bytes 786440 | tf_op jit(solution)/shard_map/ppermute | solution.py:26
  61.8 1.0 %copy-start.6 = (bf16[256,1024]{1,0:T(8,128)(2,1)S(1)}, bf16[256,1024]{1,0:T(8,128)(2,1)}, u32[]{:S(2)}) copy-start(bf16[256,1024]{1,0:T(8,128)(2,1)} %shard_map.125.refs_8_) | copy-start | bytes 1572868
  61.8 11.1 %collective-permute-start.16 = (bf16[256,512]{1,0:T(8,128)(2,1)S(1)}, bf16[256,512]{1,0:T(8,128)(2,1)S(1)}, u32[]{:S(2)}, u32[]{:S(2)}) collective-permute-start(bf16[256,512]{1,0:T(8,128)(2,1)S(1)} %shard_map.134), channel_id=1, source_target_pairs={{0,2},{2,0},{4,6},{6,4},{8,10},{10,8},{12,14},{14,12},{1,3},{3,1},... | collective-permute-start | bytes 786440 | tf_op jit(solution)/shard_map/ppermute | solution.py:26
  63.0 11.6 %collective-permute-start.14 = (bf16[256,512]{1,0:T(8,128)(2,1)S(1)}, bf16[256,512]{1,0:T(8,128)(2,1)S(1)}, u32[]{:S(2)}, u32[]{:S(2)}) collective-permute-start(bf16[256,512]{1,0:T(8,128)(2,1)S(1)} %shard_map.132), channel_id=1, source_target_pairs={{0,4},{2,6},{4,8},{6,10},{8,12},{10,14},{1,5},{3,7},{5,9},{7,11},{... | collective-permute-start | bytes 786440 | tf_op jit(solution)/shard_map/ppermute | solution.py:22
  64.9 9.0 %collective-permute-start.11 = (bf16[1,32,1024]{2,1,0:T(8,128)(2,1)S(1)}, bf16[1,32,1024]{2,1,0:T(8,128)(2,1)S(1)}, u32[]{:S(2)}, u32[]{:S(2)}) collective-permute-start(bf16[1,32,1024]{2,1,0:T(8,128)(2,1)S(1)} %get-tuple-element.35), channel_id=1, source_target_pairs={{0,8},{2,10},{4,12},{6,14},{8,0},{10,2},{12,4},{14,6},{1,9},{3,11}... | collective-permute-start | bytes 196616 | tf_op jit(solution)/shard_map/ppermute | solution.py:26

commit v3 on v2

--- a/solution.py
+++ b/solution.py
@@ -14,6 +14,20 @@
 BF16 = jnp.bfloat16
 F32 = jnp.float32
 VMEM = pl.BlockSpec(memory_space=pltpu.VMEM)
+HINT = {
+    "pick": 0.001,
+    "attend": 0.001,
+    "far_mix": 0.001,
+    "near_mix": 0.001,
+    "norm": 0.001,
+    "near_query": 0.001,
+    "weight": 0.001,
+    "out": 0.001,
+    "part": 0.001,
+    "sum": 0.001,
+    "far_query": 0.001,
+    "keys": (0.001, 0.001, 4.0, 0.001),
+}
 ANY = pl.BlockSpec(memory_space=pl.ANY)
 
 
@@ -93,16 +107,14 @@
         finish(now, ready)
 
 
-def mix_kernel(ahead, distances, project, *refs):
+def mix_kernel(distances, *refs):
     count = len(distances)
     lengths_ref, q_ref = refs[:2]
     k_refs, v_refs = refs[2 : 2 + count], refs[2 + count : 2 + 2 * count]
-    mixed_ref, total_ref = refs[-2:]
-    if project:
-        out_grad_ref, weight_ref, grad_gated_ref, total_ref = refs[2 + 2 * count :]
-        grad_gated_ref[...] = dot(out_grad_ref[...], weight_ref[...], 1, 1)
+    out_grad_ref, weight_ref, grad_gated_ref, total_ref = refs[2 + 2 * count :]
+    grad_gated_ref[...] = dot(out_grad_ref[...], weight_ref[...], 1, 1)
     tok, width = q_ref.shape
-    place = (lax.axis_index("ctx") + ahead) * tok
+    place = lax.axis_index("ctx") * tok
     ends = ends_of(lengths_ref)
 
     def pair(k_ref, v_ref, mask, dead, alive):
@@ -118,19 +130,59 @@
 
         staggered(width, lambda cols: half_scores(q_ref[:, cols], k_ref[:, cols]), finish)
 
-    if distances[0] > 0:
-        total_ref[...] = jnp.zeros_like(total_ref)
     for n, distance in enumerate(distances):
         if distance == 0:
             pair(k_refs[n], v_refs[n], own_mask(ends, place, tok, False), None, None)
         else:
             dead, alive = crossing(ends, place, distance, tok)
             pl.when(dead < tok)(functools.partial(pair, k_refs[n], v_refs[n], None, dead, alive))
-    if not project:
-        mixed_ref[...] = total_ref[...].astype(BF16)
-
-
-def norm_kernel(near_ref, far_ref, grad_gated_ref, gates_ref, gated_ref, grad_gates_ref, grad_mixed_ref):
+
+
+def attend_kernel(ahead, distances, *refs):
+    lengths_ref, q_ref = refs[:2]
+    attend_ref = refs[-1]
+    tok, width = q_ref.shape
+    heads = width // HEAD
+    place = (lax.axis_index("ctx") + ahead) * tok
+    ends = ends_of(lengths_ref)
+    for n, distance in enumerate(distances):
+        dead, alive = crossing(ends, place, distance, tok)
+
+        @pl.when(dead < tok)
+        def _(n=n, dead=dead, alive=alive):
+            number = row_numbers(tok)
+
+            def begin(cols):
+                q = jnp.where(number < alive, q_ref[:, cols], 0.0).astype(BF16)
+                return half_scores(q, jnp.where(number >= dead, refs[2 + n][:, cols], 0.0).astype(BF16))
+
+            def finish(cols, half):
+                attend_ref[n * heads + cols.start // HEAD] = silu(half).astype(BF16)
+
+            staggered(width, begin, finish)
+
+
+def far_kernel(ahead, distances, *refs):
+    lengths_ref, attend_ref = refs[:2]
+    mixed_ref, total_ref = refs[-2:]
+    tok, width = mixed_ref.shape
+    heads = width // HEAD
+    place = (lax.axis_index("ctx") + ahead) * tok
+    ends = ends_of(lengths_ref)
+    total_ref[...] = jnp.zeros_like(total_ref)
+    for n, distance in enumerate(distances):
+        dead, _ = crossing(ends, place, distance, tok)
+
+        @pl.when(dead < tok)
+        def _(n=n):
+            for head in range(heads):
+                cols = slice(head * HEAD, (head + 1) * HEAD)
+                total_ref[:, cols] += dot(attend_ref[n * heads + head], refs[2 + n][:, cols], 1, 0)
+
+    mixed_ref[...] = total_ref[...].astype(BF16)
+
+
+def norm_kernel(near_ref, far_ref, grad_gated_ref, gates_ref, gated_ref, normed_ref, grad_mixed_ref):
     mixed = near_ref[...] + far_ref[...].astype(F32)
     gates = gates_ref[...].astype(F32)
     grad_gated = grad_gated_ref[...]
@@ -138,7 +190,7 @@
     inverse = lax.rsqrt(jnp.mean(centered * centered, axis=1, keepdims=True) + EPS)
     normed = centered * inverse
     gated_ref[...] = (normed * gates).astype(BF16)
-    grad_gates_ref[...] = (grad_gated * normed).astype(BF16)
+    normed_ref[...] = normed
     grad_normed = grad_gated * gates
     grad_mixed_ref[...] = (
         (
@@ -192,7 +244,11 @@
     count = len(distances)
     lengths_ref, k_ref, v_ref = refs[:3]
     q_refs, grad_refs = refs[3 : 3 + count], refs[3 + count : 3 + 2 * count]
-    key_out, value_out, key_total, value_total = refs[-4:] if last else refs[-2:] * 2
+    if last:
+        near_ref, far_ref, key_out, value_out, query_out, key_total, value_total = refs[-7:]
+        query_out[...] = (near_ref[...] + far_ref[...].astype(F32)).astype(BF16)
+    else:
+        key_total, value_total = refs[-2:]
     tok, width = k_ref.shape
     place = lax.axis_index("ctx") * tok
     ends = ends_of(lengths_ref)
@@ -239,7 +295,8 @@
         give_ref[part] = total(2 * part + 1 - bit).astype(BF16)
 
 
-def out_kernel(gated_ref, weight_ref, out_ref):
+def out_kernel(gated_ref, weight_ref, grad_gated_ref, normed_ref, out_ref, grad_gates_ref):
+    grad_gates_ref[...] = (grad_gated_ref[...] * normed_ref[...]).astype(BF16)
     out_ref[...] = dot(gated_ref[...], weight_ref[...], 1, 0).astype(BF16)
 
 
@@ -263,12 +320,21 @@
     )
 
 
-def last_part_kernel(factor, kept_ref, came_ref, out_ref):
-    out_ref[...] = (kept_ref[0] + came_ref[0].astype(F32)) * factor
-
-
-def add_kernel(a_ref, b_ref, out_ref):
-    out_ref[...] = (a_ref[...] + b_ref[...].astype(F32)).astype(out_ref.dtype)
+def spread_kernel(step, kept_ref, came_ref, keep_ref, *give_refs):
+    own = lax.axis_index("ctx") // step
+    keep_ref[0] = kept_ref[own] + came_ref[own].astype(F32)
+    for n, give_ref in enumerate(give_refs):
+        chunk = own ^ (n + 1)
+        give_ref[0] = (kept_ref[chunk] + came_ref[chunk].astype(F32)).astype(BF16)
+
+
+def sum_kernel(factor, kept_ref, *refs):
+    rows = kept_ref[0]
+    for came_ref in refs[:-2]:
+        rows = rows + came_ref[0].astype(F32)
+    out_ref, mark_ref = refs[-2:]
+    out_ref[...] = rows * factor
+    mark_ref[...] = jnp.zeros_like(mark_ref)
 
 
 def pick_kernel(even_ref, odd_ref, out_ref):
@@ -283,11 +349,28 @@
         out_ref[...] = odd_ref[...]
 
 
+def pick_far_kernel(odd_ref, even_ref, out_ref, sem):
+    even = lax.axis_index("ctx") % 2 == 0
+
+    @pl.when(even)
+    def _():
+        copy = pltpu.make_async_copy(even_ref, out_ref, sem)
+        copy.start()
+        copy.wait()
+
+    @pl.when(jnp.logical_not(even))
+    def _():
+        out_ref[...] = odd_ref[...]
+
+
 def call(kernel, outs, args, micros, scratch=(), after=()):
     held = len(args)
 
     def body(*refs):
         kernel(*refs[:held], *refs[held + len(after) :])
+
+    if kernel is pick_far_kernel:
+        body = kernel
 
     shapes = [jax.ShapeDtypeStruct(shape, dtype) for shape, dtype in outs]
     return pl.pallas_call(
@@ -296,36 +379,34 @@
         in_specs=[VMEM] * len(args) + [ANY] * len(after),
         out_specs=[VMEM] * len(shapes),
         scratch_shapes=list(scratch),
-        cost_estimate=pl.CostEstimate(flops=int(micros * 1.0e6), bytes_accessed=0, transcendentals=0),
+        cost_estimate=pl.CostEstimate(flops=int(micros * 1.1535e9), bytes_accessed=0, transcendentals=0),
         compiler_params=pltpu.CompilerParams(vmem_limit_bytes=48 * 1024 * 1024),
     )(*args, *after)
 
 
 def picked(even_sends, odd_sends, after=()):
-    (sent,) = call(
-        pick_kernel, [(even_sends.shape, even_sends.dtype)], [even_sends, odd_sends], 0.2, (), after
-    )
+    shape = (even_sends.shape, even_sends.dtype)
+    (sent,) = call(pick_kernel, [shape], [even_sends, odd_sends], HINT["pick"], (), after)
     return sent
 
 
-def exchanged(even_sends, odd_sends):
-    return swapped(picked(even_sends, odd_sends), "ctx", 1)
+def picked_far(even_sends, odd_sends):
+    shape = (even_sends.shape, even_sends.dtype)
+    sem = [pltpu.SemaphoreType.DMA]
+    (sent,) = call(pick_far_kernel, [shape], [odd_sends], HINT["pick"], sem, [even_sends])
+    return sent
+
+
+def exchanged(even_sends, odd_sends, after=()):
+    return swapped(picked(even_sends, odd_sends, after), "ctx", 1)
 
 
 def earlier_blocks(block, most):
     blocks = {0: block}
     for distance in range(2, most + 1, 2):
         blocks[distance] = shifted(blocks[distance - 2], 2)
-        blocks[distance - 1] = exchanged(blocks[distance - 2], blocks[distance])
-    return blocks
-
-
-def later_blocks(block, most):
-    blocks = {0: block}
-    for distance in range(2, most + 1, 2):
-        blocks[distance] = shifted(blocks[distance - 2], -2)
-    for distance in range(1, most, 2):
-        blocks[distance] = exchanged(blocks[distance + 1], blocks[distance - 1])
+        sent = picked_far(blocks[distance - 2], blocks[distance])
+        blocks[distance - 1] = swapped(sent, "ctx", 1)
     return blocks
 
 
@@ -349,97 +430,122 @@
     far = [mid + d for d in back]
     back_keys = [key_at[d] for d in back] + [value_at[d] for d in back]
     near_keys = [key_at[d] for d in near] + [value_at[d] for d in near]
+    (far_attend,) = call(
+        functools.partial(attend_kernel, mid, far),
+        [((len(far) * width // HEAD, tok, tok), BF16)],
+        [lengths, query_at[mid], *[key_at[d] for d in back]],
+        HINT["attend"],
+    )
     (far_term,) = call(
-        functools.partial(mix_kernel, mid, far, False),
+        functools.partial(far_kernel, mid, far),
         one,
-        [lengths, query_at[mid], *back_keys],
-        1.0,
+        [lengths, far_attend, *[value_at[d] for d in back]],
+        HINT["far_mix"],
         [total],
     )
     far_mixed = shifted(far_term, mid)
-    sent = {d: picked(query_at[d + 1], query_at[d - 1], [far_term]) for d in range(1, reach, 2)}
-    for distance, block in sent.items():
-        query_at[distance] = swapped(block, "ctx", 1)
+    for distance in range(1, reach, 2):
+        query_at[distance] = exchanged(query_at[distance + 1], query_at[distance - 1], [far_term])
     grad_gated, near_mixed = call(
-        functools.partial(mix_kernel, 0, near, True),
+        functools.partial(mix_kernel, near),
         wide * 2,
         [lengths, q, *near_keys, out_grad, out_weight],
-        2.0,
+        HINT["near_mix"],
         (),
-        list(sent.values()),
-    )
-    gated, grad_gates, grad_mixed = call(
+        [query_at[reach]],
+    )
+    gated, normed, grad_mixed = call(
         norm_kernel,
-        one * 3,
+        [*one, *wide, *one],
         [near_mixed, far_mixed, grad_gated, gate_rows],
-        1.0,
-    )
-    grad_at = later_blocks(grad_mixed, reach)
+        HINT["norm"],
+    )
     chunk = (width // (count * cores), model)
     keep, give = call(
         weight_kernel,
         [((count, *chunk), F32), ((count, *chunk), BF16)],
         [gated, out_grad],
-        1.5,
+        HINT["weight"],
         [pltpu.VMEM((width, model), F32)],
-    )
-    (output,) = call(out_kernel, [((tok, model), BF16)], [gated, out_weight], 1.0)
+        [query_at[1]],
+    )
     came = swapped(give, "dp", 1)
-    arrived = [came]
-    step = 1
-    while step < count:
-        parts = (count // (2 * step), *chunk)
+    step, parts = 1, count
+    while parts > 4:
+        parts //= 2
         keep, give = call(
             functools.partial(part_kernel, step),
-            [(parts, F32), (parts, BF16)],
+            [((parts, *chunk), F32), ((parts, *chunk), BF16)],
             [keep, came],
-            0.8,
-            (),
-            [query_at[1]] if step == 1 else (),
+            HINT["part"],
         )
         came = swapped(give, "ctx", step)
-        arrived.append(came)
         step *= 2
-    (grad_weight,) = call(
-        functools.partial(last_part_kernel, 1.0 / math.sqrt(cores * count * tok)),
-        [(chunk, F32)],
-        [keep, came],
-        0.5,
-    )
     (near_query,) = call(
         functools.partial(query_grad_kernel, 0, near),
         wide,
         [lengths, q, grad_mixed, *near_keys],
-        2.5,
+        HINT["near_query"],
         [total],
-    )
+        [keep],
+    )
+    output, grad_gates = call(
+        out_kernel,
+        [((tok, model), BF16), *one],
+        [gated, out_weight, grad_gated, normed],
+        HINT["out"],
+        (),
+        [keep],
+    )
+    grad_at = {0: grad_mixed, 2: shifted(grad_mixed, -2)}
+    grad_at[2], *_ = lax.optimization_barrier([grad_at[2], near_query, output])
+    for distance in range(4, reach + 1, 2):
+        grad_at[distance] = shifted(grad_at[distance - 2], -2)
     (far_query_term,) = call(
         functools.partial(query_grad_kernel, mid, far),
         one,
         [lengths, query_at[mid], grad_at[mid], *back_keys],
-        1.5,
+        HINT["far_query"],
         [total],
-        [near_query, output, keep, *[query_at[d] for d in far]],
     )
     far_query = shifted(far_query_term, mid)
-    grads = ()
-    groups = [
-        [d for d in near if d % 2 == 0],
-        [d for d in near if d % 2 == 1] + [d for d in far if d % 2 == 0],
-        [d for d in far if d % 2 == 1],
-    ]
-    for n, group in enumerate(groups):
-        last = n == len(groups) - 1
-        grads = call(
+    sent = {1: picked(grad_at[2], grad_mixed, [far_query_term])}
+    groups = [[d for d in part if d % 2 == odd] for part in (near, far) for odd in (0, 1)]
+
+    def key_terms(n, carried, after=()):
+        group, last = groups[n], n == len(groups) - 1
+        return call(
             functools.partial(key_grad_kernel, group, last),
-            (one if last else wide) * 2,
-            [lengths, k, v, *[query_at[d] for d in group], *[grad_at[d] for d in group], *grads],
-            len(group) * 0.9,
+            one * 3 if last else wide * 2,
+            [lengths, k, v, *[query_at[d] for d in group], *[grad_at[d] for d in group], *carried],
+            HINT["keys"][n],
             [total] * 2 if last else (),
-            arrived[1:2] if n == 1 else (),
+            after,
         )
-    key_grad, value_grad = grads
-    (query_grad,) = call(add_kernel, one, [near_query, far_query], 0.3)
+
+    for distance in range(3, reach, 2):
+        sent[distance] = picked(grad_at[distance + 1], grad_at[distance - 1])
+    for distance, block in sent.items():
+        grad_at[distance] = swapped(block, "ctx", 1)
+    grads = key_terms(0, [], [query_at[reach - 1]])
+    grads = key_terms(1, grads, [far_query])
+    keep, *gives = call(
+        functools.partial(spread_kernel, step),
+        [((1, *chunk), F32)] + [((1, *chunk), BF16)] * (parts - 1),
+        [keep, came],
+        HINT["part"],
+        (),
+        [sent[1]],
+    )
+    shares = [swapped(give, "ctx", (n + 1) * step) for n, give in enumerate(gives)]
+    grad_weight, summed = call(
+        functools.partial(sum_kernel, 1.0 / math.sqrt(cores * count * tok)),
+        [(chunk, F32), ((8, HEAD), F32)],
+        [keep, *shares],
+        HINT["sum"],
+    )
+    grads = key_terms(2, grads, [summed])
+    key_grad, value_grad, query_grad = key_terms(3, [*grads, near_query, far_query])
     return (
         output[None],
         grad_weight,

time: 75.8 us -> 72.4 us (0.955)
  waiting for transfers between devices: 23.1 us -> 19.9 us
  local copies, waits for them, and re-layouts: 2.88 us -> 0.99 us
  Pallas kernels: 10.7 us -> 11.8 us
    ppermute x10 -> x11, waiting for transfers between devices: 14.3 us -> 9 us  [swapped(): lax.ppermute(block, axis, [(i, i ^ step) for i in range(lax.axis_size(axi...]
    ppermute x8, starting transfers between devices: 19.9 us -> 22.5 us  [shifted(): lax.ppermute(block, 'ctx', [(i, i + distance) for i in devices if i + dis...]
    ppermute x10 -> x11, starting transfers between devices: 17.7 us -> 15.2 us  [swapped(): lax.ppermute(block, axis, [(i, i ^ step) for i in range(lax.axis_size(axi...]
    ppermute x8, waiting for transfers between devices: 8.78 us -> 10.9 us  [shifted(): lax.ppermute(block, 'ctx', [(i, i + distance) for i in devices if i + dis...]
    unnamed x18 -> x16, local copies, waits for them, and re-layouts: 2.88 us -> 0.99 us
    pallas_call x21, Pallas kernels: 10.7 us -> 11.8 us  [call(): pl.pallas_call(body, out_shape=shapes, in_specs=[VMEM] * len(args) + [ANY...]
  transfers between devices with their start and end apart: 18 -> 19, of which waited for: 8 -> 8; matrix products, arithmetic and copies ran while one was open for 0% -> 0% of each run, Pallas kernels for 11% -> 13%
where the time goes in v3:
time: 72.4 us; the launch traced here: 71.2 us
  starting transfers between devices  37.7 us (52%)
  waiting for transfers between devices  19.9 us (27%)
  Pallas kernels  11.8 us (16%)
  local copies, waits for them, and re-layouts  0.99 us (1%)
  between operations  0.95 us (1%)
    ppermute x8, starting transfers between devices, shifted(): lax.ppermute(block, 'ctx', [(i, i + distance) for i in devices if i + dis...  22.5 us
    ppermute x11, starting transfers between devices, swapped(): lax.ppermute(block, axis, [(i, i ^ step) for i in range(lax.axis_size(axi...  15.2 us
    pallas_call x21, Pallas kernels, call(): pl.pallas_call(body, out_shape=shapes, in_specs=[VMEM] * len(args) + [ANY...  11.8 us
    ppermute x8, waiting for transfers between devices, shifted(): lax.ppermute(block, 'ctx', [(i, i + distance) for i in devices if i + dis...  10.9 us
    ppermute x11, waiting for transfers between devices, swapped(): lax.ppermute(block, axis, [(i, i ^ step) for i in range(lax.axis_size(axi...  9 us
  transfers between devices with their start and end apart: 19, of which 8 were waited for; matrix products, arithmetic and copies ran while one was open for 0% of the time, Pallas kernels for 13%

profile of v3, /device:TPU:0, one launch (start us, length us, event | category | flops | bytes accessed | tf_op | source)
XLA Modules:
  0.0 71.2 jit_solution(3746238977176689089)
XLA Ops:
  0.6 4.9 %collective-permute-start = (bf16[256,512]{1,0:T(8,128)(2,1)}, bf16[256,512]{1,0:T(8,128)(2,1)S(1)}, u32[]{:S(2)}, u32[]{:S(2)}) collective-permute-start(bf16[256,512]{1,0:T(8,128)(2,1)} %bitcast.10), channel_id=1, source_target_pairs={{0,4},{2,6},{4,8},{6,10},{8,12},{10,14},{1,5},{3,7},{5,9},{7,11},{... | collective-permute-start | bytes 786440 | tf_op jit(solution)/shard_map/ppermute | solution.py:36
  5.6 3.5 %collective-permute-start.2 = (bf16[256,512]{1,0:T(8,128)(2,1)}, bf16[256,512]{1,0:T(8,128)(2,1)S(1)}, u32[]{:S(2)}, u32[]{:S(2)}) collective-permute-start(bf16[256,512]{1,0:T(8,128)(2,1)} %bitcast.18), channel_id=1, source_target_pairs={{0,4},{2,6},{4,8},{6,10},{8,12},{10,14},{1,5},{3,7},{5,9},{7,11},{... | collective-permute-start | bytes 786440 | tf_op jit(solution)/shard_map/ppermute | solution.py:36
  9.1 1.3 %collective-permute-start.4 = (bf16[256,512]{1,0:T(8,128)(2,1)}, bf16[256,512]{1,0:T(8,128)(2,1)S(1)}, u32[]{:S(2)}, u32[]{:S(2)}) collective-permute-start(bf16[256,512]{1,0:T(8,128)(2,1)} %bitcast.26), channel_id=1, source_target_pairs={{4,0},{6,2},{8,4},{10,6},{12,8},{14,10},{5,1},{7,3},{9,5},{11,7},{... | collective-permute-start | bytes 786440 | tf_op jit(solution)/shard_map/ppermute | solution.py:36
  10.4 2.2 %collective-permute-done.odd_ref.refs_4_.refs_3_.refs_5_ = bf16[256,512]{1,0:T(8,128)(2,1)S(1)} collective-permute-done((bf16[256,512]{1,0:T(8,128)(2,1)}, bf16[256,512]{1,0:T(8,128)(2,1)S(1)}, u32[]{:S(2)}, u32[]{:S(2)}) %collective-permute-start) | collective-permute-done | bytes 262176 | tf_op jit(solution)/shard_map/ppermute | solution.py:36
  12.6 0.9 %copy-done = bf16[1,256,512]{2,1,0:T(8,128)(2,1)S(1)} copy-done((bf16[1,256,512]{2,1,0:T(8,128)(2,1)S(1)}, bf16[1,256,512]{2,1,0:T(8,128)(2,1)}, u32[]{:S(2)}) %copy-start) | copy-done | bytes 262168
  13.6 0.0 copy-start.7
  13.6 1.6 %collective-permute-start.1 = (bf16[256,512]{1,0:T(8,128)(2,1)S(1)}, bf16[256,512]{1,0:T(8,128)(2,1)S(1)}, u32[]{:S(2)}, u32[]{:S(2)}) collective-permute-start(bf16[256,512]{1,0:T(8,128)(2,1)S(1)} %shard_map.118), channel_id=1, source_target_pairs={{0,2},{2,0},{4,6},{6,4},{8,10},{10,8},{12,14},{14,12},{1,3},{3,1},... | collective-permute-start | bytes 786440 | tf_op jit(solution)/shard_map/ppermute | solution.py:40
  15.2 1.9 %collective-permute-done.2.odd_ref.refs_7_.refs_3_.refs_8_.refs_6_ = bf16[256,512]{1,0:T(8,128)(2,1)S(1)} collective-permute-done((bf16[256,512]{1,0:T(8,128)(2,1)}, bf16[256,512]{1,0:T(8,128)(2,1)S(1)}, u32[]{:S(2)}, u32[]{:S(2)}) %collective-permute-start.2) | collective-permute-done | bytes 262176 | tf_op jit(solution)/shard_map/ppermute | solution.py:36
  17.1 1.6 %collective-permute-start.3 = (bf16[256,512]{1,0:T(8,128)(2,1)S(1)}, bf16[256,512]{1,0:T(8,128)(2,1)S(1)}, u32[]{:S(2)}, u32[]{:S(2)}) collective-permute-start(bf16[256,512]{1,0:T(8,128)(2,1)S(1)} %shard_map.119), channel_id=1, source_target_pairs={{0,2},{2,0},{4,6},{6,4},{8,10},{10,8},{12,14},{14,12},{1,3},{3,1},... | collective-permute-start | bytes 786440 | tf_op jit(solution)/shard_map/ppermute | solution.py:40
  18.7 1.3 %collective-permute-start.5 = (bf16[256,512]{1,0:T(8,128)(2,1)S(1)}, bf16[256,512]{1,0:T(8,128)(2,1)S(1)}, u32[]{:S(2)}, u32[]{:S(2)}) collective-permute-start(bf16[256,512]{1,0:T(8,128)(2,1)S(1)} %collective-permute-done.4.refs_1_.refs_0_.refs_4_), channel_id=1, source_target_pairs={{4,0},{6,2},{8,4},{10,6},{12,8},{14,10},{5,1},{7,3},{9,5},{11,7},{... | collective-permute-start | bytes 786440 | tf_op jit(solution)/shard_map/ppermute | solution.py:36
  20.0 1.3 %collective-permute-done.1.refs_3_.refs_2_.refs_4_ = bf16[256,512]{1,0:T(8,128)(2,1)S(1)} collective-permute-done((bf16[256,512]{1,0:T(8,128)(2,1)S(1)}, bf16[256,512]{1,0:T(8,128)(2,1)S(1)}, u32[]{:S(2)}, u32[]{:S(2)}) %collective-permute-start.1) | collective-permute-done | bytes 262176 | tf_op jit(solution)/shard_map/ppermute | solution.py:40
  21.3 0.1 shard_map.121.refs_1_
  21.4 0.0 copy-start.4
  21.4 0.0 copy-start.3
  21.4 4.2 %collective-permute-done.3.refs_6_.refs_2_.refs_7_.refs_5_ = bf16[256,512]{1,0:T(8,128)(2,1)S(1)} collective-permute-done((bf16[256,512]{1,0:T(8,128)(2,1)S(1)}, bf16[256,512]{1,0:T(8,128)(2,1)S(1)}, u32[]{:S(2)}, u32[]{:S(2)}) %collective-permute-start.3) | collective-permute-done | bytes 262176 | tf_op jit(solution)/shard_map/ppermute | solution.py:40
  25.6 0.1 shard_map.122.refs_2_
  25.8 0.0 copy-start.1
  25.8 5.0 %collective-permute-start.6 = (bf16[256,512]{1,0:T(8,128)(2,1)S(1)}, bf16[256,512]{1,0:T(8,128)(2,1)S(1)}, u32[]{:S(2)}, u32[]{:S(2)}) collective-permute-start(bf16[256,512]{1,0:T(8,128)(2,1)S(1)} %shard_map.122.refs_2_), channel_id=1, source_target_pairs={{0,4},{2,6},{4,8},{6,10},{8,12},{10,14},{1,5},{3,7},{5,9},{7,11},{... | collective-permute-start | bytes 786440 | tf_op jit(solution)/shard_map/ppermute | solution.py:36
  30.9 1.0 %collective-permute-start.7 = (bf16[256,512]{1,0:T(8,128)(2,1)S(1)}, bf16[256,512]{1,0:T(8,128)(2,1)S(1)}, u32[]{:S(2)}, u32[]{:S(2)}) collective-permute-start(bf16[256,512]{1,0:T(8,128)(2,1)S(1)} %shard_map.124), channel_id=1, source_target_pairs={{0,2},{2,0},{4,6},{6,4},{8,10},{10,8},{12,14},{14,12},{1,3},{3,1},... | collective-permute-start | bytes 786440 | tf_op jit(solution)/shard_map/ppermute | solution.py:40
  31.9 0.0 copy-start.6
  31.9 0.9 %shard_map.120 = (f32[256,512]{1,0:T(8,128)S(1)}, f32[256,512]{1,0:T(8,128)S(1)}) custom-call(s32[1,4]{1,0:T(1,128)S(1)} %copy-done.7, bf16[256,512]{1,0:T(8,128)(2,1)S(1)} %bitcast.28, bf16[256,512]{1,0:T(8,128)(2,1)S(1)} %bitcast.12, bf16[256,512]{1,0:T(8,128)(2,1)S(1)} %collective-permute-done.1.refs_3_.refs_2_.refs_4_, ...), custom_call_target="tpu_custom_call" | custom-call | flops 1153500 | tf_op jit(solution)/shard_map/pallas_call | solution.py:376
  32.8 2.0 %collective-permute-done.6.refs_1_ = bf16[256,512]{1,0:T(8,128)(2,1)S(1)} collective-permute-done((bf16[256,512]{1,0:T(8,128)(2,1)S(1)}, bf16[256,512]{1,0:T(8,128)(2,1)S(1)}, u32[]{:S(2)}, u32[]{:S(2)}) %collective-permute-start.6) | collective-permute-done | bytes 262176 | tf_op jit(solution)/shard_map/ppermute | solution.py:36
  34.8 0.4 shard_map.123
  35.2 2.1 %collective-permute-done.7.refs_2_.refs_3_ = bf16[256,512]{1,0:T(8,128)(2,1)S(1)} collective-permute-done((bf16[256,512]{1,0:T(8,128)(2,1)S(1)}, bf16[256,512]{1,0:T(8,128)(2,1)S(1)}, u32[]{:S(2)}, u32[]{:S(2)}) %collective-permute-start.7) | collective-permute-done | bytes 262176 | tf_op jit(solution)/shard_map/ppermute | solution.py:40
  37.3 0.7 shard_map.125
  38.0 0.1 collective-permute-start.8
  38.0 1.3 %collective-permute-start.10 = (bf16[256,512]{1,0:T(8,128)(2,1)S(1)}, bf16[256,512]{1,0:T(8,128)(2,1)S(1)}, u32[]{:S(2)}, u32[]{:S(2)}) collective-permute-start(bf16[256,512]{1,0:T(8,128)(2,1)S(1)} %get-tuple-element.42.refs_2_.refs_1_.refs_5_), channel_id=1, source_target_pairs={{4,0},{6,2},{8,4},{10,6},{12,8},{14,10},{5,1},{7,3},{9,5},{11,7},{... | collective-permute-start | bytes 786440 | tf_op jit(solution)/shard_map/ppermute | solution.py:36
  39.4 1.5 %collective-permute-start.14 = (bf16[256,512]{1,0:T(8,128)(2,1)S(1)}, bf16[256,512]{1,0:T(8,128)(2,1)S(1)}, u32[]{:S(2)}, u32[]{:S(2)}) collective-permute-start(bf16[256,512]{1,0:T(8,128)(2,1)S(1)} %shard_map.133), channel_id=1, source_target_pairs={{0,2},{2,0},{4,6},{6,4},{8,10},{10,8},{12,14},{14,12},{1,3},{3,1},... | collective-permute-start | bytes 786440 | tf_op jit(solution)/shard_map/ppermute | solution.py:40
  40.8 0.1 shard_map.126
  41.0 0.7 collective-permute-start.9
  41.6 1.4 %shard_map.127 = (bf16[256,1024]{1,0:T(8,128)(2,1)}, bf16[256,512]{1,0:T(8,128)(2,1)}) custom-call(bf16[256,512]{1,0:T(8,128)(2,1)S(1)} %get-tuple-element.35.refs_0_, bf16[512,1024]{1,0:T(8,128)(2,1)S(1)} %copy-done.3, f32[256,512]{1,0:T(8,128)S(1)} %get-tuple-element.34.refs_2_, f32[256,512]{1,0:T(8,128)S(1)} %get-tuple-element.36.refs_3_, ...), custom_call_target="tpu_custom_call" | custom-call | flops 1153500 | tf_op jit(solution)/shard_map/pallas_call | solution.py:376
  43.0 0.8 %shard_map.128.refs_7_ = f32[256,512]{1,0:T(8,128)S(1)} custom-call(s32[1,4]{1,0:T(1,128)S(1)} %copy-done.7, bf16[256,512]{1,0:T(8,128)(2,1)S(1)} %bitcast.29, bf16[256,512]{1,0:T(8,128)(2,1)S(1)} %get-tuple-element.42.refs_2_.refs_1_.refs_5_, bf16[256,512]{1,0:T(8,128)(2,1)S(1)} %bitcast.13, ...), custom_call_target="tpu_custom_call" | custom-call | flops 1153500 | tf_op jit(solution)/shard_map/pallas_call | solution.py:376
  43.8 4.8 %collective-permute-done.10.refs_2_.refs_0_.refs_1_.refs_6_ = bf16[256,512]{1,0:T(8,128)(2,1)S(1)} collective-permute-done((bf16[256,512]{1,0:T(8,128)(2,1)S(1)}, bf16[256,512]{1,0:T(8,128)(2,1)S(1)}, u32[]{:S(2)}, u32[]{:S(2)}) %collective-permute-start.10) | collective-permute-done | bytes 262176 | tf_op jit(solution)/shard_map/ppermute | solution.py:36
  48.6 1.3 %collective-permute-start.15 = (bf16[256,512]{1,0:T(8,128)(2,1)S(1)}, bf16[256,512]{1,0:T(8,128)(2,1)S(1)}, u32[]{:S(2)}, u32[]{:S(2)}) collective-permute-start(bf16[256,512]{1,0:T(8,128)(2,1)S(1)} %collective-permute-done.10.refs_2_.refs_0_.refs_1_.refs_6_), channel_id=1, source_target_pairs={{4,0},{6,2},{8,4},{10,6},{12,8},{14,10},{5,1},{7,3},{9,5},{11,7},{... | collective-permute-start | bytes 786440 | tf_op jit(solution)/shard_map/ppermute | solution.py:36
  49.9 0.2 shard_map.129.refs_2_
  50.1 2.2 %collective-permute-start.17 = (bf16[256,512]{1,0:T(8,128)(2,1)S(1)}, bf16[256,512]{1,0:T(8,128)(2,1)S(1)}, u32[]{:S(2)}, u32[]{:S(2)}) collective-permute-start(bf16[256,512]{1,0:T(8,128)(2,1)S(1)} %shard_map.130.refs_2_), channel_id=1, source_target_pairs={{0,2},{2,0},{4,6},{6,4},{8,10},{10,8},{12,14},{14,12},{1,3},{3,1},... | collective-permute-start | bytes 786440 | tf_op jit(solution)/shard_map/ppermute | solution.py:40
  52.4 3.9 %collective-permute-start.18 = (bf16[256,512]{1,0:T(8,128)(2,1)S(1)}, bf16[256,512]{1,0:T(8,128)(2,1)S(1)}, u32[]{:S(2)}, u32[]{:S(2)}) collective-permute-start(bf16[256,512]{1,0:T(8,128)(2,1)S(1)} %shard_map.129.refs_2_), channel_id=1, source_target_pairs={{0,4},{2,6},{4,8},{6,10},{8,12},{10,14},{1,5},{3,7},{5,9},{7,11},{... | collective-permute-start | bytes 786440 | tf_op jit(solution)/shard_map/ppermute | solution.py:36
  56.3 0.1 shard_map.131
  56.4 1.5 %collective-permute-start.11 = (bf16[1,32,1024]{2,1,0:T(8,128)(2,1)S(1)}, bf16[1,32,1024]{2,1,0:T(8,128)(2,1)S(1)}, u32[]{:S(2)}, u32[]{:S(2)}) collective-permute-start(bf16[1,32,1024]{2,1,0:T(8,128)(2,1)S(1)} %get-tuple-element.45), channel_id=1, source_target_pairs={{0,4},{2,6},{4,0},{6,2},{8,12},{10,14},{12,8},{14,10},{1,5},{3,7},... | collective-permute-start | bytes 196616 | tf_op jit(solution)/shard_map/ppermute | solution.py:40
  57.9 1.6 %collective-permute-start.12 = (bf16[1,32,1024]{2,1,0:T(8,128)(2,1)S(1)}, bf16[1,32,1024]{2,1,0:T(8,128)(2,1)S(1)}, u32[]{:S(2)}, u32[]{:S(2)}) collective-permute-start(bf16[1,32,1024]{2,1,0:T(8,128)(2,1)S(1)} %get-tuple-element.46), channel_id=1, source_target_pairs={{0,8},{2,10},{4,12},{6,14},{8,0},{10,2},{12,4},{14,6},{1,9},{3,11}... | collective-permute-start | bytes 196616 | tf_op jit(solution)/shard_map/ppermute | solution.py:40
  59.5 1.4 %collective-permute-start.13 = (bf16[1,32,1024]{2,1,0:T(8,128)(2,1)S(1)}, bf16[1,32,1024]{2,1,0:T(8,128)(2,1)S(1)}, u32[]{:S(2)}, u32[]{:S(2)}) collective-permute-start(bf16[1,32,1024]{2,1,0:T(8,128)(2,1)S(1)} %get-tuple-element.47), channel_id=1, source_target_pairs={{0,12},{2,14},{4,8},{6,10},{8,4},{10,6},{12,0},{14,2},{1,13},{3,15... | collective-permute-start | bytes 196616 | tf_op jit(solution)/shard_map/ppermute | solution.py:40
  60.9 1.8 %shard_map.135 = (f32[256,512]{1,0:T(8,128)S(1)}, f32[256,512]{1,0:T(8,128)S(1)}) custom-call(s32[1,4]{1,0:T(1,128)S(1)} %copy-done.7, bf16[256,512]{1,0:T(8,128)(2,1)S(1)} %bitcast.14, bf16[256,512]{1,0:T(8,128)(2,1)S(1)} %bitcast.22, bf16[256,512]{1,0:T(8,128)(2,1)S(1)} %bitcast.30, bf16[256,512]{1,0:T(8,128)(2,1)S(1)} %collective-permute-done.4.refs_1_.refs_0_.refs_4_, ...), custom_call_target="tpu_custom_call" | custom-call | flops 1153500 | tf_op jit(solution)/shard_map/pallas_call | solution.py:376
  62.8 2.1 %collective-permute-start.16 = (bf16[256,512]{1,0:T(8,128)(2,1)S(1)}, bf16[256,512]{1,0:T(8,128)(2,1)S(1)}, u32[]{:S(2)}, u32[]{:S(2)}) collective-permute-start(bf16[256,512]{1,0:T(8,128)(2,1)S(1)} %shard_map.134), channel_id=1, source_target_pairs={{0,2},{2,0},{4,6},{6,4},{8,10},{10,8},{12,14},{14,12},{1,3},{3,1},... | collective-permute-start | bytes 786440 | tf_op jit(solution)/shard_map/ppermute | solution.py:40
  64.8 1.2 %shard_map.136 = (f32[256,512]{1,0:T(8,128)S(1)}, f32[256,512]{1,0:T(8,128)S(1)}) custom-call(s32[1,4]{1,0:T(1,128)S(1)} %copy-done.7, bf16[256,512]{1,0:T(8,128)(2,1)S(1)} %bitcast.15, bf16[256,512]{1,0:T(8,128)(2,1)S(1)} %bitcast.23, bf16[256,512]{1,0:T(8,128)(2,1)S(1)} %collective-permute-done.7.refs_2_.refs_3_, ...), custom_call_target="tpu_custom_call" | custom-call | flops 1153500 | tf_op jit(solution)/shard_map/pallas_call | solution.py:376
  66.1 0.7 shard_map.132
  66.8 1.0 %shard_map.137 = (f32[256,512]{1,0:T(8,128)S(1)}, f32[256,512]{1,0:T(8,128)S(1)}) custom-call(s32[1,4]{1,0:T(1,128)S(1)} %copy-done.7, bf16[256,512]{1,0:T(8,128)(2,1)S(1)} %bitcast.16, bf16[256,512]{1,0:T(8,128)(2,1)S(1)} %bitcast.24, bf16[256,512]{1,0:T(8,128)(2,1)S(1)} %collective-permute-done.5.refs_10_.refs_0_.refs_3_, ...), custom_call_target="tpu_custom_call" | custom-call | flops 4614000128 | tf_op jit(solution)/shard_map/pallas_call | solution.py:376
  67.8 1.4 %collective-permute-done.16.refs_4_ = bf16[256,512]{1,0:T(8,128)(2,1)S(1)} collective-permute-done((bf16[256,512]{1,0:T(8,128)(2,1)S(1)}, bf16[256,512]{1,0:T(8,128)(2,1)S(1)}, u32[]{:S(2)}, u32[]{:S(2)}) %collective-permute-start.16) | collective-permute-done | bytes 262176 | tf_op jit(solution)/shard_map/ppermute | solution.py:40
  69.2 2.1 %shard_map.138 = (bf16[256,512]{1,0:T(8,128)(2,1)}, bf16[256,512]{1,0:T(8,128)(2,1)}, bf16[256,512]{1,0:T(8,128)(2,1)}) custom-call(s32[1,4]{1,0:T(1,128)S(1)} %copy-done.7, bf16[256,512]{1,0:T(8,128)(2,1)S(1)} %bitcast.17, bf16[256,512]{1,0:T(8,128)(2,1)S(1)} %bitcast.25, bf16[256,512]{1,0:T(8,128)(2,1)S(1)} %collective-permute-done.14.refs_7_.refs_3_, ...), custom_call_target="tpu_custom_call" | custom-call | flops 1153500 | tf_op jit(solution)/shard_map/pallas_call | solution.py:376
  (27 shorter events, 0.3 us)
Async XLA Ops:
  0.6 11.9 %collective-permute-start = (bf16[256,512]{1,0:T(8,128)(2,1)}, bf16[256,512]{1,0:T(8,128)(2,1)S(1)}, u32[]{:S(2)}, u32[]{:S(2)}) collective-permute-start(bf16[256,512]{1,0:T(8,128)(2,1)} %bitcast.10), channel_id=1, source_target_pairs={{0,4},{2,6},{4,8},{6,10},{8,12},{10,14},{1,5},{3,7},{5,9},{7,11},{... | collective-permute-start | bytes 786440 | tf_op jit(solution)/shard_map/ppermute | solution.py:36
  5.6 11.5 %collective-permute-start.2 = (bf16[256,512]{1,0:T(8,128)(2,1)}, bf16[256,512]{1,0:T(8,128)(2,1)S(1)}, u32[]{:S(2)}, u32[]{:S(2)}) collective-permute-start(bf16[256,512]{1,0:T(8,128)(2,1)} %bitcast.18), channel_id=1, source_target_pairs={{0,4},{2,6},{4,8},{6,10},{8,12},{10,14},{1,5},{3,7},{5,9},{7,11},{... | collective-permute-start | bytes 786440 | tf_op jit(solution)/shard_map/ppermute | solution.py:36
  9.1 9.6 %collective-permute-start.4 = (bf16[256,512]{1,0:T(8,128)(2,1)}, bf16[256,512]{1,0:T(8,128)(2,1)S(1)}, u32[]{:S(2)}, u32[]{:S(2)}) collective-permute-start(bf16[256,512]{1,0:T(8,128)(2,1)} %bitcast.26), channel_id=1, source_target_pairs={{4,0},{6,2},{8,4},{10,6},{12,8},{14,10},{5,1},{7,3},{9,5},{11,7},{... | collective-permute-start | bytes 786440 | tf_op jit(solution)/shard_map/ppermute | solution.py:36
  12.6 0.9 %copy-start = (bf16[1,256,512]{2,1,0:T(8,128)(2,1)S(1)}, bf16[1,256,512]{2,1,0:T(8,128)(2,1)}, u32[]{:S(2)}) copy-start(bf16[1,256,512]{2,1,0:T(8,128)(2,1)} %param.8) | copy-start | bytes 786436
  13.5 3.5 %copy-start.2 = (bf16[1,256,512]{2,1,0:T(8,128)(2,1)S(1)}, bf16[1,256,512]{2,1,0:T(8,128)(2,1)}, u32[]{:S(2)}) copy-start(bf16[1,256,512]{2,1,0:T(8,128)(2,1)} %param.9) | copy-start | bytes 786436
  13.6 7.7 %copy-start.7 = (s32[1,4]{1,0:T(1,128)S(1)}, s32[1,4]{1,0:T(1,128)}, u32[]{:S(2)}) copy-start(s32[1,4]{1,0:T(1,128)} %refs_0_.17) | copy-start | bytes 52
  13.6 7.7 %collective-permute-start.1 = (bf16[256,512]{1,0:T(8,128)(2,1)S(1)}, bf16[256,512]{1,0:T(8,128)(2,1)S(1)}, u32[]{:S(2)}, u32[]{:S(2)}) collective-permute-start(bf16[256,512]{1,0:T(8,128)(2,1)S(1)} %shard_map.118), channel_id=1, source_target_pairs={{0,2},{2,0},{4,6},{6,4},{8,10},{10,8},{12,14},{14,12},{1,3},{3,1},... | collective-permute-start | bytes 786440 | tf_op jit(solution)/shard_map/ppermute | solution.py:40
  17.1 8.5 %collective-permute-start.3 = (bf16[256,512]{1,0:T(8,128)(2,1)S(1)}, bf16[256,512]{1,0:T(8,128)(2,1)S(1)}, u32[]{:S(2)}, u32[]{:S(2)}) collective-permute-start(bf16[256,512]{1,0:T(8,128)(2,1)S(1)} %shard_map.119), channel_id=1, source_target_pairs={{0,2},{2,0},{4,6},{6,4},{8,10},{10,8},{12,14},{14,12},{1,3},{3,1},... | collective-permute-start | bytes 786440 | tf_op jit(solution)/shard_map/ppermute | solution.py:40
  18.7 13.2 %collective-permute-start.5 = (bf16[256,512]{1,0:T(8,128)(2,1)S(1)}, bf16[256,512]{1,0:T(8,128)(2,1)S(1)}, u32[]{:S(2)}, u32[]{:S(2)}) collective-permute-start(bf16[256,512]{1,0:T(8,128)(2,1)S(1)} %collective-permute-done.4.refs_1_.refs_0_.refs_4_), channel_id=1, source_target_pairs={{4,0},{6,2},{8,4},{10,6},{12,8},{14,10},{5,1},{7,3},{9,5},{11,7},{... | collective-permute-start | bytes 786440 | tf_op jit(solution)/shard_map/ppermute | solution.py:36
  21.4 9.4 %copy-start.4 = (bf16[1,256,512]{2,1,0:T(8,128)(2,1)S(1)}, bf16[1,256,512]{2,1,0:T(8,128)(2,1)}, u32[]{:S(2)}) copy-start(bf16[1,256,512]{2,1,0:T(8,128)(2,1)} %param.7) | copy-start | bytes 786436
  21.4 10.5 %copy-start.3 = (bf16[512,1024]{1,0:T(8,128)(2,1)S(1)}, bf16[512,1024]{1,0:T(8,128)(2,1)}, u32[]{:S(2)}) copy-start(bf16[512,1024]{1,0:T(8,128)(2,1)} %refs_1_.1) | copy-start | bytes 3145732
  25.8 6.1 %copy-start.1 = (bf16[1,256,512]{2,1,0:T(8,128)(2,1)S(1)}, bf16[1,256,512]{2,1,0:T(8,128)(2,1)}, u32[]{:S(2)}) copy-start(bf16[1,256,512]{2,1,0:T(8,128)(2,1)} %param.8) | copy-start | bytes 786436
  25.8 6.1 %copy-start.5 = (bf16[1,256,1024]{2,1,0:T(8,128)(2,1)S(1)}, bf16[1,256,1024]{2,1,0:T(8,128)(2,1)}, u32[]{:S(2)}) copy-start(bf16[1,256,1024]{2,1,0:T(8,128)(2,1)} %param.12) | copy-start | bytes 1572868
  25.8 9.0 %collective-permute-start.6 = (bf16[256,512]{1,0:T(8,128)(2,1)S(1)}, bf16[256,512]{1,0:T(8,128)(2,1)S(1)}, u32[]{:S(2)}, u32[]{:S(2)}) collective-permute-start(bf16[256,512]{1,0:T(8,128)(2,1)S(1)} %shard_map.122.refs_2_), channel_id=1, source_target_pairs={{0,4},{2,6},{4,8},{6,10},{8,12},{10,14},{1,5},{3,7},{5,9},{7,11},{... | collective-permute-start | bytes 786440 | tf_op jit(solution)/shard_map/ppermute | solution.py:36
  30.9 6.4 %collective-permute-start.7 = (bf16[256,512]{1,0:T(8,128)(2,1)S(1)}, bf16[256,512]{1,0:T(8,128)(2,1)S(1)}, u32[]{:S(2)}, u32[]{:S(2)}) collective-permute-start(bf16[256,512]{1,0:T(8,128)(2,1)S(1)} %shard_map.124), channel_id=1, source_target_pairs={{0,2},{2,0},{4,6},{6,4},{8,10},{10,8},{12,14},{14,12},{1,3},{3,1},... | collective-permute-start | bytes 786440 | tf_op jit(solution)/shard_map/ppermute | solution.py:40
  31.9 2.9 %copy-start.6 = (bf16[1,256,512]{2,1,0:T(8,128)(2,1)S(1)}, bf16[1,256,512]{2,1,0:T(8,128)(2,1)}, u32[]{:S(2)}) copy-start(bf16[1,256,512]{2,1,0:T(8,128)(2,1)} %param.10) | copy-start | bytes 786436
  38.0 2.9 %collective-permute-start.8 = (bf16[8,32,1024]{2,1,0:T(8,128)(2,1)S(1)}, bf16[8,32,1024]{2,1,0:T(8,128)(2,1)S(1)}, u32[]{:S(2)}, u32[]{:S(2)}) collective-permute-start(bf16[8,32,1024]{2,1,0:T(8,128)(2,1)S(1)} %get-tuple-element.38), channel_id=1, source_target_pairs={{0,1},{1,0},{2,3},{3,2},{4,5},{5,4},{6,7},{7,6},{8,9},{9,8},{10,11... | collective-permute-start | bytes 1572872 | tf_op jit(solution)/shard_map/ppermute | solution.py:40
  38.0 10.6 %collective-permute-start.10 = (bf16[256,512]{1,0:T(8,128)(2,1)S(1)}, bf16[256,512]{1,0:T(8,128)(2,1)S(1)}, u32[]{:S(2)}, u32[]{:S(2)}) collective-permute-start(bf16[256,512]{1,0:T(8,128)(2,1)S(1)} %get-tuple-element.42.refs_2_.refs_1_.refs_5_), channel_id=1, source_target_pairs={{4,0},{6,2},{8,4},{10,6},{12,8},{14,10},{5,1},{7,3},{9,5},{11,7},{... | collective-permute-start | bytes 786440 | tf_op jit(solution)/shard_map/ppermute | solution.py:36
  39.4 18.5 %collective-permute-start.14 = (bf16[256,512]{1,0:T(8,128)(2,1)S(1)}, bf16[256,512]{1,0:T(8,128)(2,1)S(1)}, u32[]{:S(2)}, u32[]{:S(2)}) collective-permute-start(bf16[256,512]{1,0:T(8,128)(2,1)S(1)} %shard_map.133), channel_id=1, source_target_pairs={{0,2},{2,0},{4,6},{6,4},{8,10},{10,8},{12,14},{14,12},{1,3},{3,1},... | collective-permute-start | bytes 786440 | tf_op jit(solution)/shard_map/ppermute | solution.py:40
  41.0 15.4 %collective-permute-start.9 = (bf16[4,32,1024]{2,1,0:T(8,128)(2,1)S(1)}, bf16[4,32,1024]{2,1,0:T(8,128)(2,1)S(1)}, u32[]{:S(2)}, u32[]{:S(2)}) collective-permute-start(bf16[4,32,1024]{2,1,0:T(8,128)(2,1)S(1)} %get-tuple-element.41), channel_id=1, source_target_pairs={{0,2},{2,0},{4,6},{6,4},{8,10},{10,8},{12,14},{14,12},{1,3},{3,1},... | collective-permute-start | bytes 786440 | tf_op jit(solution)/shard_map/ppermute | solution.py:40
  48.6 10.8 %collective-permute-start.15 = (bf16[256,512]{1,0:T(8,128)(2,1)S(1)}, bf16[256,512]{1,0:T(8,128)(2,1)S(1)}, u32[]{:S(2)}, u32[]{:S(2)}) collective-permute-start(bf16[256,512]{1,0:T(8,128)(2,1)S(1)} %collective-permute-done.10.refs_2_.refs_0_.refs_1_.refs_6_), channel_id=1, source_target_pairs={{4,0},{6,2},{8,4},{10,6},{12,8},{14,10},{5,1},{7,3},{9,5},{11,7},{... | collective-permute-start | bytes 786440 | tf_op jit(solution)/shard_map/ppermute | solution.py:36
  50.1 12.6 %collective-permute-start.17 = (bf16[256,512]{1,0:T(8,128)(2,1)S(1)}, bf16[256,512]{1,0:T(8,128)(2,1)S(1)}, u32[]{:S(2)}, u32[]{:S(2)}) collective-permute-start(bf16[256,512]{1,0:T(8,128)(2,1)S(1)} %shard_map.130.refs_2_), channel_id=1, source_target_pairs={{0,2},{2,0},{4,6},{6,4},{8,10},{10,8},{12,14},{14,12},{1,3},{3,1},... | collective-permute-start | bytes 786440 | tf_op jit(solution)/shard_map/ppermute | solution.py:40
  52.4 12.5 %collective-permute-start.18 = (bf16[256,512]{1,0:T(8,128)(2,1)S(1)}, bf16[256,512]{1,0:T(8,128)(2,1)S(1)}, u32[]{:S(2)}, u32[]{:S(2)}) collective-permute-start(bf16[256,512]{1,0:T(8,128)(2,1)S(1)} %shard_map.129.refs_2_), channel_id=1, source_target_pairs={{0,4},{2,6},{4,8},{6,10},{8,12},{10,14},{1,5},{3,7},{5,9},{7,11},{... | collective-permute-start | bytes 786440 | tf_op jit(solution)/shard_map/ppermute | solution.py:36
  56.4 9.6 %collective-permute-start.11 = (bf16[1,32,1024]{2,1,0:T(8,128)(2,1)S(1)}, bf16[1,32,1024]{2,1,0:T(8,128)(2,1)S(1)}, u32[]{:S(2)}, u32[]{:S(2)}) collective-permute-start(bf16[1,32,1024]{2,1,0:T(8,128)(2,1)S(1)} %get-tuple-element.45), channel_id=1, source_target_pairs={{0,4},{2,6},{4,0},{6,2},{8,12},{10,14},{12,8},{14,10},{1,5},{3,7},... | collective-permute-start | bytes 196616 | tf_op jit(solution)/shard_map/ppermute | solution.py:40
  57.9 8.2 %collective-permute-start.12 = (bf16[1,32,1024]{2,1,0:T(8,128)(2,1)S(1)}, bf16[1,32,1024]{2,1,0:T(8,128)(2,1)S(1)}, u32[]{:S(2)}, u32[]{:S(2)}) collective-permute-start(bf16[1,32,1024]{2,1,0:T(8,128)(2,1)S(1)} %get-tuple-element.46), channel_id=1, source_target_pairs={{0,8},{2,10},{4,12},{6,14},{8,0},{10,2},{12,4},{14,6},{1,9},{3,11}... | collective-permute-start | bytes 196616 | tf_op jit(solution)/shard_map/ppermute | solution.py:40
  59.5 6.6 %collective-permute-start.13 = (bf16[1,32,1024]{2,1,0:T(8,128)(2,1)S(1)}, bf16[1,32,1024]{2,1,0:T(8,128)(2,1)S(1)}, u32[]{:S(2)}, u32[]{:S(2)}) collective-permute-start(bf16[1,32,1024]{2,1,0:T(8,128)(2,1)S(1)} %get-tuple-element.47), channel_id=1, source_target_pairs={{0,12},{2,14},{4,8},{6,10},{8,4},{10,6},{12,0},{14,2},{1,13},{3,15... | collective-permute-start | bytes 196616 | tf_op jit(solution)/shard_map/ppermute | solution.py:40
  62.8 6.4 %collective-permute-start.16 = (bf16[256,512]{1,0:T(8,128)(2,1)S(1)}, bf16[256,512]{1,0:T(8,128)(2,1)S(1)}, u32[]{:S(2)}, u32[]{:S(2)}) collective-permute-start(bf16[256,512]{1,0:T(8,128)(2,1)S(1)} %shard_map.134), channel_id=1, source_target_pairs={{0,2},{2,0},{4,6},{6,4},{8,10},{10,8},{12,14},{14,12},{1,3},{3,1},... | collective-permute-start | bytes 786440 | tf_op jit(solution)/shard_map/ppermute | solution.py:40

commit v4 on v3

--- a/solution.py
+++ b/solution.py
@@ -15,7 +15,7 @@
 F32 = jnp.float32
 VMEM = pl.BlockSpec(memory_space=pltpu.VMEM)
 HINT = {
-    "pick": 0.001,
+    "pick": 10.0,
     "attend": 0.001,
     "far_mix": 0.001,
     "near_mix": 0.001,
@@ -26,7 +26,7 @@
     "part": 0.001,
     "sum": 0.001,
     "far_query": 0.001,
-    "keys": (0.001, 0.001, 4.0, 0.001),
+    "keys": (0.001, 0.001, 0.001, 4.0, 0.001),
 }
 ANY = pl.BlockSpec(memory_space=pl.ANY)
 
@@ -461,13 +461,20 @@
         HINT["norm"],
     )
     chunk = (width // (count * cores), model)
+    (near_query,) = call(
+        functools.partial(query_grad_kernel, 0, near),
+        wide,
+        [lengths, q, grad_mixed, *near_keys],
+        HINT["near_query"],
+        [total],
+    )
     keep, give = call(
         weight_kernel,
         [((count, *chunk), F32), ((count, *chunk), BF16)],
         [gated, out_grad],
         HINT["weight"],
         [pltpu.VMEM((width, model), F32)],
-        [query_at[1]],
+        [near_query, query_at[1]],
     )
     came = swapped(give, "dp", 1)
     step, parts = 1, count
@@ -481,14 +488,6 @@
         )
         came = swapped(give, "ctx", step)
         step *= 2
-    (near_query,) = call(
-        functools.partial(query_grad_kernel, 0, near),
-        wide,
-        [lengths, q, grad_mixed, *near_keys],
-        HINT["near_query"],
-        [total],
-        [keep],
-    )
     output, grad_gates = call(
         out_kernel,
         [((tok, model), BF16), *one],
@@ -497,20 +496,9 @@
         (),
         [keep],
     )
-    grad_at = {0: grad_mixed, 2: shifted(grad_mixed, -2)}
-    grad_at[2], *_ = lax.optimization_barrier([grad_at[2], near_query, output])
-    for distance in range(4, reach + 1, 2):
-        grad_at[distance] = shifted(grad_at[distance - 2], -2)
-    (far_query_term,) = call(
-        functools.partial(query_grad_kernel, mid, far),
-        one,
-        [lengths, query_at[mid], grad_at[mid], *back_keys],
-        HINT["far_query"],
-        [total],
-    )
-    far_query = shifted(far_query_term, mid)
-    sent = {1: picked(grad_at[2], grad_mixed, [far_query_term])}
-    groups = [[d for d in part if d % 2 == odd] for part in (near, far) for odd in (0, 1)]
+    grad_at = {0: grad_mixed}
+
+    groups = [[0]] + [[d for d in part if d > 0 and d % 2 == odd] for part in (near, far) for odd in (0, 1)]
 
     def key_terms(n, carried, after=()):
         group, last = groups[n], n == len(groups) - 1
@@ -523,12 +511,25 @@
             after,
         )
 
+    grads = key_terms(0, [], [keep])
+    grad_at[2], *_ = lax.optimization_barrier([shifted(grad_mixed, -2), near_query, output, *grads])
+    for distance in range(4, reach + 1, 2):
+        grad_at[distance] = shifted(grad_at[distance - 2], -2)
+    (far_query_term,) = call(
+        functools.partial(query_grad_kernel, mid, far),
+        one,
+        [lengths, query_at[mid], grad_at[mid], *back_keys],
+        HINT["far_query"],
+        [total],
+    )
+    far_query = shifted(far_query_term, mid)
+    sent = {1: picked(grad_at[2], grad_mixed, [far_query_term])}
     for distance in range(3, reach, 2):
         sent[distance] = picked(grad_at[distance + 1], grad_at[distance - 1])
     for distance, block in sent.items():
         grad_at[distance] = swapped(block, "ctx", 1)
-    grads = key_terms(0, [], [query_at[reach - 1]])
-    grads = key_terms(1, grads, [far_query])
+    grads = key_terms(1, grads, [query_at[reach - 1]])
+    grads = key_terms(2, grads)
     keep, *gives = call(
         functools.partial(spread_kernel, step),
         [((1, *chunk), F32)] + [((1, *chunk), BF16)] * (parts - 1),
@@ -544,8 +545,8 @@
         [keep, *shares],
         HINT["sum"],
     )
-    grads = key_terms(2, grads, [summed])
-    key_grad, value_grad, query_grad = key_terms(3, [*grads, near_query, far_query])
+    grads = key_terms(3, grads, [summed, far_query])
+    key_grad, value_grad, query_grad = key_terms(4, [*grads, near_query, far_query])
     return (
         output[None],
         grad_weight,

time: 72.4 us -> 70.5 us (0.974)
  starting transfers between devices: 37.7 us -> 43.7 us
  waiting for transfers between devices: 19.9 us -> 14.4 us
  Pallas kernels: 11.8 us -> 9.11 us
    ppermute x8, waiting for transfers between devices: 10.9 us -> 5.54 us  [shifted(): lax.ppermute(block, 'ctx', [(i, i + distance) for i in devices if i + dis...]
    ppermute x11, starting transfers between devices: 15.2 us -> 18.3 us  [swapped(): lax.ppermute(block, axis, [(i, i ^ step) for i in range(lax.axis_size(axi...]
    ppermute x8, starting transfers between devices: 22.5 us -> 25.5 us  [shifted(): lax.ppermute(block, 'ctx', [(i, i + distance) for i in devices if i + dis...]
    pallas_call x21 -> x22, Pallas kernels: 11.8 us -> 9.11 us  [call(): pl.pallas_call(body, out_shape=shapes, in_specs=[VMEM] * len(args) + [ANY...]
  transfers between devices with their start and end apart: 19 -> 19, of which waited for: 8 -> 8; matrix products, arithmetic and copies ran while one was open for 0% -> 0% of each run, Pallas kernels for 13% -> 12%
where the time goes in v4:
time: 70.5 us; the launch traced here: 69.2 us
  starting transfers between devices  43.7 us (62%)
  waiting for transfers between devices  14.4 us (20%)
  Pallas kernels  9.11 us (13%)
  local copies, waits for them, and re-layouts  0.99 us (1%)
  between operations  0.95 us (1%)
    ppermute x8, starting transfers between devices, shifted(): lax.ppermute(block, 'ctx', [(i, i + distance) for i in devices if i + dis...  25.5 us
    ppermute x11, starting transfers between devices, swapped(): lax.ppermute(block, axis, [(i, i ^ step) for i in range(lax.axis_size(axi...  18.3 us
    pallas_call x22, Pallas kernels, call(): pl.pallas_call(body, out_shape=shapes, in_specs=[VMEM] * len(args) + [ANY...  9.11 us
    ppermute x11, waiting for transfers between devices, swapped(): lax.ppermute(block, axis, [(i, i ^ step) for i in range(lax.axis_size(axi...  8.87 us
    ppermute x8, waiting for transfers between devices, shifted(): lax.ppermute(block, 'ctx', [(i, i + distance) for i in devices if i + dis...  5.54 us
  transfers between devices with their start and end apart: 19, of which 8 were waited for; matrix products, arithmetic and copies ran while one was open for 0% of the time, Pallas kernels for 12%

profile of v4, /device:TPU:0, one launch (start us, length us, event | category | flops | bytes accessed | tf_op | source)
XLA Modules:
  0.0 69.2 jit_solution(17535848947500388272)
XLA Ops:
  0.6 4.9 %collective-permute-start = (bf16[256,512]{1,0:T(8,128)(2,1)}, bf16[256,512]{1,0:T(8,128)(2,1)S(1)}, u32[]{:S(2)}, u32[]{:S(2)}) collective-permute-start(bf16[256,512]{1,0:T(8,128)(2,1)} %bitcast.10), channel_id=1, source_target_pairs={{0,4},{2,6},{4,8},{6,10},{8,12},{10,14},{1,5},{3,7},{5,9},{7,11},{... | collective-permute-start | bytes 786440 | tf_op jit(solution)/shard_map/ppermute | solution.py:36
  5.6 3.5 %collective-permute-start.2 = (bf16[256,512]{1,0:T(8,128)(2,1)}, bf16[256,512]{1,0:T(8,128)(2,1)S(1)}, u32[]{:S(2)}, u32[]{:S(2)}) collective-permute-start(bf16[256,512]{1,0:T(8,128)(2,1)} %bitcast.19), channel_id=1, source_target_pairs={{0,4},{2,6},{4,8},{6,10},{8,12},{10,14},{1,5},{3,7},{5,9},{7,11},{... | collective-permute-start | bytes 786440 | tf_op jit(solution)/shard_map/ppermute | solution.py:36
  9.1 1.3 %collective-permute-start.4 = (bf16[256,512]{1,0:T(8,128)(2,1)}, bf16[256,512]{1,0:T(8,128)(2,1)S(1)}, u32[]{:S(2)}, u32[]{:S(2)}) collective-permute-start(bf16[256,512]{1,0:T(8,128)(2,1)} %bitcast.28), channel_id=1, source_target_pairs={{4,0},{6,2},{8,4},{10,6},{12,8},{14,10},{5,1},{7,3},{9,5},{11,7},{... | collective-permute-start | bytes 786440 | tf_op jit(solution)/shard_map/ppermute | solution.py:36
  10.4 2.2 %collective-permute-done.odd_ref.refs_4_.refs_3_.refs_5_ = bf16[256,512]{1,0:T(8,128)(2,1)S(1)} collective-permute-done((bf16[256,512]{1,0:T(8,128)(2,1)}, bf16[256,512]{1,0:T(8,128)(2,1)S(1)}, u32[]{:S(2)}, u32[]{:S(2)}) %collective-permute-start) | collective-permute-done | bytes 262176 | tf_op jit(solution)/shard_map/ppermute | solution.py:36
  12.6 0.9 %copy-done = bf16[1,256,512]{2,1,0:T(8,128)(2,1)S(1)} copy-done((bf16[1,256,512]{2,1,0:T(8,128)(2,1)S(1)}, bf16[1,256,512]{2,1,0:T(8,128)(2,1)}, u32[]{:S(2)}) %copy-start) | copy-done | bytes 262168
  13.6 0.0 copy-start.7
  13.6 1.6 %collective-permute-start.1 = (bf16[256,512]{1,0:T(8,128)(2,1)S(1)}, bf16[256,512]{1,0:T(8,128)(2,1)S(1)}, u32[]{:S(2)}, u32[]{:S(2)}) collective-permute-start(bf16[256,512]{1,0:T(8,128)(2,1)S(1)} %shard_map.118), channel_id=1, source_target_pairs={{0,2},{2,0},{4,6},{6,4},{8,10},{10,8},{12,14},{14,12},{1,3},{3,1},... | collective-permute-start | bytes 786440 | tf_op jit(solution)/shard_map/ppermute | solution.py:40
  15.2 1.9 %collective-permute-done.2.odd_ref.refs_7_.refs_3_.refs_8_.refs_6_ = bf16[256,512]{1,0:T(8,128)(2,1)S(1)} collective-permute-done((bf16[256,512]{1,0:T(8,128)(2,1)}, bf16[256,512]{1,0:T(8,128)(2,1)S(1)}, u32[]{:S(2)}, u32[]{:S(2)}) %collective-permute-start.2) | collective-permute-done | bytes 262176 | tf_op jit(solution)/shard_map/ppermute | solution.py:36
  17.1 1.6 %collective-permute-start.3 = (bf16[256,512]{1,0:T(8,128)(2,1)S(1)}, bf16[256,512]{1,0:T(8,128)(2,1)S(1)}, u32[]{:S(2)}, u32[]{:S(2)}) collective-permute-start(bf16[256,512]{1,0:T(8,128)(2,1)S(1)} %shard_map.119), channel_id=1, source_target_pairs={{0,2},{2,0},{4,6},{6,4},{8,10},{10,8},{12,14},{14,12},{1,3},{3,1},... | collective-permute-start | bytes 786440 | tf_op jit(solution)/shard_map/ppermute | solution.py:40
  18.7 1.3 %collective-permute-start.5 = (bf16[256,512]{1,0:T(8,128)(2,1)S(1)}, bf16[256,512]{1,0:T(8,128)(2,1)S(1)}, u32[]{:S(2)}, u32[]{:S(2)}) collective-permute-start(bf16[256,512]{1,0:T(8,128)(2,1)S(1)} %collective-permute-done.4.refs_1_.refs_0_.refs_3_), channel_id=1, source_target_pairs={{4,0},{6,2},{8,4},{10,6},{12,8},{14,10},{5,1},{7,3},{9,5},{11,7},{... | collective-permute-start | bytes 786440 | tf_op jit(solution)/shard_map/ppermute | solution.py:36
  20.0 1.3 %collective-permute-done.1.refs_3_.refs_2_.refs_4_ = bf16[256,512]{1,0:T(8,128)(2,1)S(1)} collective-permute-done((bf16[256,512]{1,0:T(8,128)(2,1)S(1)}, bf16[256,512]{1,0:T(8,128)(2,1)S(1)}, u32[]{:S(2)}, u32[]{:S(2)}) %collective-permute-start.1) | collective-permute-done | bytes 262176 | tf_op jit(solution)/shard_map/ppermute | solution.py:40
  21.3 0.1 shard_map.121.refs_1_
  21.4 4.2 %collective-permute-done.3.refs_6_.refs_2_.refs_7_.refs_5_ = bf16[256,512]{1,0:T(8,128)(2,1)S(1)} collective-permute-done((bf16[256,512]{1,0:T(8,128)(2,1)S(1)}, bf16[256,512]{1,0:T(8,128)(2,1)S(1)}, u32[]{:S(2)}, u32[]{:S(2)}) %collective-permute-start.3) | collective-permute-done | bytes 262176 | tf_op jit(solution)/shard_map/ppermute | solution.py:40
  25.6 0.1 shard_map.122.refs_2_
  25.8 0.0 copy-start.1
  25.8 0.0 copy-start.3
  25.8 4.7 %collective-permute-start.6 = (bf16[256,512]{1,0:T(8,128)(2,1)S(1)}, bf16[256,512]{1,0:T(8,128)(2,1)S(1)}, u32[]{:S(2)}, u32[]{:S(2)}) collective-permute-start(bf16[256,512]{1,0:T(8,128)(2,1)S(1)} %shard_map.122.refs_2_), channel_id=1, source_target_pairs={{0,4},{2,6},{4,8},{6,10},{8,12},{10,14},{1,5},{3,7},{5,9},{7,11},{... | collective-permute-start | bytes 786440 | tf_op jit(solution)/shard_map/ppermute | solution.py:36
  30.6 1.9 %collective-permute-start.7 = (bf16[256,512]{1,0:T(8,128)(2,1)S(1)}, bf16[256,512]{1,0:T(8,128)(2,1)S(1)}, u32[]{:S(2)}, u32[]{:S(2)}) collective-permute-start(bf16[256,512]{1,0:T(8,128)(2,1)S(1)} %shard_map.125), channel_id=1, source_target_pairs={{0,2},{2,0},{4,6},{6,4},{8,10},{10,8},{12,14},{14,12},{1,3},{3,1},... | collective-permute-start | bytes 786440 | tf_op jit(solution)/shard_map/ppermute | solution.py:40
  32.5 0.0 copy-start.6
  32.5 0.9 %shard_map.120 = (f32[256,512]{1,0:T(8,128)S(1)}, f32[256,512]{1,0:T(8,128)S(1)}) custom-call(s32[1,4]{1,0:T(1,128)S(1)} %copy-done.7, bf16[256,512]{1,0:T(8,128)(2,1)S(1)} %bitcast.30, bf16[256,512]{1,0:T(8,128)(2,1)S(1)} %bitcast.12, bf16[256,512]{1,0:T(8,128)(2,1)S(1)} %collective-permute-done.1.refs_3_.refs_2_.refs_4_, ...), custom_call_target="tpu_custom_call" | custom-call | flops 1153500 | tf_op jit(solution)/shard_map/pallas_call | solution.py:376
  33.4 1.4 %collective-permute-done.6.refs_1_ = bf16[256,512]{1,0:T(8,128)(2,1)S(1)} collective-permute-done((bf16[256,512]{1,0:T(8,128)(2,1)S(1)}, bf16[256,512]{1,0:T(8,128)(2,1)S(1)}, u32[]{:S(2)}, u32[]{:S(2)}) %collective-permute-start.6) | collective-permute-done | bytes 262176 | tf_op jit(solution)/shard_map/ppermute | solution.py:36
  34.8 0.4 shard_map.123
  35.2 1.3 %collective-permute-start.10 = (bf16[256,512]{1,0:T(8,128)(2,1)S(1)}, bf16[256,512]{1,0:T(8,128)(2,1)S(1)}, u32[]{:S(2)}, u32[]{:S(2)}) collective-permute-start(bf16[256,512]{1,0:T(8,128)(2,1)S(1)} %get-tuple-element.39.refs_2_.refs_4_.refs_1_), channel_id=1, source_target_pairs={{4,0},{6,2},{8,4},{10,6},{12,8},{14,10},{5,1},{7,3},{9,5},{11,7},{... | collective-permute-start | bytes 786440 | tf_op jit(solution)/shard_map/ppermute | solution.py:36
  36.5 0.8 %shard_map.124.refs_2_.refs_7_ = f32[256,512]{1,0:T(8,128)S(1)} custom-call(s32[1,4]{1,0:T(1,128)S(1)} %copy-done.7, bf16[256,512]{1,0:T(8,128)(2,1)S(1)} %bitcast.31, bf16[256,512]{1,0:T(8,128)(2,1)S(1)} %get-tuple-element.39.refs_2_.refs_4_.refs_1_, bf16[256,512]{1,0:T(8,128)(2,1)S(1)} %bitcast.13, ...), custom_call_target="tpu_custom_call" | custom-call | flops 1153500 | tf_op jit(solution)/shard_map/pallas_call | solution.py:376
  37.4 0.7 shard_map.126
  38.1 0.1 collective-permute-start.8
  38.2 2.4 %collective-permute-start.14 = (bf16[256,512]{1,0:T(8,128)(2,1)S(1)}, bf16[256,512]{1,0:T(8,128)(2,1)S(1)}, u32[]{:S(2)}, u32[]{:S(2)}) collective-permute-start(bf16[256,512]{1,0:T(8,128)(2,1)S(1)} %shard_map.134), channel_id=1, source_target_pairs={{0,2},{2,0},{4,6},{6,4},{8,10},{10,8},{12,14},{14,12},{1,3},{3,1},... | collective-permute-start | bytes 786440 | tf_op jit(solution)/shard_map/ppermute | solution.py:40
  40.5 0.1 shard_map.127
  40.6 1.8 %collective-permute-start.9 = (bf16[4,32,1024]{2,1,0:T(8,128)(2,1)S(1)}, bf16[4,32,1024]{2,1,0:T(8,128)(2,1)S(1)}, u32[]{:S(2)}, u32[]{:S(2)}) collective-permute-start(bf16[4,32,1024]{2,1,0:T(8,128)(2,1)S(1)} %get-tuple-element.44), channel_id=1, source_target_pairs={{0,2},{2,0},{4,6},{6,4},{8,10},{10,8},{12,14},{14,12},{1,3},{3,1},... | collective-permute-start | bytes 786440 | tf_op jit(solution)/shard_map/ppermute | solution.py:40
  42.5 0.9 %shard_map.129 = (f32[256,512]{1,0:T(8,128)S(1)}, f32[256,512]{1,0:T(8,128)S(1)}) custom-call(s32[1,4]{1,0:T(1,128)S(1)} %copy-done.7, bf16[256,512]{1,0:T(8,128)(2,1)S(1)} %bitcast.14, bf16[256,512]{1,0:T(8,128)(2,1)S(1)} %bitcast.23, bf16[256,512]{1,0:T(8,128)(2,1)S(1)} %bitcast.32, bf16[256,512]{1,0:T(8,128)(2,1)S(1)} %get-tuple-element.39.refs_2_.refs_4_.refs_1_, ...), custom_call_target="tpu_custom_call" | custom-call | flops 1153500 | tf_op jit(solution)/shard_map/pallas_call | solution.py:376
  43.4 1.3 %shard_map.128 = (bf16[256,1024]{1,0:T(8,128)(2,1)}, bf16[256,512]{1,0:T(8,128)(2,1)}) custom-call(bf16[256,512]{1,0:T(8,128)(2,1)S(1)} %get-tuple-element.37.refs_0_, bf16[512,1024]{1,0:T(8,128)(2,1)S(1)} %copy-done.3, f32[256,512]{1,0:T(8,128)S(1)} %get-tuple-element.36.refs_2_, f32[256,512]{1,0:T(8,128)S(1)} %get-tuple-element.38.refs_3_, ...), custom_call_target="tpu_custom_call" | custom-call | flops 1153500 | tf_op jit(solution)/shard_map/pallas_call | solution.py:376
  44.7 1.3 %collective-permute-start.15 = (bf16[256,512]{1,0:T(8,128)(2,1)S(1)}, bf16[256,512]{1,0:T(8,128)(2,1)S(1)}, u32[]{:S(2)}, u32[]{:S(2)}) collective-permute-start(bf16[256,512]{1,0:T(8,128)(2,1)S(1)} %collective-permute-done.10.refs_2_.refs_0_.refs_1_.refs_4_), channel_id=1, source_target_pairs={{4,0},{6,2},{8,4},{10,6},{12,8},{14,10},{5,1},{7,3},{9,5},{11,7},{... | collective-permute-start | bytes 786440 | tf_op jit(solution)/shard_map/ppermute | solution.py:36
  46.0 0.2 shard_map.130.refs_2_
  46.2 7.2 %collective-permute-start.18 = (bf16[256,512]{1,0:T(8,128)(2,1)S(1)}, bf16[256,512]{1,0:T(8,128)(2,1)S(1)}, u32[]{:S(2)}, u32[]{:S(2)}) collective-permute-start(bf16[256,512]{1,0:T(8,128)(2,1)S(1)} %shard_map.130.refs_2_), channel_id=1, source_target_pairs={{0,4},{2,6},{4,8},{6,10},{8,12},{10,14},{1,5},{3,7},{5,9},{7,11},{... | collective-permute-start | bytes 786440 | tf_op jit(solution)/shard_map/ppermute | solution.py:36
  53.4 1.1 %collective-permute-start.17 = (bf16[256,512]{1,0:T(8,128)(2,1)S(1)}, bf16[256,512]{1,0:T(8,128)(2,1)S(1)}, u32[]{:S(2)}, u32[]{:S(2)}) collective-permute-start(bf16[256,512]{1,0:T(8,128)(2,1)S(1)} %shard_map.131.refs_2_), channel_id=1, source_target_pairs={{0,2},{2,0},{4,6},{6,4},{8,10},{10,8},{12,14},{14,12},{1,3},{3,1},... | collective-permute-start | bytes 786440 | tf_op jit(solution)/shard_map/ppermute | solution.py:40
  54.5 0.1 shard_map.136
  54.6 0.1 shard_map.132
  54.7 2.4 %collective-permute-start.11 = (bf16[1,32,1024]{2,1,0:T(8,128)(2,1)S(1)}, bf16[1,32,1024]{2,1,0:T(8,128)(2,1)S(1)}, u32[]{:S(2)}, u32[]{:S(2)}) collective-permute-start(bf16[1,32,1024]{2,1,0:T(8,128)(2,1)S(1)} %get-tuple-element.49), channel_id=1, source_target_pairs={{0,4},{2,6},{4,0},{6,2},{8,12},{10,14},{12,8},{14,10},{1,5},{3,7},... | collective-permute-start | bytes 196616 | tf_op jit(solution)/shard_map/ppermute | solution.py:40
  57.1 3.5 %collective-permute-start.12 = (bf16[1,32,1024]{2,1,0:T(8,128)(2,1)S(1)}, bf16[1,32,1024]{2,1,0:T(8,128)(2,1)S(1)}, u32[]{:S(2)}, u32[]{:S(2)}) collective-permute-start(bf16[1,32,1024]{2,1,0:T(8,128)(2,1)S(1)} %get-tuple-element.50), channel_id=1, source_target_pairs={{0,8},{2,10},{4,12},{6,14},{8,0},{10,2},{12,4},{14,6},{1,9},{3,11}... | collective-permute-start | bytes 196616 | tf_op jit(solution)/shard_map/ppermute | solution.py:40
  60.6 0.0 collective-permute-start.13
  60.7 2.0 %collective-permute-start.16 = (bf16[256,512]{1,0:T(8,128)(2,1)S(1)}, bf16[256,512]{1,0:T(8,128)(2,1)S(1)}, u32[]{:S(2)}, u32[]{:S(2)}) collective-permute-start(bf16[256,512]{1,0:T(8,128)(2,1)S(1)} %shard_map.135), channel_id=1, source_target_pairs={{0,2},{2,0},{4,6},{6,4},{8,10},{10,8},{12,14},{14,12},{1,3},{3,1},... | collective-permute-start | bytes 786440 | tf_op jit(solution)/shard_map/ppermute | solution.py:40
  62.7 1.2 %shard_map.137 = (f32[256,512]{1,0:T(8,128)S(1)}, f32[256,512]{1,0:T(8,128)S(1)}) custom-call(s32[1,4]{1,0:T(1,128)S(1)} %copy-done.7, bf16[256,512]{1,0:T(8,128)(2,1)S(1)} %bitcast.16, bf16[256,512]{1,0:T(8,128)(2,1)S(1)} %bitcast.25, bf16[256,512]{1,0:T(8,128)(2,1)S(1)} %collective-permute-done.7.refs_3_, ...), custom_call_target="tpu_custom_call" | custom-call | flops 1153500 | tf_op jit(solution)/shard_map/pallas_call | solution.py:376
  63.9 1.1 %collective-permute-done.12.refs_2_ = bf16[1,32,1024]{2,1,0:T(8,128)(2,1)S(1)} collective-permute-done((bf16[1,32,1024]{2,1,0:T(8,128)(2,1)S(1)}, bf16[1,32,1024]{2,1,0:T(8,128)(2,1)S(1)}, u32[]{:S(2)}, u32[]{:S(2)}) %collective-permute-start.12) | collective-permute-done | bytes 65568 | tf_op jit(solution)/shard_map/ppermute | solution.py:40
  65.0 1.7 %collective-permute-done.13.refs_3_ = bf16[1,32,1024]{2,1,0:T(8,128)(2,1)S(1)} collective-permute-done((bf16[1,32,1024]{2,1,0:T(8,128)(2,1)S(1)}, bf16[1,32,1024]{2,1,0:T(8,128)(2,1)S(1)}, u32[]{:S(2)}, u32[]{:S(2)}) %collective-permute-start.13) | collective-permute-done | bytes 65568 | tf_op jit(solution)/shard_map/ppermute | solution.py:40
  66.7 0.7 shard_map.133
  67.4 0.1 shard_map.138
  67.5 0.6 collective-permute-done.16.refs_4_
  68.1 1.1 %shard_map.139 = (bf16[256,512]{1,0:T(8,128)(2,1)}, bf16[256,512]{1,0:T(8,128)(2,1)}, bf16[256,512]{1,0:T(8,128)(2,1)}) custom-call(s32[1,4]{1,0:T(1,128)S(1)} %copy-done.7, bf16[256,512]{1,0:T(8,128)(2,1)S(1)} %bitcast.18, bf16[256,512]{1,0:T(8,128)(2,1)S(1)} %bitcast.27, bf16[256,512]{1,0:T(8,128)(2,1)S(1)} %collective-permute-done.14.refs_7_.refs_3_, ...), custom_call_target="tpu_custom_call" | custom-call | flops 1153500 | tf_op jit(solution)/shard_map/pallas_call | solution.py:376
  (28 shorter events, 0.2 us)
Async XLA Ops:
  0.6 11.9 %collective-permute-start = (bf16[256,512]{1,0:T(8,128)(2,1)}, bf16[256,512]{1,0:T(8,128)(2,1)S(1)}, u32[]{:S(2)}, u32[]{:S(2)}) collective-permute-start(bf16[256,512]{1,0:T(8,128)(2,1)} %bitcast.10), channel_id=1, source_target_pairs={{0,4},{2,6},{4,8},{6,10},{8,12},{10,14},{1,5},{3,7},{5,9},{7,11},{... | collective-permute-start | bytes 786440 | tf_op jit(solution)/shard_map/ppermute | solution.py:36
  5.6 11.5 %collective-permute-start.2 = (bf16[256,512]{1,0:T(8,128)(2,1)}, bf16[256,512]{1,0:T(8,128)(2,1)S(1)}, u32[]{:S(2)}, u32[]{:S(2)}) collective-permute-start(bf16[256,512]{1,0:T(8,128)(2,1)} %bitcast.19), channel_id=1, source_target_pairs={{0,4},{2,6},{4,8},{6,10},{8,12},{10,14},{1,5},{3,7},{5,9},{7,11},{... | collective-permute-start | bytes 786440 | tf_op jit(solution)/shard_map/ppermute | solution.py:36
  9.1 9.6 %collective-permute-start.4 = (bf16[256,512]{1,0:T(8,128)(2,1)}, bf16[256,512]{1,0:T(8,128)(2,1)S(1)}, u32[]{:S(2)}, u32[]{:S(2)}) collective-permute-start(bf16[256,512]{1,0:T(8,128)(2,1)} %bitcast.28), channel_id=1, source_target_pairs={{4,0},{6,2},{8,4},{10,6},{12,8},{14,10},{5,1},{7,3},{9,5},{11,7},{... | collective-permute-start | bytes 786440 | tf_op jit(solution)/shard_map/ppermute | solution.py:36
  12.6 0.9 %copy-start = (bf16[1,256,512]{2,1,0:T(8,128)(2,1)S(1)}, bf16[1,256,512]{2,1,0:T(8,128)(2,1)}, u32[]{:S(2)}) copy-start(bf16[1,256,512]{2,1,0:T(8,128)(2,1)} %param.8) | copy-start | bytes 786436
  13.5 3.5 %copy-start.2 = (bf16[1,256,512]{2,1,0:T(8,128)(2,1)S(1)}, bf16[1,256,512]{2,1,0:T(8,128)(2,1)}, u32[]{:S(2)}) copy-start(bf16[1,256,512]{2,1,0:T(8,128)(2,1)} %param.9) | copy-start | bytes 786436
  13.6 7.7 %copy-start.7 = (s32[1,4]{1,0:T(1,128)S(1)}, s32[1,4]{1,0:T(1,128)}, u32[]{:S(2)}) copy-start(s32[1,4]{1,0:T(1,128)} %refs_0_.19) | copy-start | bytes 52
  13.6 7.7 %collective-permute-start.1 = (bf16[256,512]{1,0:T(8,128)(2,1)S(1)}, bf16[256,512]{1,0:T(8,128)(2,1)S(1)}, u32[]{:S(2)}, u32[]{:S(2)}) collective-permute-start(bf16[256,512]{1,0:T(8,128)(2,1)S(1)} %shard_map.118), channel_id=1, source_target_pairs={{0,2},{2,0},{4,6},{6,4},{8,10},{10,8},{12,14},{14,12},{1,3},{3,1},... | collective-permute-start | bytes 786440 | tf_op jit(solution)/shard_map/ppermute | solution.py:40
  17.1 8.5 %collective-permute-start.3 = (bf16[256,512]{1,0:T(8,128)(2,1)S(1)}, bf16[256,512]{1,0:T(8,128)(2,1)S(1)}, u32[]{:S(2)}, u32[]{:S(2)}) collective-permute-start(bf16[256,512]{1,0:T(8,128)(2,1)S(1)} %shard_map.119), channel_id=1, source_target_pairs={{0,2},{2,0},{4,6},{6,4},{8,10},{10,8},{12,14},{14,12},{1,3},{3,1},... | collective-permute-start | bytes 786440 | tf_op jit(solution)/shard_map/ppermute | solution.py:40
  18.7 13.8 %collective-permute-start.5 = (bf16[256,512]{1,0:T(8,128)(2,1)S(1)}, bf16[256,512]{1,0:T(8,128)(2,1)S(1)}, u32[]{:S(2)}, u32[]{:S(2)}) collective-permute-start(bf16[256,512]{1,0:T(8,128)(2,1)S(1)} %collective-permute-done.4.refs_1_.refs_0_.refs_3_), channel_id=1, source_target_pairs={{4,0},{6,2},{8,4},{10,6},{12,8},{14,10},{5,1},{7,3},{9,5},{11,7},{... | collective-permute-start | bytes 786440 | tf_op jit(solution)/shard_map/ppermute | solution.py:36
  21.4 9.2 %copy-start.4 = (bf16[1,256,512]{2,1,0:T(8,128)(2,1)S(1)}, bf16[1,256,512]{2,1,0:T(8,128)(2,1)}, u32[]{:S(2)}) copy-start(bf16[1,256,512]{2,1,0:T(8,128)(2,1)} %param.7) | copy-start | bytes 786436
  25.8 6.7 %copy-start.1 = (bf16[1,256,512]{2,1,0:T(8,128)(2,1)S(1)}, bf16[1,256,512]{2,1,0:T(8,128)(2,1)}, u32[]{:S(2)}) copy-start(bf16[1,256,512]{2,1,0:T(8,128)(2,1)} %param.8) | copy-start | bytes 786436
  25.8 6.7 %copy-start.3 = (bf16[512,1024]{1,0:T(8,128)(2,1)S(1)}, bf16[512,1024]{1,0:T(8,128)(2,1)}, u32[]{:S(2)}) copy-start(bf16[512,1024]{1,0:T(8,128)(2,1)} %refs_1_.1) | copy-start | bytes 3145732
  25.8 6.7 %copy-start.5 = (bf16[1,256,1024]{2,1,0:T(8,128)(2,1)S(1)}, bf16[1,256,1024]{2,1,0:T(8,128)(2,1)}, u32[]{:S(2)}) copy-start(bf16[1,256,1024]{2,1,0:T(8,128)(2,1)} %param.12) | copy-start | bytes 1572868
  25.8 9.0 %collective-permute-start.6 = (bf16[256,512]{1,0:T(8,128)(2,1)S(1)}, bf16[256,512]{1,0:T(8,128)(2,1)S(1)}, u32[]{:S(2)}, u32[]{:S(2)}) collective-permute-start(bf16[256,512]{1,0:T(8,128)(2,1)S(1)} %shard_map.122.refs_2_), channel_id=1, source_target_pairs={{0,4},{2,6},{4,8},{6,10},{8,12},{10,14},{1,5},{3,7},{5,9},{7,11},{... | collective-permute-start | bytes 786440 | tf_op jit(solution)/shard_map/ppermute | solution.py:36
  30.6 6.8 %collective-permute-start.7 = (bf16[256,512]{1,0:T(8,128)(2,1)S(1)}, bf16[256,512]{1,0:T(8,128)(2,1)S(1)}, u32[]{:S(2)}, u32[]{:S(2)}) collective-permute-start(bf16[256,512]{1,0:T(8,128)(2,1)S(1)} %shard_map.125), channel_id=1, source_target_pairs={{0,2},{2,0},{4,6},{6,4},{8,10},{10,8},{12,14},{14,12},{1,3},{3,1},... | collective-permute-start | bytes 786440 | tf_op jit(solution)/shard_map/ppermute | solution.py:40
  32.5 2.4 %copy-start.6 = (bf16[1,256,512]{2,1,0:T(8,128)(2,1)S(1)}, bf16[1,256,512]{2,1,0:T(8,128)(2,1)}, u32[]{:S(2)}) copy-start(bf16[1,256,512]{2,1,0:T(8,128)(2,1)} %param.10) | copy-start | bytes 786436
  35.2 9.5 %collective-permute-start.10 = (bf16[256,512]{1,0:T(8,128)(2,1)S(1)}, bf16[256,512]{1,0:T(8,128)(2,1)S(1)}, u32[]{:S(2)}, u32[]{:S(2)}) collective-permute-start(bf16[256,512]{1,0:T(8,128)(2,1)S(1)} %get-tuple-element.39.refs_2_.refs_4_.refs_1_), channel_id=1, source_target_pairs={{4,0},{6,2},{8,4},{10,6},{12,8},{14,10},{5,1},{7,3},{9,5},{11,7},{... | collective-permute-start | bytes 786440 | tf_op jit(solution)/shard_map/ppermute | solution.py:36
  38.1 2.5 %collective-permute-start.8 = (bf16[8,32,1024]{2,1,0:T(8,128)(2,1)S(1)}, bf16[8,32,1024]{2,1,0:T(8,128)(2,1)S(1)}, u32[]{:S(2)}, u32[]{:S(2)}) collective-permute-start(bf16[8,32,1024]{2,1,0:T(8,128)(2,1)S(1)} %get-tuple-element.41), channel_id=1, source_target_pairs={{0,1},{1,0},{2,3},{3,2},{4,5},{5,4},{6,7},{7,6},{8,9},{9,8},{10,11... | collective-permute-start | bytes 1572872 | tf_op jit(solution)/shard_map/ppermute | solution.py:40
  38.2 16.3 %collective-permute-start.14 = (bf16[256,512]{1,0:T(8,128)(2,1)S(1)}, bf16[256,512]{1,0:T(8,128)(2,1)S(1)}, u32[]{:S(2)}, u32[]{:S(2)}) collective-permute-start(bf16[256,512]{1,0:T(8,128)(2,1)S(1)} %shard_map.134), channel_id=1, source_target_pairs={{0,2},{2,0},{4,6},{6,4},{8,10},{10,8},{12,14},{14,12},{1,3},{3,1},... | collective-permute-start | bytes 786440 | tf_op jit(solution)/shard_map/ppermute | solution.py:40
  40.6 14.0 %collective-permute-start.9 = (bf16[4,32,1024]{2,1,0:T(8,128)(2,1)S(1)}, bf16[4,32,1024]{2,1,0:T(8,128)(2,1)S(1)}, u32[]{:S(2)}, u32[]{:S(2)}) collective-permute-start(bf16[4,32,1024]{2,1,0:T(8,128)(2,1)S(1)} %get-tuple-element.44), channel_id=1, source_target_pairs={{0,2},{2,0},{4,6},{6,4},{8,10},{10,8},{12,14},{14,12},{1,3},{3,1},... | collective-permute-start | bytes 786440 | tf_op jit(solution)/shard_map/ppermute | solution.py:40
  44.7 15.9 %collective-permute-start.15 = (bf16[256,512]{1,0:T(8,128)(2,1)S(1)}, bf16[256,512]{1,0:T(8,128)(2,1)S(1)}, u32[]{:S(2)}, u32[]{:S(2)}) collective-permute-start(bf16[256,512]{1,0:T(8,128)(2,1)S(1)} %collective-permute-done.10.refs_2_.refs_0_.refs_1_.refs_4_), channel_id=1, source_target_pairs={{4,0},{6,2},{8,4},{10,6},{12,8},{14,10},{5,1},{7,3},{9,5},{11,7},{... | collective-permute-start | bytes 786440 | tf_op jit(solution)/shard_map/ppermute | solution.py:36
  46.2 21.1 %collective-permute-start.18 = (bf16[256,512]{1,0:T(8,128)(2,1)S(1)}, bf16[256,512]{1,0:T(8,128)(2,1)S(1)}, u32[]{:S(2)}, u32[]{:S(2)}) collective-permute-start(bf16[256,512]{1,0:T(8,128)(2,1)S(1)} %shard_map.130.refs_2_), channel_id=1, source_target_pairs={{0,4},{2,6},{4,8},{6,10},{8,12},{10,14},{1,5},{3,7},{5,9},{7,11},{... | collective-permute-start | bytes 786440 | tf_op jit(solution)/shard_map/ppermute | solution.py:36
  53.4 7.3 %collective-permute-start.17 = (bf16[256,512]{1,0:T(8,128)(2,1)S(1)}, bf16[256,512]{1,0:T(8,128)(2,1)S(1)}, u32[]{:S(2)}, u32[]{:S(2)}) collective-permute-start(bf16[256,512]{1,0:T(8,128)(2,1)S(1)} %shard_map.131.refs_2_), channel_id=1, source_target_pairs={{0,2},{2,0},{4,6},{6,4},{8,10},{10,8},{12,14},{14,12},{1,3},{3,1},... | collective-permute-start | bytes 786440 | tf_op jit(solution)/shard_map/ppermute | solution.py:40
  54.7 9.2 %collective-permute-start.11 = (bf16[1,32,1024]{2,1,0:T(8,128)(2,1)S(1)}, bf16[1,32,1024]{2,1,0:T(8,128)(2,1)S(1)}, u32[]{:S(2)}, u32[]{:S(2)}) collective-permute-start(bf16[1,32,1024]{2,1,0:T(8,128)(2,1)S(1)} %get-tuple-element.49), channel_id=1, source_target_pairs={{0,4},{2,6},{4,0},{6,2},{8,12},{10,14},{12,8},{14,10},{1,5},{3,7},... | collective-permute-start | bytes 196616 | tf_op jit(solution)/shard_map/ppermute | solution.py:40
  57.1 7.9 %collective-permute-start.12 = (bf16[1,32,1024]{2,1,0:T(8,128)(2,1)S(1)}, bf16[1,32,1024]{2,1,0:T(8,128)(2,1)S(1)}, u32[]{:S(2)}, u32[]{:S(2)}) collective-permute-start(bf16[1,32,1024]{2,1,0:T(8,128)(2,1)S(1)} %get-tuple-element.50), channel_id=1, source_target_pairs={{0,8},{2,10},{4,12},{6,14},{8,0},{10,2},{12,4},{14,6},{1,9},{3,11}... | collective-permute-start | bytes 196616 | tf_op jit(solution)/shard_map/ppermute | solution.py:40
  60.6 6.1 %collective-permute-start.13 = (bf16[1,32,1024]{2,1,0:T(8,128)(2,1)S(1)}, bf16[1,32,1024]{2,1,0:T(8,128)(2,1)S(1)}, u32[]{:S(2)}, u32[]{:S(2)}) collective-permute-start(bf16[1,32,1024]{2,1,0:T(8,128)(2,1)S(1)} %get-tuple-element.51), channel_id=1, source_target_pairs={{0,12},{2,14},{4,8},{6,10},{8,4},{10,6},{12,0},{14,2},{1,13},{3,15... | collective-permute-start | bytes 196616 | tf_op jit(solution)/shard_map/ppermute | solution.py:40
  60.7 7.4 %collective-permute-start.16 = (bf16[256,512]{1,0:T(8,128)(2,1)S(1)}, bf16[256,512]{1,0:T(8,128)(2,1)S(1)}, u32[]{:S(2)}, u32[]{:S(2)}) collective-permute-start(bf16[256,512]{1,0:T(8,128)(2,1)S(1)} %shard_map.135), channel_id=1, source_target_pairs={{0,2},{2,0},{4,6},{6,4},{8,10},{10,8},{12,14},{14,12},{1,3},{3,1},... | collective-permute-start | bytes 786440 | tf_op jit(solution)/shard_map/ppermute | solution.py:40

commit v5 on v4

--- a/solution.py
+++ b/solution.py
@@ -228,11 +228,30 @@
 
         staggered(width, begin, finish)
 
+    def own(k_ref, v_ref, start, end):
+        shape = (end - start, end)
+        rows = place + start + lax.broadcasted_iota(jnp.int32, shape, 0)
+        columns = place + lax.broadcasted_iota(jnp.int32, shape, 1)
+        ids = place + start + lax.broadcasted_iota(jnp.int32, (end - start, 1), 0)
+        live = (columns <= rows) & (columns >= first_place(ends, ids))
+
+        def begin(cols):
+            half = half_scores(q_ref[start:end, cols], k_ref[:end, cols])
+            return half, dot(grad_ref[start:end, cols], v_ref[:end, cols], 1, 1)
+
+        def finish(cols, begun):
+            half, pull = begun
+            score_grad = jnp.where(live, pull * slopes(half)[1], 0.0).astype(BF16)
+            total_ref[start:end, cols] = dot(score_grad, k_ref[:end, cols], 1, 0)
+
+        staggered(width, begin, finish)
+
     if distances[0] > 0:
         total_ref[...] = jnp.zeros_like(total_ref)
     for n, distance in enumerate(distances):
         if distance == 0:
-            pair(k_refs[n], v_refs[n], own_mask(ends, place, tok, False), None, None)
+            for start, end in ((0, tok // 2), (tok // 2, tok)):
+                own(k_refs[n], v_refs[n], start, end)
         else:
             dead, alive = crossing(ends, place, distance, tok)
             pl.when(dead < tok)(functools.partial(pair, k_refs[n], v_refs[n], None, dead, alive))

time: 70.5 us -> 70.4 us (level)
  starting transfers between devices: 43.7 us -> 42 us
  Pallas kernels: 9.11 us -> 10.2 us
    ppermute x8, starting transfers between devices: 25.5 us -> 23.7 us  [shifted(): lax.ppermute(block, 'ctx', [(i, i + distance) for i in devices if i + dis...]
    pallas_call x22, Pallas kernels: 9.11 us -> 10.2 us  [call(): pl.pallas_call(body, out_shape=shapes, in_specs=[VMEM] * len(args) + [ANY...]
  transfers between devices with their start and end apart: 19 -> 19, of which waited for: 8 -> 8; matrix products, arithmetic and copies ran while one was open for 0% -> 0% of each run, Pallas kernels for 12% -> 13%
where the time goes in v5:
time: 70.4 us; the launch traced here: 69.1 us
  starting transfers between devices  42 us (60%)
  waiting for transfers between devices  15 us (21%)
  Pallas kernels  10.2 us (14%)
  local copies, waits for them, and re-layouts  0.99 us (1%)
  between operations  0.95 us (1%)
    ppermute x8, starting transfers between devices, shifted(): lax.ppermute(block, 'ctx', [(i, i + distance) for i in devices if i + dis...  23.7 us
    ppermute x11, starting transfers between devices, swapped(): lax.ppermute(block, axis, [(i, i ^ step) for i in range(lax.axis_size(axi...  18.3 us
    pallas_call x22, Pallas kernels, call(): pl.pallas_call(body, out_shape=shapes, in_specs=[VMEM] * len(args) + [ANY...  10.2 us
    ppermute x11, waiting for transfers between devices, swapped(): lax.ppermute(block, axis, [(i, i ^ step) for i in range(lax.axis_size(axi...  8.88 us
    ppermute x8, waiting for transfers between devices, shifted(): lax.ppermute(block, 'ctx', [(i, i + distance) for i in devices if i + dis...  6.09 us
  transfers between devices with their start and end apart: 19, of which 8 were waited for; matrix products, arithmetic and copies ran while one was open for 0% of the time, Pallas kernels for 13%

profile of v5, /device:TPU:0, one launch (start us, length us, event | category | flops | bytes accessed | tf_op | source)
XLA Modules:
  0.0 69.1 jit_solution(16514731986390380354)
XLA Ops:
  0.6 4.9 %collective-permute-start = (bf16[256,512]{1,0:T(8,128)(2,1)}, bf16[256,512]{1,0:T(8,128)(2,1)S(1)}, u32[]{:S(2)}, u32[]{:S(2)}) collective-permute-start(bf16[256,512]{1,0:T(8,128)(2,1)} %bitcast.10), channel_id=1, source_target_pairs={{0,4},{2,6},{4,8},{6,10},{8,12},{10,14},{1,5},{3,7},{5,9},{7,11},{... | collective-permute-start | bytes 786440 | tf_op jit(solution)/shard_map/ppermute | solution.py:36
  5.6 3.5 %collective-permute-start.2 = (bf16[256,512]{1,0:T(8,128)(2,1)}, bf16[256,512]{1,0:T(8,128)(2,1)S(1)}, u32[]{:S(2)}, u32[]{:S(2)}) collective-permute-start(bf16[256,512]{1,0:T(8,128)(2,1)} %bitcast.19), channel_id=1, source_target_pairs={{0,4},{2,6},{4,8},{6,10},{8,12},{10,14},{1,5},{3,7},{5,9},{7,11},{... | collective-permute-start | bytes 786440 | tf_op jit(solution)/shard_map/ppermute | solution.py:36
  9.1 1.3 %collective-permute-start.4 = (bf16[256,512]{1,0:T(8,128)(2,1)}, bf16[256,512]{1,0:T(8,128)(2,1)S(1)}, u32[]{:S(2)}, u32[]{:S(2)}) collective-permute-start(bf16[256,512]{1,0:T(8,128)(2,1)} %bitcast.28), channel_id=1, source_target_pairs={{4,0},{6,2},{8,4},{10,6},{12,8},{14,10},{5,1},{7,3},{9,5},{11,7},{... | collective-permute-start | bytes 786440 | tf_op jit(solution)/shard_map/ppermute | solution.py:36
  10.4 2.2 %collective-permute-done.odd_ref.refs_4_.refs_3_.refs_5_ = bf16[256,512]{1,0:T(8,128)(2,1)S(1)} collective-permute-done((bf16[256,512]{1,0:T(8,128)(2,1)}, bf16[256,512]{1,0:T(8,128)(2,1)S(1)}, u32[]{:S(2)}, u32[]{:S(2)}) %collective-permute-start) | collective-permute-done | bytes 262176 | tf_op jit(solution)/shard_map/ppermute | solution.py:36
  12.6 0.9 %copy-done = bf16[1,256,512]{2,1,0:T(8,128)(2,1)S(1)} copy-done((bf16[1,256,512]{2,1,0:T(8,128)(2,1)S(1)}, bf16[1,256,512]{2,1,0:T(8,128)(2,1)}, u32[]{:S(2)}) %copy-start) | copy-done | bytes 262168
  13.6 0.0 copy-start.7
  13.6 1.6 %collective-permute-start.1 = (bf16[256,512]{1,0:T(8,128)(2,1)S(1)}, bf16[256,512]{1,0:T(8,128)(2,1)S(1)}, u32[]{:S(2)}, u32[]{:S(2)}) collective-permute-start(bf16[256,512]{1,0:T(8,128)(2,1)S(1)} %shard_map.118), channel_id=1, source_target_pairs={{0,2},{2,0},{4,6},{6,4},{8,10},{10,8},{12,14},{14,12},{1,3},{3,1},... | collective-permute-start | bytes 786440 | tf_op jit(solution)/shard_map/ppermute | solution.py:40
  15.2 1.9 %collective-permute-done.2.odd_ref.refs_7_.refs_3_.refs_8_.refs_6_ = bf16[256,512]{1,0:T(8,128)(2,1)S(1)} collective-permute-done((bf16[256,512]{1,0:T(8,128)(2,1)}, bf16[256,512]{1,0:T(8,128)(2,1)S(1)}, u32[]{:S(2)}, u32[]{:S(2)}) %collective-permute-start.2) | collective-permute-done | bytes 262176 | tf_op jit(solution)/shard_map/ppermute | solution.py:36
  17.1 1.6 %collective-permute-start.3 = (bf16[256,512]{1,0:T(8,128)(2,1)S(1)}, bf16[256,512]{1,0:T(8,128)(2,1)S(1)}, u32[]{:S(2)}, u32[]{:S(2)}) collective-permute-start(bf16[256,512]{1,0:T(8,128)(2,1)S(1)} %shard_map.119), channel_id=1, source_target_pairs={{0,2},{2,0},{4,6},{6,4},{8,10},{10,8},{12,14},{14,12},{1,3},{3,1},... | collective-permute-start | bytes 786440 | tf_op jit(solution)/shard_map/ppermute | solution.py:40
  18.7 1.3 %collective-permute-start.5 = (bf16[256,512]{1,0:T(8,128)(2,1)S(1)}, bf16[256,512]{1,0:T(8,128)(2,1)S(1)}, u32[]{:S(2)}, u32[]{:S(2)}) collective-permute-start(bf16[256,512]{1,0:T(8,128)(2,1)S(1)} %collective-permute-done.4.refs_1_.refs_0_.refs_3_), channel_id=1, source_target_pairs={{4,0},{6,2},{8,4},{10,6},{12,8},{14,10},{5,1},{7,3},{9,5},{11,7},{... | collective-permute-start | bytes 786440 | tf_op jit(solution)/shard_map/ppermute | solution.py:36
  20.0 1.3 %collective-permute-done.1.refs_3_.refs_2_.refs_4_ = bf16[256,512]{1,0:T(8,128)(2,1)S(1)} collective-permute-done((bf16[256,512]{1,0:T(8,128)(2,1)S(1)}, bf16[256,512]{1,0:T(8,128)(2,1)S(1)}, u32[]{:S(2)}, u32[]{:S(2)}) %collective-permute-start.1) | collective-permute-done | bytes 262176 | tf_op jit(solution)/shard_map/ppermute | solution.py:40
  21.3 0.1 shard_map.121.refs_1_
  21.4 0.0 copy-start.4
  21.4 4.2 %collective-permute-done.3.refs_6_.refs_2_.refs_7_.refs_5_ = bf16[256,512]{1,0:T(8,128)(2,1)S(1)} collective-permute-done((bf16[256,512]{1,0:T(8,128)(2,1)S(1)}, bf16[256,512]{1,0:T(8,128)(2,1)S(1)}, u32[]{:S(2)}, u32[]{:S(2)}) %collective-permute-start.3) | collective-permute-done | bytes 262176 | tf_op jit(solution)/shard_map/ppermute | solution.py:40
  25.6 0.1 shard_map.122.refs_2_
  25.8 0.0 copy-start.1
  25.8 0.0 copy-start.5
  25.8 4.4 %collective-permute-start.6 = (bf16[256,512]{1,0:T(8,128)(2,1)S(1)}, bf16[256,512]{1,0:T(8,128)(2,1)S(1)}, u32[]{:S(2)}, u32[]{:S(2)}) collective-permute-start(bf16[256,512]{1,0:T(8,128)(2,1)S(1)} %shard_map.122.refs_2_), channel_id=1, source_target_pairs={{0,4},{2,6},{4,8},{6,10},{8,12},{10,14},{1,5},{3,7},{5,9},{7,11},{... | collective-permute-start | bytes 786440 | tf_op jit(solution)/shard_map/ppermute | solution.py:36
  30.3 1.6 %collective-permute-start.7 = (bf16[256,512]{1,0:T(8,128)(2,1)S(1)}, bf16[256,512]{1,0:T(8,128)(2,1)S(1)}, u32[]{:S(2)}, u32[]{:S(2)}) collective-permute-start(bf16[256,512]{1,0:T(8,128)(2,1)S(1)} %shard_map.125), channel_id=1, source_target_pairs={{0,2},{2,0},{4,6},{6,4},{8,10},{10,8},{12,14},{14,12},{1,3},{3,1},... | collective-permute-start | bytes 786440 | tf_op jit(solution)/shard_map/ppermute | solution.py:40
  31.9 0.0 copy-start.6
  31.9 0.9 %shard_map.120 = (f32[256,512]{1,0:T(8,128)S(1)}, f32[256,512]{1,0:T(8,128)S(1)}) custom-call(s32[1,4]{1,0:T(1,128)S(1)} %copy-done.7, bf16[256,512]{1,0:T(8,128)(2,1)S(1)} %bitcast.30, bf16[256,512]{1,0:T(8,128)(2,1)S(1)} %bitcast.12, bf16[256,512]{1,0:T(8,128)(2,1)S(1)} %collective-permute-done.1.refs_3_.refs_2_.refs_4_, ...), custom_call_target="tpu_custom_call" | custom-call | flops 1153500 | tf_op jit(solution)/shard_map/pallas_call | solution.py:395
  32.8 2.0 %collective-permute-done.6.refs_1_ = bf16[256,512]{1,0:T(8,128)(2,1)S(1)} collective-permute-done((bf16[256,512]{1,0:T(8,128)(2,1)S(1)}, bf16[256,512]{1,0:T(8,128)(2,1)S(1)}, u32[]{:S(2)}, u32[]{:S(2)}) %collective-permute-start.6) | collective-permute-done | bytes 262176 | tf_op jit(solution)/shard_map/ppermute | solution.py:36
  34.8 0.4 shard_map.123
  35.2 1.3 %collective-permute-start.10 = (bf16[256,512]{1,0:T(8,128)(2,1)S(1)}, bf16[256,512]{1,0:T(8,128)(2,1)S(1)}, u32[]{:S(2)}, u32[]{:S(2)}) collective-permute-start(bf16[256,512]{1,0:T(8,128)(2,1)S(1)} %get-tuple-element.39.refs_2_.refs_4_.refs_1_), channel_id=1, source_target_pairs={{4,0},{6,2},{8,4},{10,6},{12,8},{14,10},{5,1},{7,3},{9,5},{11,7},{... | collective-permute-start | bytes 786440 | tf_op jit(solution)/shard_map/ppermute | solution.py:36
  36.5 1.0 %shard_map.124.refs_2_.refs_7_ = f32[256,512]{1,0:T(8,128)S(1)} custom-call(s32[1,4]{1,0:T(1,128)S(1)} %copy-done.7, bf16[256,512]{1,0:T(8,128)(2,1)S(1)} %bitcast.31, bf16[256,512]{1,0:T(8,128)(2,1)S(1)} %get-tuple-element.39.refs_2_.refs_4_.refs_1_, bf16[256,512]{1,0:T(8,128)(2,1)S(1)} %bitcast.13, ...), custom_call_target="tpu_custom_call" | custom-call | flops 1153500 | tf_op jit(solution)/shard_map/pallas_call | solution.py:395
  37.6 0.7 shard_map.126
  38.2 0.1 collective-permute-start.8
  38.3 2.4 %collective-permute-start.14 = (bf16[256,512]{1,0:T(8,128)(2,1)S(1)}, bf16[256,512]{1,0:T(8,128)(2,1)S(1)}, u32[]{:S(2)}, u32[]{:S(2)}) collective-permute-start(bf16[256,512]{1,0:T(8,128)(2,1)S(1)} %shard_map.134), channel_id=1, source_target_pairs={{0,2},{2,0},{4,6},{6,4},{8,10},{10,8},{12,14},{14,12},{1,3},{3,1},... | collective-permute-start | bytes 786440 | tf_op jit(solution)/shard_map/ppermute | solution.py:40
  40.7 0.1 shard_map.127
  40.8 1.8 %collective-permute-start.9 = (bf16[4,32,1024]{2,1,0:T(8,128)(2,1)S(1)}, bf16[4,32,1024]{2,1,0:T(8,128)(2,1)S(1)}, u32[]{:S(2)}, u32[]{:S(2)}) collective-permute-start(bf16[4,32,1024]{2,1,0:T(8,128)(2,1)S(1)} %get-tuple-element.44), channel_id=1, source_target_pairs={{0,2},{2,0},{4,6},{6,4},{8,10},{10,8},{12,14},{14,12},{1,3},{3,1},... | collective-permute-start | bytes 786440 | tf_op jit(solution)/shard_map/ppermute | solution.py:40
  42.7 0.9 %shard_map.129 = (f32[256,512]{1,0:T(8,128)S(1)}, f32[256,512]{1,0:T(8,128)S(1)}) custom-call(s32[1,4]{1,0:T(1,128)S(1)} %copy-done.7, bf16[256,512]{1,0:T(8,128)(2,1)S(1)} %bitcast.14, bf16[256,512]{1,0:T(8,128)(2,1)S(1)} %bitcast.23, bf16[256,512]{1,0:T(8,128)(2,1)S(1)} %bitcast.32, bf16[256,512]{1,0:T(8,128)(2,1)S(1)} %get-tuple-element.39.refs_2_.refs_4_.refs_1_, ...), custom_call_target="tpu_custom_call" | custom-call | flops 1153500 | tf_op jit(solution)/shard_map/pallas_call | solution.py:395
  43.6 1.3 %shard_map.128 = (bf16[256,1024]{1,0:T(8,128)(2,1)}, bf16[256,512]{1,0:T(8,128)(2,1)}) custom-call(bf16[256,512]{1,0:T(8,128)(2,1)S(1)} %get-tuple-element.37.refs_0_, bf16[512,1024]{1,0:T(8,128)(2,1)S(1)} %copy-done.3, f32[256,512]{1,0:T(8,128)S(1)} %get-tuple-element.36.refs_2_, f32[256,512]{1,0:T(8,128)S(1)} %get-tuple-element.38.refs_3_, ...), custom_call_target="tpu_custom_call" | custom-call | flops 1153500 | tf_op jit(solution)/shard_map/pallas_call | solution.py:395
  44.9 1.3 %collective-permute-start.15 = (bf16[256,512]{1,0:T(8,128)(2,1)S(1)}, bf16[256,512]{1,0:T(8,128)(2,1)S(1)}, u32[]{:S(2)}, u32[]{:S(2)}) collective-permute-start(bf16[256,512]{1,0:T(8,128)(2,1)S(1)} %collective-permute-done.10.refs_2_.refs_0_.refs_1_.refs_4_), channel_id=1, source_target_pairs={{4,0},{6,2},{8,4},{10,6},{12,8},{14,10},{5,1},{7,3},{9,5},{11,7},{... | collective-permute-start | bytes 786440 | tf_op jit(solution)/shard_map/ppermute | solution.py:36
  46.2 0.2 shard_map.130.refs_2_
  46.4 5.7 %collective-permute-start.18 = (bf16[256,512]{1,0:T(8,128)(2,1)S(1)}, bf16[256,512]{1,0:T(8,128)(2,1)S(1)}, u32[]{:S(2)}, u32[]{:S(2)}) collective-permute-start(bf16[256,512]{1,0:T(8,128)(2,1)S(1)} %shard_map.130.refs_2_), channel_id=1, source_target_pairs={{0,4},{2,6},{4,8},{6,10},{8,12},{10,14},{1,5},{3,7},{5,9},{7,11},{... | collective-permute-start | bytes 786440 | tf_op jit(solution)/shard_map/ppermute | solution.py:36
  52.1 1.3 %collective-permute-start.17 = (bf16[256,512]{1,0:T(8,128)(2,1)S(1)}, bf16[256,512]{1,0:T(8,128)(2,1)S(1)}, u32[]{:S(2)}, u32[]{:S(2)}) collective-permute-start(bf16[256,512]{1,0:T(8,128)(2,1)S(1)} %shard_map.131.refs_2_), channel_id=1, source_target_pairs={{0,2},{2,0},{4,6},{6,4},{8,10},{10,8},{12,14},{14,12},{1,3},{3,1},... | collective-permute-start | bytes 786440 | tf_op jit(solution)/shard_map/ppermute | solution.py:40
  53.4 1.0 %shard_map.136 = (f32[256,512]{1,0:T(8,128)S(1)}, f32[256,512]{1,0:T(8,128)S(1)}) custom-call(s32[1,4]{1,0:T(1,128)S(1)} %copy-done.7, bf16[256,512]{1,0:T(8,128)(2,1)S(1)} %bitcast.15, bf16[256,512]{1,0:T(8,128)(2,1)S(1)} %bitcast.24, bf16[256,512]{1,0:T(8,128)(2,1)S(1)} %collective-permute-done.4.refs_1_.refs_0_.refs_3_, ...), custom_call_target="tpu_custom_call" | custom-call | flops 1153500 | tf_op jit(solution)/shard_map/pallas_call | solution.py:395
  54.5 0.1 shard_map.132
  54.6 3.3 %collective-permute-start.11 = (bf16[1,32,1024]{2,1,0:T(8,128)(2,1)S(1)}, bf16[1,32,1024]{2,1,0:T(8,128)(2,1)S(1)}, u32[]{:S(2)}, u32[]{:S(2)}) collective-permute-start(bf16[1,32,1024]{2,1,0:T(8,128)(2,1)S(1)} %get-tuple-element.49), channel_id=1, source_target_pairs={{0,4},{2,6},{4,0},{6,2},{8,12},{10,14},{12,8},{14,10},{1,5},{3,7},... | collective-permute-start | bytes 196616 | tf_op jit(solution)/shard_map/ppermute | solution.py:40
  57.9 3.0 %collective-permute-start.12 = (bf16[1,32,1024]{2,1,0:T(8,128)(2,1)S(1)}, bf16[1,32,1024]{2,1,0:T(8,128)(2,1)S(1)}, u32[]{:S(2)}, u32[]{:S(2)}) collective-permute-start(bf16[1,32,1024]{2,1,0:T(8,128)(2,1)S(1)} %get-tuple-element.50), channel_id=1, source_target_pairs={{0,8},{2,10},{4,12},{6,14},{8,0},{10,2},{12,4},{14,6},{1,9},{3,11}... | collective-permute-start | bytes 196616 | tf_op jit(solution)/shard_map/ppermute | solution.py:40
  61.0 1.6 %collective-permute-start.16 = (bf16[256,512]{1,0:T(8,128)(2,1)S(1)}, bf16[256,512]{1,0:T(8,128)(2,1)S(1)}, u32[]{:S(2)}, u32[]{:S(2)}) collective-permute-start(bf16[256,512]{1,0:T(8,128)(2,1)S(1)} %shard_map.135), channel_id=1, source_target_pairs={{0,2},{2,0},{4,6},{6,4},{8,10},{10,8},{12,14},{14,12},{1,3},{3,1},... | collective-permute-start | bytes 786440 | tf_op jit(solution)/shard_map/ppermute | solution.py:40
  62.6 1.2 %shard_map.137 = (f32[256,512]{1,0:T(8,128)S(1)}, f32[256,512]{1,0:T(8,128)S(1)}) custom-call(s32[1,4]{1,0:T(1,128)S(1)} %copy-done.7, bf16[256,512]{1,0:T(8,128)(2,1)S(1)} %bitcast.16, bf16[256,512]{1,0:T(8,128)(2,1)S(1)} %bitcast.25, bf16[256,512]{1,0:T(8,128)(2,1)S(1)} %collective-permute-done.7.refs_3_, ...), custom_call_target="tpu_custom_call" | custom-call | flops 1153500 | tf_op jit(solution)/shard_map/pallas_call | solution.py:395
  63.8 1.2 %collective-permute-done.12.refs_2_ = bf16[1,32,1024]{2,1,0:T(8,128)(2,1)S(1)} collective-permute-done((bf16[1,32,1024]{2,1,0:T(8,128)(2,1)S(1)}, bf16[1,32,1024]{2,1,0:T(8,128)(2,1)S(1)}, u32[]{:S(2)}, u32[]{:S(2)}) %collective-permute-start.12) | collective-permute-done | bytes 65568 | tf_op jit(solution)/shard_map/ppermute | solution.py:40
  65.0 2.0 %collective-permute-done.13.refs_3_ = bf16[1,32,1024]{2,1,0:T(8,128)(2,1)S(1)} collective-permute-done((bf16[1,32,1024]{2,1,0:T(8,128)(2,1)S(1)}, bf16[1,32,1024]{2,1,0:T(8,128)(2,1)S(1)}, u32[]{:S(2)}, u32[]{:S(2)}) %collective-permute-start.13) | collective-permute-done | bytes 65568 | tf_op jit(solution)/shard_map/ppermute | solution.py:40
  67.0 0.7 shard_map.133
  67.7 0.1 shard_map.138
  67.8 0.1 collective-permute-done.16.refs_4_
  68.0 1.1 %shard_map.139 = (bf16[256,512]{1,0:T(8,128)(2,1)}, bf16[256,512]{1,0:T(8,128)(2,1)}, bf16[256,512]{1,0:T(8,128)(2,1)}) custom-call(s32[1,4]{1,0:T(1,128)S(1)} %copy-done.7, bf16[256,512]{1,0:T(8,128)(2,1)S(1)} %bitcast.18, bf16[256,512]{1,0:T(8,128)(2,1)S(1)} %bitcast.27, bf16[256,512]{1,0:T(8,128)(2,1)S(1)} %collective-permute-done.14.refs_7_.refs_3_, ...), custom_call_target="tpu_custom_call" | custom-call | flops 1153500 | tf_op jit(solution)/shard_map/pallas_call | solution.py:395
  (28 shorter events, 0.2 us)
Async XLA Ops:
  0.6 11.9 %collective-permute-start = (bf16[256,512]{1,0:T(8,128)(2,1)}, bf16[256,512]{1,0:T(8,128)(2,1)S(1)}, u32[]{:S(2)}, u32[]{:S(2)}) collective-permute-start(bf16[256,512]{1,0:T(8,128)(2,1)} %bitcast.10), channel_id=1, source_target_pairs={{0,4},{2,6},{4,8},{6,10},{8,12},{10,14},{1,5},{3,7},{5,9},{7,11},{... | collective-permute-start | bytes 786440 | tf_op jit(solution)/shard_map/ppermute | solution.py:36
  5.6 11.5 %collective-permute-start.2 = (bf16[256,512]{1,0:T(8,128)(2,1)}, bf16[256,512]{1,0:T(8,128)(2,1)S(1)}, u32[]{:S(2)}, u32[]{:S(2)}) collective-permute-start(bf16[256,512]{1,0:T(8,128)(2,1)} %bitcast.19), channel_id=1, source_target_pairs={{0,4},{2,6},{4,8},{6,10},{8,12},{10,14},{1,5},{3,7},{5,9},{7,11},{... | collective-permute-start | bytes 786440 | tf_op jit(solution)/shard_map/ppermute | solution.py:36
  9.1 9.6 %collective-permute-start.4 = (bf16[256,512]{1,0:T(8,128)(2,1)}, bf16[256,512]{1,0:T(8,128)(2,1)S(1)}, u32[]{:S(2)}, u32[]{:S(2)}) collective-permute-start(bf16[256,512]{1,0:T(8,128)(2,1)} %bitcast.28), channel_id=1, source_target_pairs={{4,0},{6,2},{8,4},{10,6},{12,8},{14,10},{5,1},{7,3},{9,5},{11,7},{... | collective-permute-start | bytes 786440 | tf_op jit(solution)/shard_map/ppermute | solution.py:36
  12.6 0.9 %copy-start = (bf16[1,256,512]{2,1,0:T(8,128)(2,1)S(1)}, bf16[1,256,512]{2,1,0:T(8,128)(2,1)}, u32[]{:S(2)}) copy-start(bf16[1,256,512]{2,1,0:T(8,128)(2,1)} %param.8) | copy-start | bytes 786436
  13.5 3.5 %copy-start.2 = (bf16[1,256,512]{2,1,0:T(8,128)(2,1)S(1)}, bf16[1,256,512]{2,1,0:T(8,128)(2,1)}, u32[]{:S(2)}) copy-start(bf16[1,256,512]{2,1,0:T(8,128)(2,1)} %param.9) | copy-start | bytes 786436
  13.6 7.7 %copy-start.7 = (s32[1,4]{1,0:T(1,128)S(1)}, s32[1,4]{1,0:T(1,128)}, u32[]{:S(2)}) copy-start(s32[1,4]{1,0:T(1,128)} %refs_0_.19) | copy-start | bytes 52
  13.6 7.7 %collective-permute-start.1 = (bf16[256,512]{1,0:T(8,128)(2,1)S(1)}, bf16[256,512]{1,0:T(8,128)(2,1)S(1)}, u32[]{:S(2)}, u32[]{:S(2)}) collective-permute-start(bf16[256,512]{1,0:T(8,128)(2,1)S(1)} %shard_map.118), channel_id=1, source_target_pairs={{0,2},{2,0},{4,6},{6,4},{8,10},{10,8},{12,14},{14,12},{1,3},{3,1},... | collective-permute-start | bytes 786440 | tf_op jit(solution)/shard_map/ppermute | solution.py:40
  17.1 8.5 %collective-permute-start.3 = (bf16[256,512]{1,0:T(8,128)(2,1)S(1)}, bf16[256,512]{1,0:T(8,128)(2,1)S(1)}, u32[]{:S(2)}, u32[]{:S(2)}) collective-permute-start(bf16[256,512]{1,0:T(8,128)(2,1)S(1)} %shard_map.119), channel_id=1, source_target_pairs={{0,2},{2,0},{4,6},{6,4},{8,10},{10,8},{12,14},{14,12},{1,3},{3,1},... | collective-permute-start | bytes 786440 | tf_op jit(solution)/shard_map/ppermute | solution.py:40
  18.7 13.2 %collective-permute-start.5 = (bf16[256,512]{1,0:T(8,128)(2,1)S(1)}, bf16[256,512]{1,0:T(8,128)(2,1)S(1)}, u32[]{:S(2)}, u32[]{:S(2)}) collective-permute-start(bf16[256,512]{1,0:T(8,128)(2,1)S(1)} %collective-permute-done.4.refs_1_.refs_0_.refs_3_), channel_id=1, source_target_pairs={{4,0},{6,2},{8,4},{10,6},{12,8},{14,10},{5,1},{7,3},{9,5},{11,7},{... | collective-permute-start | bytes 786440 | tf_op jit(solution)/shard_map/ppermute | solution.py:36
  21.4 8.9 %copy-start.4 = (bf16[1,256,512]{2,1,0:T(8,128)(2,1)S(1)}, bf16[1,256,512]{2,1,0:T(8,128)(2,1)}, u32[]{:S(2)}) copy-start(bf16[1,256,512]{2,1,0:T(8,128)(2,1)} %param.7) | copy-start | bytes 786436
  25.8 6.1 %copy-start.1 = (bf16[1,256,512]{2,1,0:T(8,128)(2,1)S(1)}, bf16[1,256,512]{2,1,0:T(8,128)(2,1)}, u32[]{:S(2)}) copy-start(bf16[1,256,512]{2,1,0:T(8,128)(2,1)} %param.8) | copy-start | bytes 786436
  25.8 6.1 %copy-start.3 = (bf16[512,1024]{1,0:T(8,128)(2,1)S(1)}, bf16[512,1024]{1,0:T(8,128)(2,1)}, u32[]{:S(2)}) copy-start(bf16[512,1024]{1,0:T(8,128)(2,1)} %refs_1_.1) | copy-start | bytes 3145732
  25.8 6.1 %copy-start.5 = (bf16[1,256,1024]{2,1,0:T(8,128)(2,1)S(1)}, bf16[1,256,1024]{2,1,0:T(8,128)(2,1)}, u32[]{:S(2)}) copy-start(bf16[1,256,1024]{2,1,0:T(8,128)(2,1)} %param.12) | copy-start | bytes 1572868
  25.8 9.0 %collective-permute-start.6 = (bf16[256,512]{1,0:T(8,128)(2,1)S(1)}, bf16[256,512]{1,0:T(8,128)(2,1)S(1)}, u32[]{:S(2)}, u32[]{:S(2)}) collective-permute-start(bf16[256,512]{1,0:T(8,128)(2,1)S(1)} %shard_map.122.refs_2_), channel_id=1, source_target_pairs={{0,4},{2,6},{4,8},{6,10},{8,12},{10,14},{1,5},{3,7},{5,9},{7,11},{... | collective-permute-start | bytes 786440 | tf_op jit(solution)/shard_map/ppermute | solution.py:36
  30.3 7.2 %collective-permute-start.7 = (bf16[256,512]{1,0:T(8,128)(2,1)S(1)}, bf16[256,512]{1,0:T(8,128)(2,1)S(1)}, u32[]{:S(2)}, u32[]{:S(2)}) collective-permute-start(bf16[256,512]{1,0:T(8,128)(2,1)S(1)} %shard_map.125), channel_id=1, source_target_pairs={{0,2},{2,0},{4,6},{6,4},{8,10},{10,8},{12,14},{14,12},{1,3},{3,1},... | collective-permute-start | bytes 786440 | tf_op jit(solution)/shard_map/ppermute | solution.py:40
  31.9 2.9 %copy-start.6 = (bf16[1,256,512]{2,1,0:T(8,128)(2,1)S(1)}, bf16[1,256,512]{2,1,0:T(8,128)(2,1)}, u32[]{:S(2)}) copy-start(bf16[1,256,512]{2,1,0:T(8,128)(2,1)} %param.10) | copy-start | bytes 786436
  35.2 9.7 %collective-permute-start.10 = (bf16[256,512]{1,0:T(8,128)(2,1)S(1)}, bf16[256,512]{1,0:T(8,128)(2,1)S(1)}, u32[]{:S(2)}, u32[]{:S(2)}) collective-permute-start(bf16[256,512]{1,0:T(8,128)(2,1)S(1)} %get-tuple-element.39.refs_2_.refs_4_.refs_1_), channel_id=1, source_target_pairs={{4,0},{6,2},{8,4},{10,6},{12,8},{14,10},{5,1},{7,3},{9,5},{11,7},{... | collective-permute-start | bytes 786440 | tf_op jit(solution)/shard_map/ppermute | solution.py:36
  38.2 2.5 %collective-permute-start.8 = (bf16[8,32,1024]{2,1,0:T(8,128)(2,1)S(1)}, bf16[8,32,1024]{2,1,0:T(8,128)(2,1)S(1)}, u32[]{:S(2)}, u32[]{:S(2)}) collective-permute-start(bf16[8,32,1024]{2,1,0:T(8,128)(2,1)S(1)} %get-tuple-element.41), channel_id=1, source_target_pairs={{0,1},{1,0},{2,3},{3,2},{4,5},{5,4},{6,7},{7,6},{8,9},{9,8},{10,11... | collective-permute-start | bytes 1572872 | tf_op jit(solution)/shard_map/ppermute | solution.py:40
  38.3 15.1 %collective-permute-start.14 = (bf16[256,512]{1,0:T(8,128)(2,1)S(1)}, bf16[256,512]{1,0:T(8,128)(2,1)S(1)}, u32[]{:S(2)}, u32[]{:S(2)}) collective-permute-start(bf16[256,512]{1,0:T(8,128)(2,1)S(1)} %shard_map.134), channel_id=1, source_target_pairs={{0,2},{2,0},{4,6},{6,4},{8,10},{10,8},{12,14},{14,12},{1,3},{3,1},... | collective-permute-start | bytes 786440 | tf_op jit(solution)/shard_map/ppermute | solution.py:40
  40.8 13.6 %collective-permute-start.9 = (bf16[4,32,1024]{2,1,0:T(8,128)(2,1)S(1)}, bf16[4,32,1024]{2,1,0:T(8,128)(2,1)S(1)}, u32[]{:S(2)}, u32[]{:S(2)}) collective-permute-start(bf16[4,32,1024]{2,1,0:T(8,128)(2,1)S(1)} %get-tuple-element.44), channel_id=1, source_target_pairs={{0,2},{2,0},{4,6},{6,4},{8,10},{10,8},{12,14},{14,12},{1,3},{3,1},... | collective-permute-start | bytes 786440 | tf_op jit(solution)/shard_map/ppermute | solution.py:40
  44.9 16.0 %collective-permute-start.15 = (bf16[256,512]{1,0:T(8,128)(2,1)S(1)}, bf16[256,512]{1,0:T(8,128)(2,1)S(1)}, u32[]{:S(2)}, u32[]{:S(2)}) collective-permute-start(bf16[256,512]{1,0:T(8,128)(2,1)S(1)} %collective-permute-done.10.refs_2_.refs_0_.refs_1_.refs_4_), channel_id=1, source_target_pairs={{4,0},{6,2},{8,4},{10,6},{12,8},{14,10},{5,1},{7,3},{9,5},{11,7},{... | collective-permute-start | bytes 786440 | tf_op jit(solution)/shard_map/ppermute | solution.py:36
  46.4 21.3 %collective-permute-start.18 = (bf16[256,512]{1,0:T(8,128)(2,1)S(1)}, bf16[256,512]{1,0:T(8,128)(2,1)S(1)}, u32[]{:S(2)}, u32[]{:S(2)}) collective-permute-start(bf16[256,512]{1,0:T(8,128)(2,1)S(1)} %shard_map.130.refs_2_), channel_id=1, source_target_pairs={{0,4},{2,6},{4,8},{6,10},{8,12},{10,14},{1,5},{3,7},{5,9},{7,11},{... | collective-permute-start | bytes 786440 | tf_op jit(solution)/shard_map/ppermute | solution.py:36
  52.1 8.9 %collective-permute-start.17 = (bf16[256,512]{1,0:T(8,128)(2,1)S(1)}, bf16[256,512]{1,0:T(8,128)(2,1)S(1)}, u32[]{:S(2)}, u32[]{:S(2)}) collective-permute-start(bf16[256,512]{1,0:T(8,128)(2,1)S(1)} %shard_map.131.refs_2_), channel_id=1, source_target_pairs={{0,2},{2,0},{4,6},{6,4},{8,10},{10,8},{12,14},{14,12},{1,3},{3,1},... | collective-permute-start | bytes 786440 | tf_op jit(solution)/shard_map/ppermute | solution.py:40
  54.6 9.2 %collective-permute-start.11 = (bf16[1,32,1024]{2,1,0:T(8,128)(2,1)S(1)}, bf16[1,32,1024]{2,1,0:T(8,128)(2,1)S(1)}, u32[]{:S(2)}, u32[]{:S(2)}) collective-permute-start(bf16[1,32,1024]{2,1,0:T(8,128)(2,1)S(1)} %get-tuple-element.49), channel_id=1, source_target_pairs={{0,4},{2,6},{4,0},{6,2},{8,12},{10,14},{12,8},{14,10},{1,5},{3,7},... | collective-permute-start | bytes 196616 | tf_op jit(solution)/shard_map/ppermute | solution.py:40
  57.9 7.1 %collective-permute-start.12 = (bf16[1,32,1024]{2,1,0:T(8,128)(2,1)S(1)}, bf16[1,32,1024]{2,1,0:T(8,128)(2,1)S(1)}, u32[]{:S(2)}, u32[]{:S(2)}) collective-permute-start(bf16[1,32,1024]{2,1,0:T(8,128)(2,1)S(1)} %get-tuple-element.50), channel_id=1, source_target_pairs={{0,8},{2,10},{4,12},{6,14},{8,0},{10,2},{12,4},{14,6},{1,9},{3,11}... | collective-permute-start | bytes 196616 | tf_op jit(solution)/shard_map/ppermute | solution.py:40
  60.9 6.1 %collective-permute-start.13 = (bf16[1,32,1024]{2,1,0:T(8,128)(2,1)S(1)}, bf16[1,32,1024]{2,1,0:T(8,128)(2,1)S(1)}, u32[]{:S(2)}, u32[]{:S(2)}) collective-permute-start(bf16[1,32,1024]{2,1,0:T(8,128)(2,1)S(1)} %get-tuple-element.51), channel_id=1, source_target_pairs={{0,12},{2,14},{4,8},{6,10},{8,4},{10,6},{12,0},{14,2},{1,13},{3,15... | collective-permute-start | bytes 196616 | tf_op jit(solution)/shard_map/ppermute | solution.py:40
  61.0 7.0 %collective-permute-start.16 = (bf16[256,512]{1,0:T(8,128)(2,1)S(1)}, bf16[256,512]{1,0:T(8,128)(2,1)S(1)}, u32[]{:S(2)}, u32[]{:S(2)}) collective-permute-start(bf16[256,512]{1,0:T(8,128)(2,1)S(1)} %shard_map.135), channel_id=1, source_target_pairs={{0,2},{2,0},{4,6},{6,4},{8,10},{10,8},{12,14},{14,12},{1,3},{3,1},... | collective-permute-start | bytes 786440 | tf_op jit(solution)/shard_map/ppermute | solution.py:40
